TPU v7x, 32 devices: a whole 2x2x4 slice. The times are simulated.
32 devices in a mesh: dp: 4 (over z), ctx: 4 (over y, core), fsdp: 2 (over x).
Axes of the slice: x: 2, y: 2, z: 4, core: 2. Of those that a mesh axis runs over, the one named last changes fastest.
Arguments:
- tokens: bfloat16 [8, 1024, 2048], P(('dp', 'fsdp'), 'ctx'), may hold values from -6 to 6
- segment_ids: int32 [8, 1024], P(('dp', 'fsdp'), 'ctx'), may hold values from 0 to 2, as said below
- cotangent: bfloat16 [8, 1024, 2048], P(('dp', 'fsdp'), 'ctx'), may hold values from -6 to 6
- ln1_gain: bfloat16 [2048], P(('dp', 'fsdp')), may hold values from 0.5 to 1.5
- ln1_bias: bfloat16 [2048], P(('dp', 'fsdp')), may hold values from -1.796875 to 1.796875
- w_qkv: bfloat16 [2048, 6144], P(('dp', 'fsdp')), may hold values from -0.125 to 0.125
- b_qkv: bfloat16 [6144], P(('dp', 'fsdp')), may hold values from -3 to 3
- w_out: bfloat16 [2048, 2048], P(('dp', 'fsdp')), may hold values from -2 to 2
- ln2_gain: bfloat16 [2048], P(('dp', 'fsdp')), may hold values from 0.29882812 to 3
- ln2_bias: bfloat16 [2048], P(('dp', 'fsdp')), may hold values from -1.796875 to 1.796875
- w_gate_up: bfloat16 [2048, 11264], P(('dp', 'fsdp')), may hold values from -0.125 to 0.125
- w_down: bfloat16 [5632, 2048], P(('dp', 'fsdp')), may hold values from -0.078125 to 0.078125
Outputs:
- mixed: bfloat16 [8, 1024, 2048], P(('dp', 'fsdp'), 'ctx')
- input_grad: float32 [8, 1024, 2048], P(('dp', 'fsdp'), 'ctx')
- ln1_gain_grad: float32 [2048], P(('dp', 'fsdp'))
- ln1_bias_grad: float32 [2048], P(('dp', 'fsdp'))
- w_qkv_grad: float32 [2048, 6144], P(('dp', 'fsdp'))
- b_qkv_grad: float32 [6144], P(('dp', 'fsdp'))
- w_out_grad: float32 [2048, 2048], P(('dp', 'fsdp'))
- ln2_gain_grad: float32 [2048], P(('dp', 'fsdp'))
- ln2_bias_grad: float32 [2048], P(('dp', 'fsdp'))
- w_gate_up_grad: float32 [2048, 11264], P(('dp', 'fsdp'))
- w_down_grad: float32 [5632, 2048], P(('dp', 'fsdp'))
Inputs may be any that keep to these rules, and one draw needn't show every extreme that they name: `segment_ids`: in every row the ids never fall and the row holds exactly three nonempty documents, numbered 0, 1 and 2 in order.
All inputs are finite; a program needn't handle non-finite values.
Results may differ from a plain program's by a relative error of at most 0.02.
Values may be sent and summed in bfloat16 or wider, within the bound.
No kernel may reach another device: no remote copies, remote signals or barrier semaphores. Data moves between devices by JAX's collectives and lax.ppermute only.
A program may use at most 512 MiB of HBM per device.

v0:
```python
import jax
import jax.numpy as jnp
from jax import lax
from jax.sharding import PartitionSpec as P

D = 2048
H = 32
E = 64
FF = 5632
ROT = 16


epsilon = 1e-05
masked_score = -1e30


def layer_stats(values):
    average = jnp.mean(values, axis=-1, keepdims=True)
    centred = values - average
    variance = jnp.mean(centred * centred, axis=-1, keepdims=True)
    inverse = lax.rsqrt(variance + epsilon)
    return (centred * inverse, inverse)


def layer_norm_back(grad_normed, normal, inverse, scale_gain):
    grad_scaled = grad_normed * scale_gain
    first_mean = jnp.mean(grad_scaled, axis=-1, keepdims=True)
    second_mean = jnp.mean(grad_scaled * normal, axis=-1, keepdims=True)
    return inverse * (grad_scaled - first_mean - normal * second_mean)


def rotary_tables(positions):
    half = ROT // 2
    freqs = 10000.0 ** (-jnp.arange(half, dtype=jnp.float32) * 2.0 / ROT)
    angles = positions.astype(jnp.float32)[:, None] * freqs[None, :]
    return (jnp.cos(angles)[:, None, :], jnp.sin(angles)[:, None, :])


def rotate(values, cosine, sine):
    half = ROT // 2
    first = values[..., :half]
    second = values[..., half:ROT]
    return jnp.concatenate(
        [first * cosine - second * sine, second * cosine + first * sine, values[..., ROT:]], axis=-1
    )


def contract_rows(left, right):
    return lax.dot_general(
        left, right, (((0,), (0,)), ((), ())), preferred_element_type=jnp.float32
    )


def contract_cols(left, right):
    return lax.dot_general(
        left, right, (((1,), (1,)), ((), ())), preferred_element_type=jnp.float32
    )


def body(
    tokens,
    segment_ids,
    cotangent,
    ln1_gain,
    ln1_bias,
    w_qkv,
    b_qkv,
    w_out,
    ln2_gain,
    ln2_bias,
    w_gate_up,
    w_down,
):
    rows = tokens.shape[1]
    scale = E ** (-0.5)
    inputs = tokens[0].astype(jnp.float32)
    seg_local = segment_ids[0]
    seg_float = seg_local.astype(jnp.float32)
    ctx_count = lax.axis_size("ctx")
    positions = lax.axis_index("ctx") * rows + jnp.arange(rows, dtype=jnp.int32)
    cosine, sine = rotary_tables(positions)
    gain_one, bias_one, qkv_full, qkv_bias_full, out_full = (
        lax.all_gather(ln1_gain, ("dp", "fsdp"), axis=0, tiled=True),
        lax.all_gather(ln1_bias, ("dp", "fsdp"), axis=0, tiled=True),
        lax.all_gather(w_qkv, ("dp", "fsdp"), axis=0, tiled=True),
        lax.all_gather(b_qkv, ("dp", "fsdp"), axis=0, tiled=True),
        lax.all_gather(w_out, ("dp", "fsdp"), axis=0, tiled=True),
    )
    normal_one, inverse_one = layer_stats(inputs)
    normed_one = (normal_one * gain_one.astype(jnp.float32) + bias_one.astype(jnp.float32)).astype(
        jnp.bfloat16
    )
    projected = jnp.dot(
        normed_one, qkv_full, preferred_element_type=jnp.float32
    ) + qkv_bias_full.astype(jnp.float32)
    queries = rotate(projected[:, :D].reshape(rows, H, E), cosine, sine).astype(jnp.bfloat16)
    keys = rotate(projected[:, D : 2 * D].reshape(rows, H, E), cosine, sine).astype(jnp.bfloat16)
    values = projected[:, 2 * D :].reshape(rows, H, E).astype(jnp.bfloat16)
    seg_keys = seg_local.astype(jnp.bfloat16)
    running_top = jnp.full((H, rows), masked_score, jnp.float32)
    running_acc = jnp.zeros((rows, H, E), jnp.float32)
    key_blk = lax.all_gather(keys, "ctx", axis=0, tiled=True)
    value_blk = lax.all_gather(values, "ctx", axis=0, tiled=True)
    seg_blk = lax.all_gather(seg_keys, "ctx", axis=0, tiled=True)
    count = key_blk.shape[0]
    scores = (
        jnp.einsum("qhe,khe->hqk", queries, key_blk, preferred_element_type=jnp.float32) * scale
    )
    key_pos = jnp.arange(count, dtype=jnp.int32)
    allowed = (key_pos[None, :] <= positions[:, None]) & (
        seg_blk.astype(jnp.float32)[None, :] == seg_float[:, None]
    )
    scores = jnp.where(allowed[None], scores, masked_score)
    new_top = jnp.maximum(running_top, jnp.max(scores, axis=-1))
    weights = jnp.where(allowed[None], jnp.exp(scores - new_top[..., None]), 0.0)
    factor = jnp.exp(running_top - new_top)
    new_total = jnp.sum(weights, axis=-1)
    new_acc = running_acc * factor.T[:, :, None] + jnp.einsum(
        "hqk,khe->qhe", weights.astype(jnp.bfloat16), value_blk, preferred_element_type=jnp.float32
    )
    log_total = new_top + jnp.log(new_total)
    attended_f = new_acc / new_total.T[:, :, None]
    attended = attended_f.reshape(rows, D).astype(jnp.bfloat16)
    hidden = inputs + jnp.dot(attended, out_full, preferred_element_type=jnp.float32)
    gain_two, bias_two, gate_up_full, down_full = (
        lax.all_gather(ln2_gain, ("dp", "fsdp"), axis=0, tiled=True),
        lax.all_gather(ln2_bias, ("dp", "fsdp"), axis=0, tiled=True),
        lax.all_gather(w_gate_up, ("dp", "fsdp"), axis=0, tiled=True),
        lax.all_gather(w_down, ("dp", "fsdp"), axis=0, tiled=True),
    )
    normal_two, inverse_two = layer_stats(hidden)
    normed_two = (normal_two * gain_two.astype(jnp.float32) + bias_two.astype(jnp.float32)).astype(
        jnp.bfloat16
    )
    gate_up = jnp.dot(normed_two, gate_up_full, preferred_element_type=jnp.float32)
    gate = gate_up[:, :FF]
    upward = gate_up[:, FF:]
    sigma = jax.nn.sigmoid(gate)
    swish = gate * sigma
    activ = (swish * upward).astype(jnp.bfloat16)
    result = hidden + jnp.dot(activ, down_full, preferred_element_type=jnp.float32)
    grad_out = cotangent[0]
    gain_two, bias_two, gate_up_full, down_full = (
        lax.all_gather(ln2_gain, ("dp", "fsdp"), axis=0, tiled=True),
        lax.all_gather(ln2_bias, ("dp", "fsdp"), axis=0, tiled=True),
        lax.all_gather(w_gate_up, ("dp", "fsdp"), axis=0, tiled=True),
        lax.all_gather(w_down, ("dp", "fsdp"), axis=0, tiled=True),
    )
    columns = lax.all_to_all(activ, ("dp", "fsdp"), split_axis=1, concat_axis=0, tiled=True)
    down_grad = contract_rows(columns, lax.all_gather(grad_out, ("dp", "fsdp"), axis=0, tiled=True))
    grad_activ = contract_cols(grad_out, down_full)
    grad_gate = grad_activ * upward * sigma * (1.0 + gate * (1.0 - sigma))
    grad_up = grad_activ * swish
    grad_gate_up = jnp.concatenate([grad_gate, grad_up], axis=1).astype(jnp.bfloat16)
    gate_up_grad = lax.psum_scatter(
        contract_rows(normed_two, grad_gate_up).astype(jnp.bfloat16),
        ("dp", "fsdp"),
        scatter_dimension=0,
        tiled=True,
    )
    grad_normed_two = contract_cols(grad_gate_up, gate_up_full)
    gain_two_grad = jnp.sum(grad_normed_two * normal_two, axis=0)
    bias_two_grad = jnp.sum(grad_normed_two, axis=0)
    grad_hidden = grad_out.astype(jnp.float32) + layer_norm_back(
        grad_normed_two, normal_two, inverse_two, gain_two.astype(jnp.float32)
    )
    grad_branch = grad_hidden.astype(jnp.bfloat16)
    gain_one, bias_one, qkv_full, qkv_bias_full, out_full = (
        lax.all_gather(ln1_gain, ("dp", "fsdp"), axis=0, tiled=True),
        lax.all_gather(ln1_bias, ("dp", "fsdp"), axis=0, tiled=True),
        lax.all_gather(w_qkv, ("dp", "fsdp"), axis=0, tiled=True),
        lax.all_gather(b_qkv, ("dp", "fsdp"), axis=0, tiled=True),
        lax.all_gather(w_out, ("dp", "fsdp"), axis=0, tiled=True),
    )
    grad_attended = contract_cols(grad_branch, out_full).astype(jnp.bfloat16)
    grad_heads = grad_attended.reshape(rows, H, E)
    delta = jnp.sum(grad_heads.astype(jnp.float32) * attended_f, axis=-1).T
    key_all, value_all, seg_all = (
        lax.all_gather(keys, "ctx", axis=0, tiled=True),
        lax.all_gather(values, "ctx", axis=0, tiled=True),
        lax.all_gather(seg_keys, "ctx", axis=0, tiled=True),
    )
    length = key_all.shape[0]
    group = 1
    while ctx_count % (group * 2) == 0 and rows * group * 2 <= 512:
        group = group * 2
    block = rows * group
    blocks = length // block

    def key_block(grad_query, index):
        start = index * block
        key_blk = lax.dynamic_slice_in_dim(key_all, start, block, 0)
        value_blk = lax.dynamic_slice_in_dim(value_all, start, block, 0)
        seg_blk = lax.dynamic_slice_in_dim(seg_all, start, block, 0)
        scores = (
            jnp.einsum("qhe,khe->hqk", queries, key_blk, preferred_element_type=jnp.float32) * scale
        )
        key_pos = start + jnp.arange(block, dtype=jnp.int32)
        allowed = (key_pos[None, :] <= positions[:, None]) & (
            seg_blk.astype(jnp.float32)[None, :] == seg_float[:, None]
        )
        weights = jnp.where(allowed[None], jnp.exp(scores - log_total[..., None]), 0.0)
        grad_weights = jnp.einsum(
            "qhe,khe->hqk", grad_heads, value_blk, preferred_element_type=jnp.float32
        )
        grad_scores = (weights * (grad_weights - delta[..., None])).astype(jnp.bfloat16)
        grad_query = grad_query + jnp.einsum(
            "hqk,khe->qhe", grad_scores, key_blk, preferred_element_type=jnp.float32
        )
        grad_key = (
            jnp.einsum("hqk,qhe->khe", grad_scores, queries, preferred_element_type=jnp.float32)
            * scale
        )
        grad_value = jnp.einsum(
            "hqk,qhe->khe",
            weights.astype(jnp.bfloat16),
            grad_heads,
            preferred_element_type=jnp.float32,
        )
        return (grad_query, (grad_key, grad_value))

    grad_query, (key_terms, value_terms) = lax.scan(
        key_block, jnp.zeros((rows, H, E), jnp.float32), jnp.arange(blocks)
    )
    key_grad, value_grad = (
        lax.psum_scatter(
            key_terms.reshape(length, D).astype(jnp.bfloat16),
            "ctx",
            scatter_dimension=0,
            tiled=True,
        ).astype(jnp.float32),
        lax.psum_scatter(
            value_terms.reshape(length, D).astype(jnp.bfloat16),
            "ctx",
            scatter_dimension=0,
            tiled=True,
        ).astype(jnp.float32),
    )
    grad_queries = rotate(grad_query * scale, cosine, -sine).reshape(rows, D)
    grad_keys = rotate(key_grad.reshape(rows, H, E), cosine, -sine).reshape(rows, D)
    grad_qkv = jnp.concatenate([grad_queries, grad_keys, value_grad], axis=1).astype(jnp.bfloat16)
    qkv_bias_grad = jnp.sum(grad_qkv.astype(jnp.float32), axis=0)
    grad_normed_one = contract_cols(grad_qkv, qkv_full)
    gain_one_grad = jnp.sum(grad_normed_one * normal_one, axis=0)
    bias_one_grad = jnp.sum(grad_normed_one, axis=0)
    input_grad = grad_hidden + layer_norm_back(
        grad_normed_one, normal_one, inverse_one, gain_one.astype(jnp.float32)
    )
    qkv_part = contract_rows(normed_one, grad_qkv)
    out_part = contract_rows(attended, grad_branch)
    attn_grad = lax.psum_scatter(
        jnp.concatenate([qkv_part, out_part], axis=1).astype(jnp.bfloat16),
        ("dp", "fsdp"),
        scatter_dimension=0,
        tiled=True,
    ).astype(jnp.float32)
    qkv_grad = attn_grad[:, : 3 * D]
    out_grad = attn_grad[:, 3 * D :]
    small_parts = (
        lax.psum_scatter(
            gain_one_grad.astype(jnp.bfloat16), ("dp", "fsdp"), scatter_dimension=0, tiled=True
        ).astype(jnp.float32),
        lax.psum_scatter(
            bias_one_grad.astype(jnp.bfloat16), ("dp", "fsdp"), scatter_dimension=0, tiled=True
        ).astype(jnp.float32),
        lax.psum_scatter(
            qkv_bias_grad.astype(jnp.bfloat16), ("dp", "fsdp"), scatter_dimension=0, tiled=True
        ).astype(jnp.float32),
        lax.psum_scatter(
            gain_two_grad.astype(jnp.bfloat16), ("dp", "fsdp"), scatter_dimension=0, tiled=True
        ).astype(jnp.float32),
        lax.psum_scatter(
            bias_two_grad.astype(jnp.bfloat16), ("dp", "fsdp"), scatter_dimension=0, tiled=True
        ).astype(jnp.float32),
    )
    summed = (
        lax.psum(small_parts[0].astype(jnp.bfloat16), "ctx").astype(jnp.float32),
        lax.psum(small_parts[1].astype(jnp.bfloat16), "ctx").astype(jnp.float32),
        lax.psum(qkv_grad.astype(jnp.bfloat16), "ctx").astype(jnp.float32),
        lax.psum(small_parts[2].astype(jnp.bfloat16), "ctx").astype(jnp.float32),
        lax.psum(out_grad.astype(jnp.bfloat16), "ctx").astype(jnp.float32),
        lax.psum(small_parts[3].astype(jnp.bfloat16), "ctx").astype(jnp.float32),
        lax.psum(small_parts[4].astype(jnp.bfloat16), "ctx").astype(jnp.float32),
        lax.psum(gate_up_grad, "ctx").astype(jnp.float32),
        lax.psum(down_grad.astype(jnp.bfloat16), "ctx").astype(jnp.float32),
    )
    return (
        result.astype(jnp.bfloat16)[None],
        input_grad[None],
        summed[0],
        summed[1],
        summed[2],
        summed[3],
        summed[4],
        summed[5],
        summed[6],
        summed[7],
        summed[8],
    )


def solution(mesh):
    placed = (
        P(("dp", "fsdp"), "ctx", None),
        P(("dp", "fsdp"), "ctx"),
        P(("dp", "fsdp"), "ctx", None),
        P(("dp", "fsdp")),
        P(("dp", "fsdp")),
        P(("dp", "fsdp"), None),
        P(("dp", "fsdp")),
        P(("dp", "fsdp"), None),
        P(("dp", "fsdp")),
        P(("dp", "fsdp")),
        P(("dp", "fsdp"), None),
        P(("dp", "fsdp"), None),
    )
    return jax.shard_map(
        body,
        mesh=mesh,
        in_specs=placed,
        out_specs=(
            P(("dp", "fsdp"), "ctx", None),
            P(("dp", "fsdp"), "ctx", None),
            P(("dp", "fsdp")),
            P(("dp", "fsdp")),
            P(("dp", "fsdp"), None),
            P(("dp", "fsdp")),
            P(("dp", "fsdp"), None),
            P(("dp", "fsdp")),
            P(("dp", "fsdp")),
            P(("dp", "fsdp"), None),
            P(("dp", "fsdp"), None),
        ),
        check_vma=False,
    )
```

profile of v0, /device:TPU:0, one launch (start us, length us, event | category | flops | bytes accessed | tf_op | source)
XLA Modules:
  0.0 3989.9 jit_solution(9690901123750171152)
XLA Ops:
  8.0 67.4 %all-gather.4 = bf16[8,1,768]{2,1,0:T(2,128)(2,1)S(1)} all-gather(bf16[1,1,768]{2,1,0:T(2,128)(2,1)S(1)} %reshape.321), channel_id=1, replica_groups=mesh['dp'=4,'ctx'=4,'fsdp'=2] {'dp','fsdp'}, dimensions={0}, use_global_device_ids=true | all-gather | bytes 13824 | tf_op jit(solution)/shard_map/all_gather | solution.py:86
  75.5 21.4 all-gather.3
  97.0 23.6 all-gather.2
  122.0 371.4 %all-gather.15.cloned.1.call-done = bf16[2048,6144]{1,0:T(8,128)(2,1)} async-done(((bf16[256,6144]{1,0:T(8,128)(2,1)}), bf16[2048,6144]{1,0:T(8,128)(2,1)}) %all-gather.15.cloned.1.call-update) | async-done | bytes 25165840 | tf_op jit(solution)/shard_map/all_gather | solution.py:85
  493.4 11.8 convolution_add_fusion
  528.0 19.3 all-gather.6
  547.3 16.4 all-gather.5
  567.6 16.3 fusion.24
  583.9 15.7 fusion.25
  599.7 18.3 fusion.79
  618.0 99.1 %all-gather.21.cloned.1.call-done = bf16[2048,2048]{1,0:T(8,128)(2,1)} async-done(((bf16[256,2048]{1,0:T(8,128)(2,1)}), bf16[2048,2048]{1,0:T(8,128)(2,1)}) %all-gather.21.cloned.1.call-update) | async-done | bytes 8388624 | tf_op jit(solution)/shard_map/all_gather | solution.py:87
  725.1 865.2 %all-gather.23.cloned.1.call-done = bf16[2048,11264]{1,0:T(8,128)(2,1)} async-done(((bf16[256,11264]{1,0:T(8,128)(2,1)}), bf16[2048,11264]{1,0:T(8,128)(2,1)}) %all-gather.23.cloned.1.call-update) | async-done | bytes 46137360 | tf_op jit(solution)/shard_map/all_gather | solution.py:128
  1590.4 24.5 fusion.76
  1614.9 418.0 %all-gather.25.cloned.1.call-done = bf16[5632,2048]{1,0:T(8,128)(2,1)} async-done(((bf16[704,2048]{1,0:T(8,128)(2,1)}), bf16[5632,2048]{1,0:T(8,128)(2,1)}) %all-gather.25.cloned.1.call-update) | async-done | bytes 23068688 | tf_op jit(solution)/shard_map/all_gather | solution.py:129
  2032.9 18.6 multiply_convert_fusion.1
  2051.5 23.3 multiply_reduce_fusion
  2090.8 87.0 %while.15 = (s32[]{:T(128)}, f32[256,32,64]{0,2,1:T(8,128)S(1)}, bf16[2,512,32,64]{1,3,2,0:T(8,128)(2,1)}, bf16[2,512,32,64]{1,3,2,0:T(8,128)(2,1)}, s32[2]{0:T(...) while((s32[]{:T(128)}, f32[256,32,64]{0,2,1:T(8,128)S(1)}, ...), condition=%wide.region_10.11_spmd.clone, body=%wide.region_9.10_spmd.clone.sunk | while | flops 2728789248 | bytes 153596272 | solution.py:222
  2102.8 10.7 fusion.124
  2123.9 10.6 bitcast_dynamic-update-slice_fusion.5
  2146.0 10.7 fusion.124
  2207.0 25.2 reduce-scatter.7.cloned.1.call-done
  2236.6 43.5 %reduce-scatter.9.cloned.1.call-done = bf16[256,2048]{0,1:T(8,128)(2,1)} async-done(((bf16[1024,2048]{0,1:T(8,128)(2,1)}), bf16[256,2048]{0,1:T(8,128)(2,1)}) %reduce-scatter.9.cloned.1.call-update) | async-done | bytes 1048592 | tf_op jit(solution)/shard_map/reduce_scatter | solution.py:232
  2280.1 12.8 convolution_convert_fusion.1
  2292.9 22.9 pad_maximum_fusion
  2317.4 21.6 convolution_convert_fusion
  2343.7 122.1 %all_to_all.19 = bf16[256,8,704]{0,2,1:T(8,128)(2,1)S(1)} all-to-all(bf16[256,8,704]{0,2,1:T(8,128)(2,1)} %bitcast.166), channel_id=1, replica_groups=mesh['dp'=4,'ctx'=4,'fsdp'=2] {'dp','fsdp'}, dimensions={1} | all-to-all | bytes 5767168 | tf_op jit(solution)/shard_map/all_to_all | solution.py:149
  2478.3 529.2 %reduce-scatter.11.cloned.1.call-done = bf16[256,8192]{1,0:T(8,128)(2,1)} async-done(((bf16[2048,8192]{1,0:T(8,128)(2,1)}), bf16[256,8192]{1,0:T(8,128)(2,1)}) %reduce-scatter.11.cloned.1.call-update) | async-done | bytes 4194320 | tf_op jit(solution)/shard_map/reduce_scatter | solution.py:251
  3013.6 723.6 %reduce-scatter.13.cloned.1.call-done = bf16[256,11264]{1,0:T(8,128)(2,1)} async-done(((bf16[2048,11264]{1,0:T(8,128)(2,1)}), bf16[256,11264]{1,0:T(8,128)(2,1)}) %reduce-scatter.13.cloned.1.call-update) | async-done | bytes 5767184
  3739.7 13.9 fusion.46
  3754.7 13.7 fusion.54
  3768.4 34.3 all-reduce.6
  3816.0 150.4 %all-reduce.11.cloned.1.call-done = (bf16[256,6144]{1,0:T(8,128)(2,1)}, bf16[256,2048]{1,0:T(8,128)(2,1)}, bf16[256,11264]{1,0:T(8,128)(2,1)}, bf16[704,2048]{1,0:T(8,128)(2,1)}) async-done(((bf16[256,6144]{1,0:T(8,128)(2,1)}, bf16[256,2048]{1,0:T(8,128)(2,1)}, bf16[256,11264]{1,0:T(8,128)(2,1)}, bf16[704,2048]{1,0:T(8,128)(2,1)}), (bf16[256,6144]{1,0:T(8,128)(2,1)}, bf16[256,2048]{1,0:T(8,128)(2,1)}, ...) | async-done | bytes 12845072 | tf_op jit(solution)/shard_map/psum | solution.py:279
  (248 shorter events, 195.6 us)
Async XLA Ops:
  7.2 68.3 %copy-start.49 = (bf16[256]{0:T(256)(128)(2,1)S(1)}, bf16[256]{0:T(256)(128)(2,1)}, u32[]{:S(2)}) copy-start(bf16[256]{0:T(256)(128)(2,1)} %param.18) | copy-start | bytes 1540
  7.2 89.8 %copy-start.50 = (bf16[256]{0:T(256)(128)(2,1)S(1)}, bf16[256]{0:T(256)(128)(2,1)}, u32[]{:S(2)}) copy-start(bf16[256]{0:T(256)(128)(2,1)} %param.17) | copy-start | bytes 1540
  7.2 113.4 %copy-start.3 = (bf16[1,256,2048]{2,1,0:T(8,128)(2,1)S(1)}, bf16[1,256,2048]{2,1,0:T(8,128)(2,1)}, u32[]{:S(2)}) copy-start(bf16[1,256,2048]{2,1,0:T(8,128)(2,1)} %param.14) | copy-start | bytes 3145732
  7.2 486.2 %all-gather.15.cloned.1.call-start = ((), (), s32[]{:S(2)}) async-start(), calls=%async_computation.5 | async-start | bytes 28311552 | tf_op jit(solution)/shard_map/all_gather | solution.py:85
  8.0 559.6 %all-gather.17.cloned.1.call-start = ((), (), s32[]{:S(2)}) async-start(), calls=%async_computation.6 | async-start | bytes 5242880 | tf_op jit(solution)/shard_map/all_gather | solution.py:102
  97.0 396.5 %copy-start.25 = (f32[8,1,256]{2,1,0:T(1,128)}, f32[8,1,256]{2,1,0:T(1,128)S(1)}, u32[]{:S(2)}) copy-start(f32[8,1,256]{2,1,0:T(1,128)S(1)} %convert_element_type.219) | copy-start | bytes 24580
  120.6 372.9 %copy-start.21 = (f32[8,1,256]{2,1,0:T(1,128)}, f32[8,1,256]{2,1,0:T(1,128)S(1)}, u32[]{:S(2)}) copy-start(f32[8,1,256]{2,1,0:T(1,128)S(1)} %convert_element_type.218) | copy-start | bytes 24580
  120.8 372.6 %copy-start.33 = (f32[256]{0:T(256)}, f32[256]{0:T(256)S(1)}, u32[]{:S(2)}) copy-start(f32[256]{0:T(256)S(1)} %broadcast_multiply_fusion.6) | copy-start | bytes 3076
  121.3 372.2 %copy-start.35 = (f32[256]{0:T(256)}, f32[256]{0:T(256)S(1)}, u32[]{:S(2)}) copy-start(f32[256]{0:T(256)S(1)} %add_rsqrt_fusion.1) | copy-start | bytes 3076
  122.0 392.7 %copy-start.37 = (f32[256,8]{0,1:T(8,128)}, f32[256,8]{0,1:T(8,128)S(1)}, u32[]{:S(2)}) copy-start(f32[256,8]{0,1:T(8,128)S(1)} %get-tuple-element.207) | copy-start | bytes 24580
  517.9 81.8 %all-gather.19.cloned.1.call-start = ((), (), s32[]{:S(2)}) async-start(), calls=%async_computation.7 | async-start | bytes 5242880 | tf_op jit(solution)/shard_map/all_gather | solution.py:103
  521.0 196.1 %all-gather.21.cloned.1.call-start = ((), (), s32[]{:S(2)}) async-start(), calls=%async_computation.8 | async-start | bytes 9437184 | tf_op jit(solution)/shard_map/all_gather | solution.py:87
  521.6 1068.8 %all-gather.23.cloned.1.call-start = ((), (), s32[]{:S(2)}) async-start(), calls=%async_computation.9 | async-start | bytes 51904512 | tf_op jit(solution)/shard_map/all_gather | solution.py:128
  522.2 1510.7 %all-gather.25.cloned.1.call-start = ((), (), s32[]{:S(2)}) async-start(), calls=%async_computation.10 | async-start | bytes 25952256 | tf_op jit(solution)/shard_map/all_gather | solution.py:129
  522.8 1709.5 %reduce-scatter.7.cloned.1.call-start = ((), (), s32[]{:S(2)}) async-start(), calls=%async_computation.11 | async-start | bytes 5242880 | tf_op jit(solution)/shard_map/reduce_scatter | solution.py:226
  547.3 1043.1 %copy-start.27 = (f32[8,1,256]{2,1,0:T(1,128)}, f32[8,1,256]{2,1,0:T(1,128)S(1)}, u32[]{:S(2)}) copy-start(f32[8,1,256]{2,1,0:T(1,128)S(1)} %convert_element_type.222) | copy-start | bytes 24580
  563.8 1511.0 %copy-start.23 = (f32[8,1,256]{2,1,0:T(1,128)}, f32[8,1,256]{2,1,0:T(1,128)S(1)}, u32[]{:S(2)}) copy-start(f32[8,1,256]{2,1,0:T(1,128)S(1)} %convert_element_type.221) | copy-start | bytes 24580
  723.4 1351.3 %copy-start.29 = (f32[256]{0:T(256)}, f32[256]{0:T(256)S(1)}, u32[]{:S(2)}) copy-start(f32[256]{0:T(256)S(1)} %broadcast_multiply_fusion.5) | copy-start | bytes 3076
  725.1 1349.7 %copy-start.31 = (f32[256]{0:T(256)}, f32[256]{0:T(256)S(1)}, u32[]{:S(2)}) copy-start(f32[256]{0:T(256)S(1)} %add_rsqrt_fusion) | copy-start | bytes 3076
  2187.6 92.5 %reduce-scatter.9.cloned.1.call-start = ((), (), s32[]{:S(2)}) async-start(), calls=%async_computation.12 | async-start | bytes 5242880 | tf_op jit(solution)/shard_map/reduce_scatter | solution.py:232
  2197.6 270.2 %all-gather.27.cloned.1.call-start = ((), (), s32[]{:S(2)}) async-start(), calls=%async_computation.14 | async-start | bytes 9437184 | tf_op jit(solution)/shard_map/all_gather | solution.py:150
  2198.4 809.1 %reduce-scatter.11.cloned.1.call-start = ((), (), s32[]{:S(2)}) async-start(), calls=%async_computation.13 | async-start | bytes 37748736 | tf_op jit(solution)/shard_map/reduce_scatter | solution.py:251
  2235.0 45.1 %copy-start.4 = (bf16[1,256,2048]{2,1,0:T(8,128)(2,1)S(1)}, bf16[1,256,2048]{2,1,0:T(8,128)(2,1)}, u32[]{:S(2)}) copy-start(bf16[1,256,2048]{2,1,0:T(8,128)(2,1)} %param.14) | copy-start | bytes 3145732
  2235.0 45.1 %copy-start.22 = (f32[8,1,256]{2,1,0:T(1,128)S(1)}, f32[8,1,256]{2,1,0:T(1,128)}, u32[]{:S(2)}) copy-start(f32[8,1,256]{2,1,0:T(1,128)} %copy-done.21) | copy-start | bytes 24580
  2235.0 45.1 %copy-start.26 = (f32[8,1,256]{2,1,0:T(1,128)S(1)}, f32[8,1,256]{2,1,0:T(1,128)}, u32[]{:S(2)}) copy-start(f32[8,1,256]{2,1,0:T(1,128)} %copy-done.25) | copy-start | bytes 24580
  2235.0 45.1 %copy-start.34 = (f32[256]{0:T(256)S(1)}, f32[256]{0:T(256)}, u32[]{:S(2)}) copy-start(f32[256]{0:T(256)} %copy-done.33) | copy-start | bytes 3076
  2235.0 45.1 %copy-start.36 = (f32[256]{0:T(256)S(1)}, f32[256]{0:T(256)}, u32[]{:S(2)}) copy-start(f32[256]{0:T(256)} %copy-done.35) | copy-start | bytes 3076
  2236.4 56.5 %copy-start.8 = (bf16[256,32,64]{0,2,1:T(8,128)(2,1)}, bf16[256,32,64]{0,2,1:T(8,128)(2,1)S(1)}, u32[]{:S(2)}) copy-start(bf16[256,32,64]{0,2,1:T(8,128)(2,1)S(1)} %pad_maximum_fusion.8) | copy-start | bytes 3145732
  2236.6 56.3 %copy-start.10 = (bf16[256,32,64]{0,2,1:T(8,128)(2,1)}, bf16[256,32,64]{0,2,1:T(8,128)(2,1)S(1)}, u32[]{:S(2)}) copy-start(bf16[256,32,64]{0,2,1:T(8,128)(2,1)S(1)} %pad_maximum_fusion.7) | copy-start | bytes 3145732
  2315.9 1421.3 %reduce-scatter.13.cloned.1.call-start = ((), (), s32[]{:S(2)}) async-start(), calls=%async_computation.15 | async-start | bytes 51904512
  2339.1 1627.3 %all-reduce.11.cloned.1.call-start = ((), (), s32[]{:S(2)}) async-start(), calls=%async_computation.16 | async-start | bytes 25690112 | tf_op jit(solution)/shard_map/psum | solution.py:279
  3754.6 57.7 %copy-start.7 = (f32[256,2048]{1,0:T(8,128)S(1)}, f32[256,2048]{1,0:T(8,128)}, u32[]{:S(2)}) copy-start(f32[256,2048]{1,0:T(8,128)} %copy-done.5) | copy-start | bytes 6291460
  (39 other events, 351.9 us)
Sparse Core Ops, SparseCore 0:
  9.6 483.7 all-gather.14
  518.0 34.9 all-gather.16
  555.1 35.0 all-gather.18
  592.1 124.9 all-gather.20
  718.5 871.8 all-gather.22
  1591.7 441.0 all-gather.24
  2187.7 44.4 reduce-scatter.6
  2235.5 44.5 reduce-scatter.8
  2282.2 178.7 all-gather.26
  2464.6 542.8 reduce-scatter.10
  3011.3 725.8 reduce-scatter.12
  3741.1 225.2 all-reduce.10
where the time goes:
time: 4000 us; the launch traced here: 3990 us
  waiting for transfers between devices  3230 us (81%)
  blocking collectives  316 us (8%)
  matrix products  286 us (7%)
  other arithmetic  77.9 us (2%)
  local copies, waits for them, and re-layouts  61.7 us (2%)
    all_gather x1, waiting for transfers between devices, body(): lax.all_gather(w_gate_up, ('dp', 'fsdp'), axis=0, tiled=True)  865 us
    unnamed x13, waiting for transfers between devices  727 us
    reduce_scatter x1, waiting for transfers between devices, body(): lax.psum_scatter(jnp.concatenate([qkv_part, out_part], axis=1).astype(jnp...  529 us
    all_gather x1, waiting for transfers between devices, body(): lax.all_gather(w_down, ('dp', 'fsdp'), axis=0, tiled=True)  418 us
    all_gather x1, waiting for transfers between devices, body(): lax.all_gather(w_qkv, ('dp', 'fsdp'), axis=0, tiled=True)  371 us
    psum x1, waiting for transfers between devices, body(): lax.psum(qkv_grad.astype(jnp.bfloat16), 'ctx').astype(jnp.float32)  150 us
    all_to_all x1, blocking collectives, body(): lax.all_to_all(activ, ('dp', 'fsdp'), split_axis=1, concat_axis=0, tiled=...  122 us
    all_gather x1, waiting for transfers between devices, body(): lax.all_gather(w_out, ('dp', 'fsdp'), axis=0, tiled=True)  99.1 us
  transfers between devices with their start and end apart: 12, of which 9 were waited for; matrix products, arithmetic and copies ran while one was open for 6% of the time, Pallas kernels for 0%

commit v1 on v0

v1 whole, which is shorter than its diff:
```python
import jax
import jax.numpy as jnp
from jax import lax
from jax.sharding import PartitionSpec as P

D = 2048
H = 32
E = 64
FF = 5632
ROT = 16

epsilon = 1e-05
masked_score = -1e30
scale = E ** (-0.5)


def swap(block, axis, bit):
    count = lax.axis_size(axis)
    return lax.ppermute(block, axis, [(i, i ^ bit) for i in range(count)])


def tie(value, *others):
    return lax.optimization_barrier((value, *others))[0]


def shard_index():
    return lax.axis_index("dp") * lax.axis_size("fsdp") + lax.axis_index("fsdp")


def gather_shards(block):
    near = [block] + [swap(block, "dp", r) for r in range(1, lax.axis_size("dp"))]
    blocks = []
    for part in near:
        blocks.append(part)
        for r in range(1, lax.axis_size("fsdp")):
            blocks.append(swap(part, "fsdp", r))
    return blocks


def scatter_shards(blocks):
    far = lax.axis_size("dp")
    wide = lax.axis_size("fsdp")
    parts = blocks.reshape((far, wide) + blocks.shape[1:])
    total = parts[:, 0]
    for r in range(1, wide):
        total = total + swap(parts[:, r].astype(jnp.bfloat16), "fsdp", r).astype(jnp.float32)
    mine = total[0]
    for r in range(1, far):
        mine = mine + swap(total[r].astype(jnp.bfloat16), "dp", r).astype(jnp.float32)
    return mine


def ctx_gather(block):
    count = lax.axis_size("ctx")
    found = {0: block}
    bit = count // 2
    while bit >= 1:
        for r in list(found):
            found[r | bit] = swap(found[r], "ctx", bit)
        bit //= 2
    return [found[r] for r in range(count)]


def ctx_scatter(rows):
    count = lax.axis_size("ctx")
    size = rows.shape[0] // count
    parts = {r: rows[r * size : (r + 1) * size] for r in range(count)}
    bit = 1
    while bit < count:
        parts = {
            r: parts[r]
            + swap(parts[r | bit].astype(jnp.bfloat16), "ctx", bit).astype(jnp.float32)
            for r in parts
            if not r & bit
        }
        bit *= 2
    return parts[0]


def reorder(array, index, axis):
    count = array.shape[axis]
    bit = 1
    while bit < count:
        shape = array.shape[:axis] + (count // (2 * bit), 2, bit) + array.shape[axis + 1 :]
        split = array.reshape(shape)
        first = lax.index_in_dim(split, 0, axis + 1, keepdims=True)
        second = lax.index_in_dim(split, 1, axis + 1, keepdims=True)
        flip = (index & bit) != 0
        split = jnp.concatenate(
            [jnp.where(flip, second, first), jnp.where(flip, first, second)], axis=axis + 1
        )
        array = split.reshape(array.shape)
        bit *= 2
    return array


def layer_stats(values):
    average = jnp.mean(values, axis=-1, keepdims=True)
    centred = values - average
    variance = jnp.mean(centred * centred, axis=-1, keepdims=True)
    inverse = lax.rsqrt(variance + epsilon)
    return (centred * inverse, inverse)


def layer_norm_back(grad_normed, normal, inverse, scale_gain):
    grad_scaled = grad_normed * scale_gain
    first_mean = jnp.mean(grad_scaled, axis=-1, keepdims=True)
    second_mean = jnp.mean(grad_scaled * normal, axis=-1, keepdims=True)
    return inverse * (grad_scaled - first_mean - normal * second_mean)


def rotary_tables(positions):
    half = ROT // 2
    freqs = 10000.0 ** (-jnp.arange(half, dtype=jnp.float32) * 2.0 / ROT)
    angles = positions.astype(jnp.float32)[:, None] * freqs[None, :]
    return (jnp.cos(angles)[:, None, :], jnp.sin(angles)[:, None, :])


def rotate(values, cosine, sine):
    half = ROT // 2
    first = values[..., :half]
    second = values[..., half:ROT]
    return jnp.concatenate(
        [first * cosine - second * sine, second * cosine + first * sine, values[..., ROT:]], axis=-1
    )


def mul(left, right):
    return jnp.dot(left, right, preferred_element_type=jnp.float32)


def contract_rows(left, right):
    return lax.dot_general(
        left, right, (((0,), (0,)), ((), ())), preferred_element_type=jnp.float32
    )


def contract_cols(left, right):
    return lax.dot_general(
        left, right, (((1,), (1,)), ((), ())), preferred_element_type=jnp.float32
    )


def pick(array, index, axis):
    return lax.dynamic_index_in_dim(array, index, axis, keepdims=False)


def body(
    tokens,
    segment_ids,
    cotangent,
    ln1_gain,
    ln1_bias,
    w_qkv,
    b_qkv,
    w_out,
    ln2_gain,
    ln2_bias,
    w_gate_up,
    w_down,
):
    rows = tokens.shape[1]
    count = lax.axis_size("ctx")
    ctx = lax.axis_index("ctx")
    shards = lax.axis_size("dp") * lax.axis_size("fsdp")
    shard = shard_index()
    length = rows * count
    depth = D // shards
    heads = H // count
    even = (H // shards) % count == 0

    if even:
        qkv_mine = pick(w_qkv.reshape(depth, 3, shards, count, -1), ctx, 3).reshape(depth, -1)
        out_mine = pick(w_out.reshape(count, -1, D), ctx, 0)
    else:
        qkv_mine = pick(w_qkv.reshape(depth, 3, count, -1), ctx, 2).reshape(depth, -1)
        out_mine = w_out
    gate_up_mine = pick(w_gate_up.reshape(depth, 2, shards, count, -1), ctx, 3).reshape(depth, -1)
    down_mine = pick(w_down.reshape(count, -1, D), ctx, 0)

    small = jnp.concatenate([ln1_gain, ln1_bias, ln2_gain, ln2_bias, b_qkv])
    small_all = reorder(jnp.stack(gather_shards(small)), shard, 0).astype(jnp.float32)
    gain_one = small_all[:, :depth].reshape(D)
    bias_one = small_all[:, depth : 2 * depth].reshape(D)
    gain_two = small_all[:, 2 * depth : 3 * depth].reshape(D)
    bias_two = small_all[:, 3 * depth : 4 * depth].reshape(D)
    qkv_bias = small_all[:, 4 * depth :].reshape(3 * D)
    if even:
        bias_mine = pick(qkv_bias.reshape(3, shards, count, -1), ctx, 2).reshape(-1)
    else:
        bias_mine = pick(qkv_bias.reshape(3, count, -1), ctx, 1).reshape(-1)

    token_rows = jnp.concatenate(ctx_gather(tokens[0]), axis=0)
    segments = jnp.concatenate(ctx_gather(segment_ids), axis=1)[0]
    positions = jnp.concatenate(
        [(ctx ^ r) * rows + jnp.arange(rows, dtype=jnp.int32) for r in range(count)]
    )
    cosine, sine = rotary_tables(positions)

    qkv_all = jnp.concatenate(gather_shards(qkv_mine), axis=0)
    out_all = jnp.stack(gather_shards(tie(out_mine, qkv_all)))
    out_all = reorder(out_all, shard, 0).reshape(-1, D)
    if not even:
        out_all = pick(out_all.reshape(count, -1, D), ctx, 0)
    gate_up_all = jnp.concatenate(gather_shards(tie(gate_up_mine, qkv_all)), axis=0)
    cot_rows = jnp.concatenate(ctx_gather(tie(cotangent[0], token_rows)), axis=0)
    down_all = jnp.stack(gather_shards(tie(down_mine, gate_up_all)))
    down_all = reorder(down_all, shard, 0).reshape(-1, D)

    def to_shard_order(array):
        n = array.shape[0]
        return reorder(array.reshape(n, shards, depth), shard, 1).reshape(n, D)

    normal_one, inverse_one = layer_stats(token_rows.astype(jnp.float32))
    normed_one = to_shard_order((normal_one * gain_one + bias_one).astype(jnp.bfloat16))
    projected = mul(normed_one, qkv_all) + bias_mine
    width = heads * E
    queries = rotate(projected[:, :width].reshape(length, heads, E), cosine, sine).astype(
        jnp.bfloat16
    )
    keys = rotate(projected[:, width : 2 * width].reshape(length, heads, E), cosine, sine).astype(
        jnp.bfloat16
    )
    values = projected[:, 2 * width :].reshape(length, heads, E).astype(jnp.bfloat16)
    allowed = (positions[None, :] <= positions[:, None]) & (segments[None, :] == segments[:, None])
    scores = jnp.einsum("qhe,khe->hqk", queries, keys, preferred_element_type=jnp.float32) * scale
    scores = jnp.where(allowed[None], scores, masked_score)
    top = jnp.max(scores, axis=-1, keepdims=True)
    weights = jnp.exp(scores - top)
    weights = weights / jnp.sum(weights, axis=-1, keepdims=True)
    low_weights = weights.astype(jnp.bfloat16)
    attended_f = jnp.einsum("hqk,khe->qhe", low_weights, values, preferred_element_type=jnp.float32)
    attended = attended_f.reshape(length, width).astype(jnp.bfloat16)

    hidden = tokens[0].astype(jnp.float32) + ctx_scatter(mul(attended, out_all))
    normal_two, inverse_two = layer_stats(hidden)
    normed_two = to_shard_order((normal_two * gain_two + bias_two).astype(jnp.bfloat16))
    normed_two = jnp.concatenate(ctx_gather(normed_two), axis=0)
    gate_up = mul(normed_two, gate_up_all)
    units = FF // count
    gate = gate_up[:, :units]
    upward = gate_up[:, units:]
    sigma = jax.nn.sigmoid(gate)
    swish = gate * sigma
    activ = (swish * upward).astype(jnp.bfloat16)
    mixed = hidden + ctx_scatter(mul(activ, down_all))

    grad_activ = contract_cols(cot_rows, down_all)
    grad_gate = grad_activ * upward * sigma * (1.0 + gate * (1.0 - sigma))
    grad_up = grad_activ * swish
    grad_gate_up = jnp.concatenate([grad_gate, grad_up], axis=1).astype(jnp.bfloat16)
    down_part = contract_rows(activ, cot_rows).reshape(shards, -1, D)
    down_grad = scatter_shards(reorder(down_part, shard, 0))
    gate_up_part = contract_rows(normed_two, grad_gate_up).reshape(shards, depth, 2 * units)
    gate_up_grad = scatter_shards(tie(gate_up_part, down_grad))

    grad_normed_two = ctx_scatter(contract_cols(grad_gate_up, gate_up_all))
    grad_normed_two = to_shard_order(grad_normed_two)
    gain_two_grad = jnp.sum(grad_normed_two * normal_two, axis=0)
    bias_two_grad = jnp.sum(grad_normed_two, axis=0)
    grad_hidden = cotangent[0].astype(jnp.float32) + layer_norm_back(
        grad_normed_two, normal_two, inverse_two, gain_two
    )
    grad_branch = jnp.concatenate(ctx_gather(grad_hidden.astype(jnp.bfloat16)), axis=0)

    grad_attended = contract_cols(grad_branch, out_all).astype(jnp.bfloat16)
    out_part = contract_rows(attended, grad_branch)
    grad_heads = grad_attended.reshape(length, heads, E)
    grad_weights = jnp.einsum("qhe,khe->hqk", grad_heads, values, preferred_element_type=jnp.float32)
    delta = jnp.sum(weights * grad_weights, axis=-1, keepdims=True)
    grad_scores = (weights * (grad_weights - delta)).astype(jnp.bfloat16)
    grad_queries = (
        jnp.einsum("hqk,khe->qhe", grad_scores, keys, preferred_element_type=jnp.float32) * scale
    )
    grad_keys = (
        jnp.einsum("hqk,qhe->khe", grad_scores, queries, preferred_element_type=jnp.float32) * scale
    )
    grad_values = jnp.einsum(
        "hqk,qhe->khe", low_weights, grad_heads, preferred_element_type=jnp.float32
    )
    grad_qkv = jnp.concatenate(
        [
            rotate(grad_queries, cosine, -sine).reshape(length, width),
            rotate(grad_keys, cosine, -sine).reshape(length, width),
            grad_values.reshape(length, width),
        ],
        axis=1,
    ).astype(jnp.bfloat16)
    qkv_bias_part = jnp.sum(grad_qkv.astype(jnp.float32), axis=0)
    qkv_part = contract_rows(normed_one, grad_qkv).reshape(shards, depth, 3 * width)

    grad_normed_one = to_shard_order(ctx_scatter(contract_cols(grad_qkv, qkv_all)))
    normal_mine = normal_one[:rows]
    gain_one_grad = jnp.sum(grad_normed_one * normal_mine, axis=0)
    bias_one_grad = jnp.sum(grad_normed_one, axis=0)
    input_grad = grad_hidden + layer_norm_back(
        grad_normed_one, normal_mine, inverse_one[:rows], gain_one
    )

    qkv_grad = scatter_shards(tie(qkv_part, gate_up_grad))

    def ctx_blocks(block):
        found = jnp.stack(ctx_gather(block.astype(jnp.bfloat16)))
        return reorder(found, ctx, 0).astype(jnp.float32)

    down_out = ctx_blocks(down_grad).reshape(-1, D)
    gate_up_out = ctx_blocks(gate_up_grad).reshape(count, depth, 2, shards, -1)
    gate_up_out = gate_up_out.transpose(1, 2, 3, 0, 4).reshape(depth, 2 * FF)
    if even:
        out_part = out_part.reshape(shards, -1, D)
        out_out = ctx_blocks(scatter_shards(reorder(out_part, shard, 0))).reshape(-1, D)
        qkv_out = ctx_blocks(qkv_grad).reshape(count, depth, 3, shards, -1)
        qkv_out = qkv_out.transpose(1, 2, 3, 0, 4).reshape(depth, 3 * D)
        qkv_bias_rows = ctx_blocks(qkv_bias_part).reshape(count, 3, shards, -1)
        qkv_bias_rows = qkv_bias_rows.transpose(1, 2, 0, 3).reshape(shards, -1)
    else:
        spread = jnp.zeros((count,) + out_part.shape, jnp.float32)
        spread = lax.dynamic_update_index_in_dim(spread, out_part, ctx, 0)
        out_part = spread.reshape(shards, depth, D)
        out_out = scatter_shards(reorder(out_part, shard, 0))
        out_out = lax.psum(out_out.astype(jnp.bfloat16), "ctx").astype(jnp.float32)
        qkv_out = ctx_blocks(qkv_grad).reshape(count, depth, 3, -1)
        qkv_out = qkv_out.transpose(1, 2, 0, 3).reshape(depth, 3 * D)
        qkv_bias_rows = ctx_blocks(qkv_bias_part).reshape(count, 3, -1)
        qkv_bias_rows = qkv_bias_rows.transpose(1, 0, 2).reshape(shards, -1)

    norm_parts = jnp.concatenate(
        [
            part.reshape(shards, depth)
            for part in (gain_one_grad, bias_one_grad, gain_two_grad, bias_two_grad)
        ],
        axis=1,
    )
    bit = 1
    while bit < count:
        norm_parts = norm_parts + swap(norm_parts, "ctx", bit)
        bit *= 2
    small_parts = jnp.concatenate([norm_parts, qkv_bias_rows], axis=1)
    small_grad = scatter_shards(reorder(small_parts, shard, 0))

    return (
        mixed.astype(jnp.bfloat16)[None],
        input_grad[None],
        small_grad[:depth],
        small_grad[depth : 2 * depth],
        qkv_out,
        small_grad[4 * depth :],
        out_out,
        small_grad[2 * depth : 3 * depth],
        small_grad[3 * depth : 4 * depth],
        gate_up_out,
        down_out,
    )


def solution(mesh):
    shards = ("dp", "fsdp")
    row = P(shards, "ctx", None)
    vector = P(shards)
    matrix = P(shards, None)
    return jax.shard_map(
        body,
        mesh=mesh,
        in_specs=(
            row,
            P(shards, "ctx"),
            row,
            vector,
            vector,
            matrix,
            vector,
            matrix,
            vector,
            vector,
            matrix,
            matrix,
        ),
        out_specs=(
            row,
            row,
            vector,
            vector,
            matrix,
            vector,
            matrix,
            vector,
            vector,
            matrix,
            matrix,
        ),
        check_vma=False,
    )
```

time: 4000 us -> 1630 us (0.41)
  waiting for transfers between devices: 3230 us -> 740 us
  blocking collectives: 316 us -> 0 us
  other arithmetic: 77.9 us -> 302 us
  local copies, waits for them, and re-layouts: 61.7 us -> 246 us
  starting transfers between devices: 0.69 us -> 113 us
  matrix products: 286 us -> 219 us
    all_gather x7 -> x0, waiting for transfers between devices: 1750 us -> none  [the longest x1 865 us: body(): lax.all_gather(w_gate_up, ('dp', 'fsdp'), axis=0, tiled=True)]
    ppermute x0 -> x99, waiting for transfers between devices: none -> 740 us  [swap(): return lax.ppermute(block, axis, [(i, i ^ bit) for i in range(count)])]
    unnamed x13 -> x0, waiting for transfers between devices: 727 us -> none
    reduce_scatter x3 -> x0, waiting for transfers between devices: 598 us -> none  [the longest x1 529 us: body(): lax.psum_scatter(jnp.concatenate([qkv_part, out_part], axis=1).astype(jnp...]
    all_gather x6 -> x0, blocking collectives: 153 us -> none  [the longest x1 67.4 us: body(): lax.all_gather(b_qkv, ('dp', 'fsdp'), axis=0, tiled=True)]
    psum x1 -> x0, waiting for transfers between devices: 150 us -> none  [body(): lax.psum(qkv_grad.astype(jnp.bfloat16), 'ctx').astype(jnp.float32)]
    all_to_all x1 -> x0, blocking collectives: 122 us -> none  [body(): lax.all_to_all(activ, ('dp', 'fsdp'), split_axis=1, concat_axis=0, tiled=...]
    ppermute x0 -> x99, starting transfers between devices: none -> 113 us  [swap(): return lax.ppermute(block, axis, [(i, i ^ bit) for i in range(count)])]
  transfers between devices with their start and end apart: 12 -> 99, of which waited for: 9 -> 36; matrix products, arithmetic and copies ran while one was open for 6% -> 39% of each run, Pallas kernels for 0% -> 0%
where the time goes in v1:
time: 1630 us; the launch traced here: 1620 us
  waiting for transfers between devices  740 us (45%)
  other arithmetic  302 us (19%)
  local copies, waits for them, and re-layouts  246 us (15%)
  matrix products  219 us (13%)
  starting transfers between devices  113 us (7%)
    ppermute x99, waiting for transfers between devices, swap(): return lax.ppermute(block, axis, [(i, i ^ bit) for i in range(count)])  740 us
    ppermute x99, starting transfers between devices, swap(): return lax.ppermute(block, axis, [(i, i ^ bit) for i in range(count)])  113 us
    unnamed x199, local copies, waits for them, and re-layouts  101 us
    select_n x40, other arithmetic, reorder(): jnp.where(flip, second, first)  67.5 us
    concatenate x31, other arithmetic, reorder(): jnp.concatenate([jnp.where(flip, second, first), jnp.where(flip, first, s...  66.6 us
    dot_general x4, matrix products, contract_cols(): lax.dot_general(left, right, (((1,), (1,)), ((), ())), preferred_element_...  49.5 us
    dot_general x4, matrix products, mul(): return jnp.dot(left, right, preferred_element_type=jnp.float32)  40.5 us
    dot_general x4, matrix products, contract_rows(): lax.dot_general(left, right, (((0,), (0,)), ((), ())), preferred_element_...  38.6 us
  transfers between devices with their start and end apart: 99, of which 36 were waited for; matrix products, arithmetic and copies ran while one was open for 39% of the time, Pallas kernels for 0%

profile of v1, /device:TPU:0, one launch (start us, length us, event | category | flops | bytes accessed | tf_op | source)
XLA Modules:
  0.0 1622.6 jit_solution(6856546771216617262)
XLA Ops:
  46.9 17.7 %collective-permute-done.15 = bf16[256,1536]{0,1:T(8,128)(2,1)} collective-permute-done((bf16[256,1536]{0,1:T(8,128)(2,1)}, bf16[256,1536]{0,1:T(8,128)(2,1)}, u32[]{:S(2)}, u32[]{:S(2)}) %collective-permute-start.15) | collective-permute-done | bytes 786464 | tf_op jit(solution)/shard_map/ppermute | solution.py:19
  66.3 31.1 %collective-permute-done.11 = bf16[256,1536]{0,1:T(8,128)(2,1)} collective-permute-done((bf16[256,1536]{0,1:T(8,128)(2,1)}, bf16[256,1536]{0,1:T(8,128)(2,1)}, u32[]{:S(2)}, u32[]{:S(2)}) %collective-permute-start.11) | collective-permute-done | bytes 786464 | tf_op jit(solution)/shard_map/ppermute | solution.py:19
  99.2 14.5 collective-permute-done.13
  129.2 21.3 %collective-permute-done.14 = bf16[256,1536]{0,1:T(8,128)(2,1)} collective-permute-done((bf16[256,1536]{0,1:T(8,128)(2,1)}, bf16[256,1536]{0,1:T(8,128)(2,1)}, u32[]{:S(2)}, u32[]{:S(2)}) %collective-permute-start.14) | collective-permute-done | bytes 786464 | tf_op jit(solution)/shard_map/ppermute | solution.py:19
  158.6 16.5 %collective-permute-start.23 = (bf16[64,2048]{1,0:T(8,128)(2,1)S(1)}, bf16[64,2048]{1,0:T(8,128)(2,1)}, u32[]{:S(2)}, u32[]{:S(2)}) collective-permute-start(bf16[64,2048]{1,0:T(8,128)(2,1)S(1)} %dynamic-slice_bitcast_fusion.1), channel_id=1, source_target_pairs={{0,16},{8,24},{16,0},{24,8},{1,17},{9,25},{17,1},{25,9},{2,18},{10... | collective-permute-start | bytes 786440 | tf_op jit(solution)/shard_map/ppermute | solution.py:19
  206.1 26.4 %add_convert_fusion = bf16[1024,4,2,1,256]{4,2,1,0,3:T(2,128)(2,1)S(1)} fusion(f32[1024]{0:T(1024)S(1)} %add_rsqrt_fusion, f32[1024]{0:T(1024)S(1)} %broadcast_multiply_fusion, bf16[256,4,2,1,256]{4,2,1,0,3:T(2,128)(2,1)} %concatenate.222, bf16[256,4,2,1,256]{4,2,1,0,3:T(2,128)(2,1)} %concatenate.221, bf16[256,4,2,1,256]{4,2,1,0,3:T(2,128)(2,1)} %concatenate.220, ...), kind=kLoop, calls=%fused_computation.21 | loop fusion | flops 18874368 | bytes 8413184 | tf_op jit(solution)/shard_map/convert_element_type | solution.py:215
  314.9 19.7 %fusion.88 = (f32[8,1024]{1,0:T(8,128)S(1)}, f32[8,1024,1024]{1,2,0:T(8,128)}) fusion(pred[1024,1024]{0,1:T(8,128)(4,1)} %compare_and_fusion, bf16[1024,8,48]{0,2,1:T(8,128)(2,1)} %slice.1104, bf16[1024,8,8]{0,2,1:T(8,128)(2,1)S(1)} %get-tuple-element.176, bf16[1024,8,8]{0,2,1:T(8,128)(2,1)S(1)} %get-tuple-element.177, bf16[1024,8,48]{0,2,1:T(8,128)(2,1)} %slice.1105, ...), kind=kOutput, calls=%fused_computation.369 | convolution fusion | flops 1113588736 | bytes 36732928 | tf_op jit(solution)/shard_map/sub | solution.py:229
  334.7 13.0 fusion.44
  366.5 22.7 %collective-permute-done.33 = bf16[256,2816]{0,1:T(8,128)(2,1)} collective-permute-done((bf16[256,2816]{0,1:T(8,128)(2,1)}, bf16[256,2816]{0,1:T(8,128)(2,1)}, u32[]{:S(2)}, u32[]{:S(2)}) %collective-permute-start.33) | collective-permute-done | bytes 1441824 | tf_op jit(solution)/shard_map/ppermute | solution.py:19
  396.4 87.4 %collective-permute-done.36 = bf16[256,2816]{0,1:T(8,128)(2,1)} collective-permute-done((bf16[256,2816]{0,1:T(8,128)(2,1)}, bf16[256,2816]{0,1:T(8,128)(2,1)}, u32[]{:S(2)}, u32[]{:S(2)}) %collective-permute-start.36) | collective-permute-done | bytes 1441824 | tf_op jit(solution)/shard_map/ppermute | solution.py:19
  509.9 38.0 %collective-permute-done.37 = bf16[256,2816]{0,1:T(8,128)(2,1)} collective-permute-done((bf16[256,2816]{0,1:T(8,128)(2,1)}, bf16[256,2816]{0,1:T(8,128)(2,1)}, u32[]{:S(2)}, u32[]{:S(2)}) %collective-permute-start.37) | collective-permute-done | bytes 1441824 | tf_op jit(solution)/shard_map/ppermute | solution.py:19
  576.8 41.5 %collective-permute-done.43 = bf16[176,2048]{1,0:T(8,128)(2,1)S(1)} collective-permute-done((bf16[176,2048]{1,0:T(8,128)(2,1)S(1)}, bf16[176,2048]{1,0:T(8,128)(2,1)S(1)}, u32[]{:S(2)}, u32[]{:S(2)}) %collective-permute-start.43) | collective-permute-done | bytes 720928 | tf_op jit(solution)/shard_map/ppermute | solution.py:19
  622.2 43.1 %collective-permute-done.42 = bf16[176,2048]{1,0:T(8,128)(2,1)S(1)} collective-permute-done((bf16[176,2048]{1,0:T(8,128)(2,1)S(1)}, bf16[176,2048]{1,0:T(8,128)(2,1)S(1)}, u32[]{:S(2)}, u32[]{:S(2)}) %collective-permute-start.42) | collective-permute-done | bytes 720928 | tf_op jit(solution)/shard_map/ppermute | solution.py:19
  671.4 19.0 %fusion.93 = f32[1024,2816]{1,0:T(8,128)} fusion(bf16[1024,2048]{1,0:T(8,128)(2,1)S(1)} %constant_dynamic-update-slice_fusion.8, bf16[2048,2816]{0,1:T(8,128)(2,1)} %constant_dynamic-update-slice_fusion.12), kind=kOutput, calls=%fused_computation.374 | convolution fusion | flops 11811160064 | bytes 27262976 | tf_op jit(solution)/shard_map/dot_general | solution.py:129
  690.4 14.9 multiply_convert_fusion.2
  723.4 18.3 %fusion.90 = (bf16[1024,2048]{1,0:T(8,128)(2,1)S(1)}, f32[1024,2048]{1,0:T(8,128)}) fusion(bf16[2048,2816]{0,1:T(8,128)(2,1)} %constant_dynamic-update-slice_fusion.12, bf16[1024,1408]{1,0:T(8,128)(2,1)} %get-tuple-element.73, bf16[1024,1408]{1,0:T(8,128)(2,1)S(1)} %copy-done.66), kind=kOutput, calls=%fused_computation.371 | convolution fusion | flops 11824791552 | bytes 29884416 | tf_op jit(solution)/shard_map/dot_general | solution.py:139
  811.2 14.7 collective-permute-done.55
  883.4 15.6 fusion.16
  900.3 15.4 collective-permute-done.74
  915.6 29.2 %collective-permute-done.73 = bf16[176,2048]{1,0:T(8,128)(2,1)S(1)} collective-permute-done((bf16[176,2048]{1,0:T(8,128)(2,1)}, bf16[176,2048]{1,0:T(8,128)(2,1)S(1)}, u32[]{:S(2)}, u32[]{:S(2)}) %collective-permute-start.73) | collective-permute-done | bytes 720928 | tf_op jit(solution)/shard_map/ppermute | solution.py:19
  993.0 14.7 fusion.47
  1007.7 21.5 %multiply_reduce_fusion = (f32[8,1024]{1,0:T(8,128)S(1)}, f32[8,1024,1024]{1,2,0:T(8,128)}) fusion(f32[8,1024,1024]{1,2,0:T(8,128)} %get-tuple-element.210, f32[8,1024]{1,0:T(8,128)S(1)} %copy-done.54, bf16[1024,8,64]{0,2,1:T(8,128)(2,1)S(1)} %bitcast.386, bf16[1024,8,64]{0,2,1:T(8,128)(2,1)S(1)} %bitcast.362), kind=kOutput, calls=%fused_computation.2 | convolution fusion | flops 1098899456 | bytes 69271552 | tf_op jit(solution)/shard_map/qhe,khe->hqk/dot_general | solution.py:269
  1029.2 28.6 %multiply_convert_fusion = bf16[8,1024,1024]{1,2,0:T(8,128)(2,1)} fusion(f32[8,1024,1024]{1,2,0:T(8,128)} %get-tuple-element.218, f32[8,1024]{1,0:T(8,128)S(1)} %get-tuple-element.217, f32[8,1024,1024]{1,2,0:T(8,128)} %get-tuple-element.210, f32[8,1024]{1,0:T(8,128)S(1)} %copy-done.54), kind=kLoop, calls=%fused_computation.1 | loop fusion | flops 33554432 | bytes 83951616 | tf_op jit(solution)/shard_map/convert_element_type | solution.py:271
  1134.3 17.5 %collective-permute-done.86 = bf16[4,64,2048]{2,1,0:T(8,128)(2,1)} collective-permute-done((bf16[4,64,2048]{2,1,0:T(8,128)(2,1)}, bf16[4,64,2048]{2,1,0:T(8,128)(2,1)}, u32[]{:S(2)}, u32[]{:S(2)}) %collective-permute-start.86) | collective-permute-done | bytes 1048608 | tf_op jit(solution)/shard_map/ppermute | solution.py:19
  1188.8 23.0 %collective-permute-done.61 = bf16[256,2048]{1,0:T(8,128)(2,1)S(1)} collective-permute-done((bf16[256,2048]{1,0:T(8,128)(2,1)S(1)}, bf16[256,2048]{1,0:T(8,128)(2,1)S(1)}, u32[]{:S(2)}, u32[]{:S(2)}) %collective-permute-start.61) | collective-permute-done | bytes 1048608 | tf_op jit(solution)/shard_map/ppermute | solution.py:19
  1260.9 31.5 %collective-permute-done.76 = bf16[256,2816]{0,1:T(8,128)(2,1)} collective-permute-done((bf16[256,2816]{0,1:T(8,128)(2,1)}, bf16[256,2816]{0,1:T(8,128)(2,1)}, u32[]{:S(2)}, u32[]{:S(2)}) %collective-permute-start.76) | collective-permute-done | bytes 1441824 | tf_op jit(solution)/shard_map/ppermute | solution.py:19
  1292.4 31.2 %collective-permute-done.78 = bf16[256,2816]{0,1:T(8,128)(2,1)} collective-permute-done((bf16[256,2816]{0,1:T(8,128)(2,1)}, bf16[256,2816]{0,1:T(8,128)(2,1)}, u32[]{:S(2)}, u32[]{:S(2)}) %collective-permute-start.78) | collective-permute-done | bytes 1441824 | tf_op jit(solution)/shard_map/ppermute | solution.py:19
  1323.6 60.6 %collective-permute-done.77 = bf16[256,2816]{0,1:T(8,128)(2,1)} collective-permute-done((bf16[256,2816]{0,1:T(8,128)(2,1)}, bf16[256,2816]{0,1:T(8,128)(2,1)}, u32[]{:S(2)}, u32[]{:S(2)}) %collective-permute-start.77) | collective-permute-done | bytes 1441824 | tf_op jit(solution)/shard_map/ppermute | solution.py:19
  1396.9 24.1 %collective-permute-done.94 = bf16[256,2816]{0,1:T(8,128)(2,1)} collective-permute-done((bf16[256,2816]{0,1:T(8,128)(2,1)}, bf16[256,2816]{0,1:T(8,128)(2,1)}, u32[]{:S(2)}, u32[]{:S(2)}) %collective-permute-start.94) | collective-permute-done | bytes 1441824 | tf_op jit(solution)/shard_map/ppermute | solution.py:19
  1420.9 42.0 %collective-permute-done.67 = bf16[4,1792]{1,0:T(4,128)(2,1)S(1)} collective-permute-done((bf16[4,1792]{1,0:T(4,128)(2,1)S(1)}, bf16[4,1792]{1,0:T(4,128)(2,1)S(1)}, u32[]{:S(2)}, u32[]{:S(2)}) %collective-permute-start.67) | collective-permute-done | bytes 14368 | tf_op jit(solution)/shard_map/ppermute | solution.py:19
  1492.3 26.5 %collective-permute-done.80 = bf16[256,1536]{1,0:T(8,128)(2,1)S(1)} collective-permute-done((bf16[256,1536]{1,0:T(8,128)(2,1)}, bf16[256,1536]{1,0:T(8,128)(2,1)S(1)}, u32[]{:S(2)}, u32[]{:S(2)}) %collective-permute-start.80) | collective-permute-done | bytes 786464 | tf_op jit(solution)/shard_map/ppermute | solution.py:19
  1525.9 29.1 %collective-permute-done.81 = bf16[256,1536]{1,0:T(8,128)(2,1)} collective-permute-done((bf16[256,1536]{1,0:T(8,128)(2,1)S(1)}, bf16[256,1536]{1,0:T(8,128)(2,1)}, u32[]{:S(2)}, u32[]{:S(2)}) %collective-permute-start.81) | collective-permute-done | bytes 786464 | tf_op jit(solution)/shard_map/ppermute | solution.py:19
  (622 shorter events, 749.1 us)
Async XLA Ops:
  36.7 83.2 %collective-permute-start.1 = (bf16[256,2048]{1,0:T(8,128)(2,1)}, bf16[256,2048]{1,0:T(8,128)(2,1)}, u32[]{:S(2)}, u32[]{:S(2)}) collective-permute-start(bf16[256,2048]{1,0:T(8,128)(2,1)} %bitcast.321), channel_id=1, source_target_pairs={{0,4},{2,6},{4,0},{6,2},{1,5},{3,7},{5,1},{7,3},{8,12},{10,14},{12... | collective-permute-start | bytes 3145736 | tf_op jit(solution)/shard_map/ppermute | solution.py:19
  41.8 80.6 %collective-permute-start = (bf16[256,2048]{1,0:T(8,128)(2,1)}, bf16[256,2048]{1,0:T(8,128)(2,1)}, u32[]{:S(2)}, u32[]{:S(2)}) collective-permute-start(bf16[256,2048]{1,0:T(8,128)(2,1)} %bitcast.322), channel_id=1, source_target_pairs={{0,2},{2,0},{4,6},{6,4},{1,3},{3,1},{5,7},{7,5},{8,10},{10,8},{12,... | collective-permute-start | bytes 3145736 | tf_op jit(solution)/shard_map/ppermute | solution.py:19
  45.8 67.9 %collective-permute-start.13 = (bf16[256,1536]{0,1:T(8,128)(2,1)}, bf16[256,1536]{0,1:T(8,128)(2,1)}, u32[]{:S(2)}, u32[]{:S(2)}) collective-permute-start(bf16[256,1536]{0,1:T(8,128)(2,1)} %bitcast.353), channel_id=1, source_target_pairs={{0,16},{8,24},{16,0},{24,8},{1,17},{9,25},{17,1},{25,9},{2,18},{10... | collective-permute-start | bytes 2359304 | tf_op jit(solution)/shard_map/ppermute | solution.py:19
  122.5 74.5 %collective-permute-start.2 = (bf16[256,2048]{1,0:T(8,128)(2,1)}, bf16[256,2048]{1,0:T(8,128)(2,1)}, u32[]{:S(2)}, u32[]{:S(2)}) collective-permute-start(bf16[256,2048]{1,0:T(8,128)(2,1)} %collective-permute-done.1), channel_id=1, source_target_pairs={{0,2},{2,0},{4,6},{6,4},{1,3},{3,1},{5,7},{7,5},{8,10},{10,8},{12,... | collective-permute-start | bytes 3145736 | tf_op jit(solution)/shard_map/ppermute | solution.py:19
  176.6 186.3 %collective-permute-start.34 = (bf16[256,2816]{0,1:T(8,128)(2,1)}, bf16[256,2816]{0,1:T(8,128)(2,1)}, u32[]{:S(2)}, u32[]{:S(2)}) collective-permute-start(bf16[256,2816]{0,1:T(8,128)(2,1)} %bitcast.28), channel_id=1, source_target_pairs={{0,8},{8,0},{16,24},{24,16},{1,9},{9,1},{17,25},{25,17},{2,10},{10... | collective-permute-start | bytes 4325384 | tf_op jit(solution)/shard_map/ppermute | solution.py:19
  191.1 103.4 %collective-permute-start.26 = (bf16[64,2048]{1,0:T(8,128)(2,1)S(1)}, bf16[64,2048]{1,0:T(8,128)(2,1)}, u32[]{:S(2)}, u32[]{:S(2)}) collective-permute-start(bf16[64,2048]{1,0:T(8,128)(2,1)S(1)} %collective-permute-done.25), channel_id=1, source_target_pairs={{0,1},{1,0},{2,3},{3,2},{4,5},{5,4},{6,7},{7,6},{8,9},{9,8},{10,11... | collective-permute-start | bytes 786440 | tf_op jit(solution)/shard_map/ppermute | solution.py:19
  192.5 98.5 %collective-permute-start.24 = (bf16[64,2048]{1,0:T(8,128)(2,1)}, bf16[64,2048]{1,0:T(8,128)(2,1)}, u32[]{:S(2)}, u32[]{:S(2)}) collective-permute-start(bf16[64,2048]{1,0:T(8,128)(2,1)} %collective-permute-done.23), channel_id=1, source_target_pairs={{0,1},{1,0},{2,3},{3,2},{4,5},{5,4},{6,7},{7,6},{8,9},{9,8},{10,11... | collective-permute-start | bytes 786440 | tf_op jit(solution)/shard_map/ppermute | solution.py:19
  193.1 96.9 %collective-permute-start.22 = (bf16[64,2048]{1,0:T(8,128)(2,1)}, bf16[64,2048]{1,0:T(8,128)(2,1)S(1)}, u32[]{:S(2)}, u32[]{:S(2)}) collective-permute-start(bf16[64,2048]{1,0:T(8,128)(2,1)} %collective-permute-done.21), channel_id=1, source_target_pairs={{0,1},{1,0},{2,3},{3,2},{4,5},{5,4},{6,7},{7,6},{8,9},{9,8},{10,11... | collective-permute-start | bytes 786440 | tf_op jit(solution)/shard_map/ppermute | solution.py:19
  362.9 120.9 %collective-permute-start.36 = (bf16[256,2816]{0,1:T(8,128)(2,1)}, bf16[256,2816]{0,1:T(8,128)(2,1)}, u32[]{:S(2)}, u32[]{:S(2)}) collective-permute-start(bf16[256,2816]{0,1:T(8,128)(2,1)} %bitcast.28), channel_id=1, source_target_pairs={{0,16},{8,24},{16,0},{24,8},{1,17},{9,25},{17,1},{25,9},{2,18},{10... | collective-permute-start | bytes 4325384 | tf_op jit(solution)/shard_map/ppermute | solution.py:19
  363.0 122.3 %collective-permute-start.51 = (bf16[256,2048]{1,0:T(8,128)(2,1)S(1)}, bf16[256,2048]{1,0:T(8,128)(2,1)}, u32[]{:S(2)}, u32[]{:S(2)}) collective-permute-start(bf16[256,2048]{1,0:T(8,128)(2,1)S(1)} %bitcast.350), channel_id=1, source_target_pairs={{0,4},{2,6},{4,0},{6,2},{1,5},{3,7},{5,1},{7,3},{8,12},{10,14},{12... | collective-permute-start | bytes 3145736 | tf_op jit(solution)/shard_map/ppermute | solution.py:19
  389.3 97.9 %collective-permute-start.27 = (bf16[256,2048]{1,0:T(8,128)(2,1)S(1)}, bf16[256,2048]{1,0:T(8,128)(2,1)S(1)}, u32[]{:S(2)}, u32[]{:S(2)}) collective-permute-start(bf16[256,2048]{1,0:T(8,128)(2,1)S(1)} %copy-done.28), channel_id=1, source_target_pairs={{0,2},{2,0},{4,6},{6,4},{1,3},{3,1},{5,7},{7,5},{8,10},{10,8},{12,... | collective-permute-start | bytes 3145736 | tf_op jit(solution)/shard_map/ppermute | solution.py:19
  389.3 98.0 %collective-permute-start.29 = (bf16[256,2048]{1,0:T(8,128)(2,1)S(1)}, bf16[256,2048]{1,0:T(8,128)(2,1)S(1)}, u32[]{:S(2)}, u32[]{:S(2)}) collective-permute-start(bf16[256,2048]{1,0:T(8,128)(2,1)S(1)} %fusion.37), channel_id=1, source_target_pairs={{0,4},{2,6},{4,0},{6,2},{1,5},{3,7},{5,1},{7,3},{8,12},{10,14},{12... | collective-permute-start | bytes 3145736 | tf_op jit(solution)/shard_map/ppermute | solution.py:19
  394.9 109.9 %collective-permute-start.35 = (bf16[256,2816]{0,1:T(8,128)(2,1)}, bf16[256,2816]{0,1:T(8,128)(2,1)}, u32[]{:S(2)}, u32[]{:S(2)}) collective-permute-start(bf16[256,2816]{0,1:T(8,128)(2,1)} %collective-permute-done.34), channel_id=1, source_target_pairs={{0,1},{1,0},{2,3},{3,2},{4,5},{5,4},{6,7},{7,6},{8,9},{9,8},{10,11... | collective-permute-start | bytes 4325384 | tf_op jit(solution)/shard_map/ppermute | solution.py:19
  483.8 69.3 %collective-permute-start.39 = (bf16[256,2816]{0,1:T(8,128)(2,1)}, bf16[256,2816]{0,1:T(8,128)(2,1)}, u32[]{:S(2)}, u32[]{:S(2)}) collective-permute-start(bf16[256,2816]{0,1:T(8,128)(2,1)} %collective-permute-done.38), channel_id=1, source_target_pairs={{0,1},{1,0},{2,3},{3,2},{4,5},{5,4},{6,7},{7,6},{8,9},{9,8},{10,11... | collective-permute-start | bytes 4325384 | tf_op jit(solution)/shard_map/ppermute | solution.py:19
  485.3 62.6 %collective-permute-start.37 = (bf16[256,2816]{0,1:T(8,128)(2,1)}, bf16[256,2816]{0,1:T(8,128)(2,1)}, u32[]{:S(2)}, u32[]{:S(2)}) collective-permute-start(bf16[256,2816]{0,1:T(8,128)(2,1)} %collective-permute-done.36), channel_id=1, source_target_pairs={{0,1},{1,0},{2,3},{3,2},{4,5},{5,4},{6,7},{7,6},{8,9},{9,8},{10,11... | collective-permute-start | bytes 4325384 | tf_op jit(solution)/shard_map/ppermute | solution.py:19
  487.2 76.3 %collective-permute-start.52 = (bf16[256,2048]{1,0:T(8,128)(2,1)}, bf16[256,2048]{1,0:T(8,128)(2,1)}, u32[]{:S(2)}, u32[]{:S(2)}) collective-permute-start(bf16[256,2048]{1,0:T(8,128)(2,1)} %collective-permute-done.51), channel_id=1, source_target_pairs={{0,2},{2,0},{4,6},{6,4},{1,3},{3,1},{5,7},{7,5},{8,10},{10,8},{12,... | collective-permute-start | bytes 3145736 | tf_op jit(solution)/shard_map/ppermute | solution.py:19
  559.0 62.9 %collective-permute-start.31 = (bf16[256,2048]{1,0:T(8,128)(2,1)S(1)}, bf16[256,2048]{1,0:T(8,128)(2,1)S(1)}, u32[]{:S(2)}, u32[]{:S(2)}) collective-permute-start(bf16[256,2048]{1,0:T(8,128)(2,1)S(1)} %reshape_reshape.131), channel_id=1, source_target_pairs={{0,4},{2,6},{4,0},{6,2},{1,5},{3,7},{5,1},{7,3},{8,12},{10,14},{12... | collective-permute-start | bytes 3145736 | tf_op jit(solution)/shard_map/ppermute | solution.py:19
  742.9 68.3 %collective-permute-start.53 = (bf16[256,2048]{1,0:T(8,128)(2,1)S(1)}, bf16[256,2048]{1,0:T(8,128)(2,1)S(1)}, u32[]{:S(2)}, u32[]{:S(2)}) collective-permute-start(bf16[256,2048]{1,0:T(8,128)(2,1)S(1)} %get-tuple-element.106), channel_id=1, source_target_pairs={{0,2},{2,0},{4,6},{6,4},{1,3},{3,1},{5,7},{7,5},{8,10},{10,8},{12,... | collective-permute-start | bytes 3145736 | tf_op jit(solution)/shard_map/ppermute | solution.py:19
  744.6 107.8 %collective-permute-start.47 = (bf16[256,2048]{1,0:T(8,128)(2,1)}, bf16[256,2048]{1,0:T(8,128)(2,1)}, u32[]{:S(2)}, u32[]{:S(2)}) collective-permute-start(bf16[256,2048]{1,0:T(8,128)(2,1)} %get-tuple-element.108), channel_id=1, source_target_pairs={{0,2},{2,0},{4,6},{6,4},{1,3},{3,1},{5,7},{7,5},{8,10},{10,8},{12,... | collective-permute-start | bytes 3145736 | tf_op jit(solution)/shard_map/ppermute | solution.py:19
  744.6 62.7 %collective-permute-start.48 = (bf16[256,2048]{1,0:T(8,128)(2,1)S(1)}, bf16[256,2048]{1,0:T(8,128)(2,1)}, u32[]{:S(2)}, u32[]{:S(2)}) collective-permute-start(bf16[256,2048]{1,0:T(8,128)(2,1)S(1)} %get-tuple-element.109), channel_id=1, source_target_pairs={{0,2},{2,0},{4,6},{6,4},{1,3},{3,1},{5,7},{7,5},{8,10},{10,8},{12,... | collective-permute-start | bytes 3145736 | tf_op jit(solution)/shard_map/ppermute | solution.py:19
  805.9 64.4 %collective-permute-start.71 = (bf16[4,176,2048]{2,1,0:T(8,128)(2,1)}, bf16[4,176,2048]{2,1,0:T(8,128)(2,1)}, u32[]{:S(2)}, u32[]{:S(2)}) collective-permute-start(bf16[4,176,2048]{2,1,0:T(8,128)(2,1)} %fusion.24), channel_id=1, source_target_pairs={{0,1},{1,0},{2,3},{3,2},{4,5},{5,4},{6,7},{7,6},{8,9},{9,8},{10,11... | collective-permute-start | bytes 8650760 | tf_op jit(solution)/shard_map/ppermute | solution.py:19
  859.3 128.2 %collective-permute-start.56 = (bf16[256,2048]{1,0:T(8,128)(2,1)}, bf16[256,2048]{1,0:T(8,128)(2,1)}, u32[]{:S(2)}, u32[]{:S(2)}) collective-permute-start(bf16[256,2048]{1,0:T(8,128)(2,1)} %get-tuple-element.66), channel_id=1, source_target_pairs={{0,2},{2,0},{4,6},{6,4},{1,3},{3,1},{5,7},{7,5},{8,10},{10,8},{12,... | collective-permute-start | bytes 3145736 | tf_op jit(solution)/shard_map/ppermute | solution.py:19
  883.4 104.1 %collective-permute-start.58 = (bf16[256,2048]{1,0:T(8,128)(2,1)}, bf16[256,2048]{1,0:T(8,128)(2,1)}, u32[]{:S(2)}, u32[]{:S(2)}) collective-permute-start(bf16[256,2048]{1,0:T(8,128)(2,1)} %collective-permute-done.57), channel_id=1, source_target_pairs={{0,2},{2,0},{4,6},{6,4},{1,3},{3,1},{5,7},{7,5},{8,10},{10,8},{12,... | collective-permute-start | bytes 3145736 | tf_op jit(solution)/shard_map/ppermute | solution.py:19
  947.5 180.4 %collective-permute-start.96 = (bf16[176,2048]{1,0:T(8,128)(2,1)}, bf16[176,2048]{1,0:T(8,128)(2,1)}, u32[]{:S(2)}, u32[]{:S(2)}) collective-permute-start(bf16[176,2048]{1,0:T(8,128)(2,1)} %fusion.52), channel_id=1, source_target_pairs={{0,2},{2,0},{4,6},{6,4},{1,3},{3,1},{5,7},{7,5},{8,10},{10,8},{12,... | collective-permute-start | bytes 2162696 | tf_op jit(solution)/shard_map/ppermute | solution.py:19
  947.5 179.5 %collective-permute-start.97 = (bf16[176,2048]{1,0:T(8,128)(2,1)}, bf16[176,2048]{1,0:T(8,128)(2,1)}, u32[]{:S(2)}, u32[]{:S(2)}) collective-permute-start(bf16[176,2048]{1,0:T(8,128)(2,1)} %fusion.52), channel_id=1, source_target_pairs={{0,4},{2,6},{4,0},{6,2},{1,5},{3,7},{5,1},{7,3},{8,12},{10,14},{12... | collective-permute-start | bytes 2162696 | tf_op jit(solution)/shard_map/ppermute | solution.py:19
  986.0 257.5 %collective-permute-start.75 = (bf16[4,256,2816]{1,2,0:T(8,128)(2,1)}, bf16[4,256,2816]{1,2,0:T(8,128)(2,1)}, u32[]{:S(2)}, u32[]{:S(2)}) collective-permute-start(bf16[4,256,2816]{1,2,0:T(8,128)(2,1)} %bitcast.334), channel_id=1, source_target_pairs={{0,1},{1,0},{2,3},{3,2},{4,5},{5,4},{6,7},{7,6},{8,9},{9,8},{10,11... | collective-permute-start | bytes 17301512 | tf_op jit(solution)/shard_map/ppermute | solution.py:19
  1257.2 66.4 %collective-permute-start.78 = (bf16[256,2816]{0,1:T(8,128)(2,1)}, bf16[256,2816]{0,1:T(8,128)(2,1)}, u32[]{:S(2)}, u32[]{:S(2)}) collective-permute-start(bf16[256,2816]{0,1:T(8,128)(2,1)} %get-tuple-element.88), channel_id=1, source_target_pairs={{0,24},{8,16},{16,8},{24,0},{1,25},{9,17},{17,9},{25,1},{2,26},{10... | collective-permute-start | bytes 4325384 | tf_op jit(solution)/shard_map/ppermute | solution.py:19
  1259.8 124.4 %collective-permute-start.77 = (bf16[256,2816]{0,1:T(8,128)(2,1)}, bf16[256,2816]{0,1:T(8,128)(2,1)}, u32[]{:S(2)}, u32[]{:S(2)}) collective-permute-start(bf16[256,2816]{0,1:T(8,128)(2,1)} %get-tuple-element.89), channel_id=1, source_target_pairs={{0,16},{8,24},{16,0},{24,8},{1,17},{9,25},{17,1},{25,9},{2,18},{10... | collective-permute-start | bytes 4325384 | tf_op jit(solution)/shard_map/ppermute | solution.py:19
  1394.5 83.9 %collective-permute-start.79 = (bf16[4,256,1536]{2,1,0:T(8,128)(2,1)}, bf16[4,256,1536]{2,1,0:T(8,128)(2,1)}, u32[]{:S(2)}, u32[]{:S(2)}) collective-permute-start(bf16[4,256,1536]{2,1,0:T(8,128)(2,1)} %fusion.21), channel_id=1, source_target_pairs={{0,1},{1,0},{2,3},{3,2},{4,5},{5,4},{6,7},{7,6},{8,9},{9,8},{10,11... | collective-permute-start | bytes 9437192 | tf_op jit(solution)/shard_map/ppermute | solution.py:19
  1395.2 67.7 %collective-permute-start.67 = (bf16[4,1792]{1,0:T(4,128)(2,1)S(1)}, bf16[4,1792]{1,0:T(4,128)(2,1)S(1)}, u32[]{:S(2)}, u32[]{:S(2)}) collective-permute-start(bf16[4,1792]{1,0:T(4,128)(2,1)S(1)} %bitcast.384), channel_id=1, source_target_pairs={{0,1},{1,0},{2,3},{3,2},{4,5},{5,4},{6,7},{7,6},{8,9},{9,8},{10,11... | collective-permute-start | bytes 43016 | tf_op jit(solution)/shard_map/ppermute | solution.py:19
  1396.8 78.7 %collective-permute-start.93 = (bf16[256,2816]{0,1:T(8,128)(2,1)}, bf16[256,2816]{0,1:T(8,128)(2,1)S(1)}, u32[]{:S(2)}, u32[]{:S(2)}) collective-permute-start(bf16[256,2816]{0,1:T(8,128)(2,1)} %fusion.27), channel_id=1, source_target_pairs={{0,2},{2,0},{4,6},{6,4},{1,3},{3,1},{5,7},{7,5},{8,10},{10,8},{12,... | collective-permute-start | bytes 4325384 | tf_op jit(solution)/shard_map/ppermute | solution.py:19
  1490.2 64.8 %collective-permute-start.81 = (bf16[256,1536]{1,0:T(8,128)(2,1)S(1)}, bf16[256,1536]{1,0:T(8,128)(2,1)}, u32[]{:S(2)}, u32[]{:S(2)}) collective-permute-start(bf16[256,1536]{1,0:T(8,128)(2,1)S(1)} %get-tuple-element.124), channel_id=1, source_target_pairs={{0,16},{8,24},{16,0},{24,8},{1,17},{9,25},{17,1},{25,9},{2,18},{10... | collective-permute-start | bytes 2359304 | tf_op jit(solution)/shard_map/ppermute | solution.py:19
  (140 other events, 3531.4 us)

commit v2 on v1

--- a/solution.py
+++ b/solution.py
@@ -1,6 +1,10 @@
+import math
+
 import jax
 import jax.numpy as jnp
 from jax import lax
+from jax.experimental import pallas as pl
+from jax.experimental.pallas import tpu as pltpu
 from jax.sharding import PartitionSpec as P
 
 D = 2048
@@ -353,13 +357,912 @@
     )
 
 
+def call(kernel, grid, in_specs, out_specs, out_shape, scratch=(), limit=48):
+    return pl.pallas_call(
+        kernel,
+        grid=grid,
+        in_specs=in_specs,
+        out_specs=out_specs,
+        out_shape=out_shape,
+        scratch_shapes=list(scratch),
+        compiler_params=pltpu.CompilerParams(vmem_limit_bytes=limit * 1024 * 1024),
+        cost_estimate=pl.CostEstimate(flops=1, bytes_accessed=1, transcendentals=0),
+    )
+
+
+def sds(shape, dtype):
+    return jax.ShapeDtypeStruct(shape, dtype)
+
+
+def smem():
+    return pl.BlockSpec(memory_space=pltpu.SMEM)
+
+
+def whole(array):
+    zeros = (0,) * array.ndim
+    return pl.BlockSpec(array.shape, lambda *_: zeros)
+
+
+def take_columns(places, w, count, shards, groups, pad):
+    depth = w.shape[0]
+    each = w.shape[1] // groups
+    unit = each // (shards * count)
+    tile = depth // 4
+
+    def kernel(places_ref, w_ref, o_ref):
+        for i in range(count):
+
+            @pl.when(places_ref[0] == i)
+            def _():
+                o_ref[...] = jnp.concatenate(
+                    [
+                        w_ref[:, (s * count + i) * unit : (s * count + i + 1) * unit]
+                        for s in range(shards)
+                    ],
+                    axis=1,
+                )
+
+    return call(
+        kernel,
+        (groups, 4),
+        [smem(), pl.BlockSpec((tile, each), lambda g, m: (m, g))],
+        pl.BlockSpec((tile, each // count), lambda g, m: (m, g)),
+        sds((depth + pad, w.shape[1] // count), jnp.bfloat16),
+    )(places, w)
+
+
+def spread_columns(places, near, far, count, shards, groups):
+    depth = near.shape[1]
+    each = near.shape[2] // groups
+    unit = each // shards
+    half = count // 2
+    tile = depth // 8
+
+    def kernel(places_ref, near_ref, far_ref, o_ref):
+        blocks = []
+        for i in range(count):
+            at = places_ref[1 + i]
+            block = jnp.where(
+                at < half, near_ref[jnp.minimum(at, half - 1)], far_ref[jnp.maximum(at - half, 0)]
+            )
+            blocks.append(block.astype(jnp.float32))
+        for s in range(shards):
+            o_ref[:, s * count * unit : (s + 1) * count * unit] = jnp.concatenate(
+                [block[:, s * unit : (s + 1) * unit] for block in blocks], axis=1
+            )
+
+    spec = pl.BlockSpec((half, tile, each), lambda g, m: (0, m, g))
+    return call(
+        kernel,
+        (groups, 8),
+        [smem(), spec, spec],
+        pl.BlockSpec((tile, each * count), lambda g, m: (m, g)),
+        sds((depth, groups * each * count), jnp.float32),
+    )(places, near, far)
+
+
+def spread_rows(places, near, far, count):
+    half, size, width = near.shape
+
+    def kernel(places_ref, near_ref, far_ref, o_ref):
+        at = places_ref[1 + pl.program_id(0)]
+        block = jnp.where(
+            at < half, near_ref[jnp.minimum(at, half - 1)], far_ref[jnp.maximum(at - half, 0)]
+        )
+        o_ref[...] = block.astype(jnp.float32)
+
+    return call(
+        kernel,
+        (count,),
+        [smem(), whole(near), whole(far)],
+        pl.BlockSpec((size, width), lambda m: (m, 0)),
+        sds((count * size, width), jnp.float32),
+    )(places, near, far)
+
+
+def norm_stats(values):
+    average = jnp.mean(values, axis=-1, keepdims=True)
+    centred = values - average
+    inverse = lax.rsqrt(jnp.mean(centred * centred, axis=-1, keepdims=True) + epsilon)
+    return centred * inverse, inverse
+
+
+def norm_columns(places_ref, first, gain_ref, bias_ref, normal, o_ref, plain_ref):
+    shards, depth = gain_ref.shape
+    plain_ref[...] = normal
+    for r in range(shards):
+        start = pl.multiple_of(places_ref[first + r] * depth, depth)
+        block = plain_ref[:, pl.ds(start, depth)]
+        o_ref[:, r * depth : (r + 1) * depth] = (
+            block * gain_ref[r : r + 1] + bias_ref[r : r + 1]
+        ).astype(jnp.bfloat16)
+
+
+def norm_tokens(places, tokens, gain, bias, count):
+    rows = tokens.shape[0]
+    tile = rows // 8
+
+    def kernel(places_ref, x_ref, gain_ref, bias_ref, o_ref, plain_ref):
+        normal, _ = norm_stats(x_ref[...].astype(jnp.float32))
+        norm_columns(places_ref, 1 + count, gain_ref, bias_ref, normal, o_ref, plain_ref)
+
+    spec = pl.BlockSpec((tile, D), lambda m: (m, 0))
+    return call(
+        kernel,
+        (8,),
+        [smem(), spec, whole(gain), whole(bias)],
+        spec,
+        sds((rows, D), jnp.bfloat16),
+        [pltpu.VMEM((tile, D), jnp.float32)],
+    )(places, tokens, gain, bias)
+
+
+def norm_hidden(places, tokens, pieces, gain, bias, count):
+    rows = tokens.shape[0]
+    tile = rows // 4
+
+    def kernel(places_ref, x_ref, *refs):
+        piece_refs = refs[: len(pieces)]
+        gain_ref, bias_ref, hidden_ref, o_ref, plain_ref = refs[len(pieces) :]
+        hidden = x_ref[...].astype(jnp.float32)
+        for ref in piece_refs:
+            hidden = hidden + ref[...].astype(jnp.float32)
+        hidden_ref[...] = hidden
+        normal, _ = norm_stats(hidden)
+        norm_columns(places_ref, 1 + count, gain_ref, bias_ref, normal, o_ref, plain_ref)
+
+    spec = pl.BlockSpec((tile, D), lambda m: (m, 0))
+    return call(
+        kernel,
+        (4,),
+        [smem()] + [spec] * (1 + len(pieces)) + [whole(gain), whole(bias)],
+        [spec, spec],
+        [sds((rows, D), jnp.float32), sds((rows, D), jnp.bfloat16)],
+        [pltpu.VMEM((tile, D), jnp.float32)],
+    )(places, tokens, *pieces, gain, bias)
+
+
+def norm_back(places, source, pieces, gain, added, count, low):
+    rows = source.shape[0]
+    tile = rows // 4
+    shards, depth = gain.shape
+
+    def kernel(places_ref, x_ref, added_ref, gain_ref, *refs):
+        piece_refs = refs[: len(pieces)]
+        out_refs = refs[len(pieces) : -2]
+        sums_ref = out_refs[-1]
+        grad_ref, gain_plain = refs[-2:]
+        for r in range(shards):
+            start = pl.multiple_of(places_ref[1 + count + r] * depth, depth)
+            at = slice(r * depth, (r + 1) * depth)
+            block = piece_refs[0][:, at].astype(jnp.float32)
+            for ref in piece_refs[1:]:
+                block = block + ref[:, at].astype(jnp.float32)
+            grad_ref[:, pl.ds(start, depth)] = block
+            gain_plain[:, pl.ds(start, depth)] = jnp.broadcast_to(
+                gain_ref[r : r + 1], (8, depth)
+            )
+        normal, inverse = norm_stats(x_ref[...].astype(jnp.float32))
+        grad = grad_ref[...]
+
+        @pl.when(pl.program_id(0) == 0)
+        def _():
+            sums_ref[...] = jnp.zeros_like(sums_ref)
+
+        sums_ref[0:1] += jnp.sum(grad * normal, axis=0, keepdims=True)
+        sums_ref[1:2] += jnp.sum(grad, axis=0, keepdims=True)
+        scaled = grad * gain_plain[0:1]
+        first = jnp.mean(scaled, axis=-1, keepdims=True)
+        second = jnp.mean(scaled * normal, axis=-1, keepdims=True)
+        total = added_ref[...].astype(jnp.float32) + inverse * (scaled - first - normal * second)
+        out_refs[0][...] = total
+        if low:
+            out_refs[1][...] = total.astype(jnp.bfloat16)
+
+    spec = pl.BlockSpec((tile, D), lambda m: (m, 0))
+    sums = pl.BlockSpec((2, D), lambda m: (0, 0))
+    return call(
+        kernel,
+        (4,),
+        [smem(), spec, spec, whole(gain)] + [spec] * len(pieces),
+        [spec] + [spec] * low + [sums],
+        [sds((rows, D), jnp.float32)]
+        + [sds((rows, D), jnp.bfloat16)] * low
+        + [sds((2, D), jnp.float32)],
+        [pltpu.VMEM((tile, D), jnp.float32), pltpu.VMEM((8, D), jnp.float32)],
+    )(places, source, added, gain, *pieces)
+
+
+def column_specs(parts, depth, width, at):
+    specs = []
+    for part in parts:
+        if part.ndim == 2:
+            specs.append(pl.BlockSpec((depth, width), lambda *i: (0, at(*i))))
+        else:
+            lead = part.shape[0]
+            specs.append(pl.BlockSpec((lead, depth, width), lambda *i: (0, 0, at(*i))))
+    return specs
+
+
+def times_rows(values, refs, depth):
+    total = None
+    start = 0
+    for ref in refs:
+        block = ref[...]
+        block = block.reshape(-1, block.shape[-1])
+        stop = start + block.shape[0]
+        term = jnp.dot(values[:, start:stop], block, preferred_element_type=jnp.float32)
+        total = term if total is None else total + term
+        start = stop
+    return total
+
+
+def project(normed, parts, bias, tables, depth):
+    length = normed.shape[0]
+    width = bias.shape[1] // 3
+    tile = length // 4
+
+    def kernel(x_ref, a_ref, b_ref, c_ref, d_ref, bias_ref, cos_ref, low_ref, high_ref, o_ref):
+        total = times_rows(x_ref[...], (a_ref, b_ref, c_ref, d_ref), depth) + bias_ref[...]
+
+        @pl.when(pl.program_id(0) < 2)
+        def _():
+            times = width // 128
+            cosine = jnp.concatenate([cos_ref[...]] * times, axis=1)
+            low = jnp.concatenate([low_ref[...]] * times, axis=1)
+            high = jnp.concatenate([high_ref[...]] * times, axis=1)
+            turned = (
+                total * cosine
+                + pltpu.roll(total, width - ROT // 2, 1) * low
+                + pltpu.roll(total, ROT // 2, 1) * high
+            )
+            o_ref[...] = turned.astype(jnp.bfloat16)
+
+        @pl.when(pl.program_id(0) == 2)
+        def _():
+            o_ref[...] = total.astype(jnp.bfloat16)
+
+    table = pl.BlockSpec((tile, 128), lambda n, m: (m, 0))
+    return call(
+        kernel,
+        (3, 4),
+        [pl.BlockSpec((tile, D), lambda n, m: (m, 0))]
+        + column_specs(parts, depth, width, lambda n, m: n)
+        + [pl.BlockSpec((1, width), lambda n, m: (0, n)), table, table, table],
+        pl.BlockSpec((tile, width), lambda n, m: (m, n)),
+        sds((length, 3 * width), jnp.bfloat16),
+    )(normed, *parts, bias, *tables)
+
+
+def head_lanes(values, head):
+    lanes = lax.broadcasted_iota(jnp.int32, values.shape, 1)
+    return jnp.where((lanes >= head * E) & (lanes < (head + 1) * E), values, jnp.zeros_like(values))
+
+
+def to_plain_rows(places_ref, source_ref, target_ref, count):
+    rows = target_ref.shape[0] // count
+    for b in range(count):
+        start = pl.multiple_of(places_ref[1 + b] * rows, rows)
+        target_ref[b * rows : (b + 1) * rows] = source_ref[pl.ds(start, rows)]
+
+
+def masked(scores, keys_seg, query_seg, first):
+    ks = lax.broadcasted_iota(jnp.int32, scores.shape, 0)
+    qs = lax.broadcasted_iota(jnp.int32, scores.shape, 1) + first
+    return (ks <= qs) & (keys_seg == query_seg)
+
+
+def attend(places, qkv, seg_col, seg_row, count, heads):
+    length = qkv.shape[0]
+    pairs = heads // 2
+    step = math.gcd(length, 256)
+    rows = length // count
+
+    def kernel(places_ref, q_ref, k_ref, v_ref, col_ref, row_ref, o_ref, log_ref, qs, ks, vt, os):
+        to_plain_rows(places_ref, q_ref, qs, count)
+        to_plain_rows(places_ref, k_ref, ks, count)
+        to_plain_rows(places_ref, v_ref, os, count)
+        vt[...] = jnp.transpose(os[...].astype(jnp.float32)).astype(jnp.bfloat16)
+        for a in range(length // step):
+            n = (a + 1) * step
+            halves = []
+            for h in range(2):
+                query = head_lanes(qs[a * step : n], h)
+                scores = lax.dot_general(
+                    ks[0:n], query, (((1,), (1,)), ((), ())), preferred_element_type=jnp.float32
+                )
+                allowed = masked(scores, col_ref[0:n], row_ref[:, a * step : n], a * step)
+                scores = jnp.where(allowed, scores * scale, masked_score)
+                top = jnp.max(scores, axis=0, keepdims=True)
+                weights = jnp.exp(scores - top)
+                total = jnp.sum(weights, axis=0, keepdims=True)
+                out = jnp.dot(
+                    vt[h * E : (h + 1) * E, 0:n],
+                    weights.astype(jnp.bfloat16),
+                    preferred_element_type=jnp.float32,
+                )
+                halves.append(out / total)
+                log_ref[0, h : h + 1, a * step : n] = top + jnp.log(total)
+            os[a * step : n] = jnp.transpose(jnp.concatenate(halves, axis=0)).astype(jnp.bfloat16)
+        for b in range(count):
+            start = pl.multiple_of(places_ref[1 + b] * rows, rows)
+            o_ref[pl.ds(start, rows)] = os[b * rows : (b + 1) * rows]
+
+    def columns(group):
+        return pl.BlockSpec((length, 128), lambda p: (0, group * pairs + p))
+
+    scratch = pltpu.VMEM((length, 128), jnp.bfloat16)
+    return call(
+        kernel,
+        (pairs,),
+        [smem(), columns(0), columns(1), columns(2), whole(seg_col), whole(seg_row)],
+        [columns(0), pl.BlockSpec((1, 2, length), lambda p: (p, 0, 0))],
+        [
+            sds((length, heads * E), jnp.bfloat16),
+            sds((pairs, 2, length), jnp.float32),
+        ],
+        [scratch, scratch, pltpu.VMEM((128, length), jnp.bfloat16), scratch],
+    )(places, qkv, qkv, qkv, seg_col, seg_row)
+
+
+def attend_back(places, qkv, grad_attended, logs, seg_col, seg_row, tables, count, heads):
+    length = qkv.shape[0]
+    pairs = heads // 2
+    step = math.gcd(length, 256)
+    rows = length // count
+
+    def kernel(
+        places_ref,
+        q_ref,
+        k_ref,
+        v_ref,
+        g_ref,
+        log_ref,
+        col_ref,
+        row_ref,
+        cos_ref,
+        low_ref,
+        high_ref,
+        dq_ref,
+        dk_ref,
+        dv_ref,
+        sums_ref,
+        qs,
+        ks,
+        vs,
+        gs,
+        kt,
+        dq,
+        dk,
+        dv,
+    ):
+        to_plain_rows(places_ref, q_ref, qs, count)
+        to_plain_rows(places_ref, k_ref, ks, count)
+        to_plain_rows(places_ref, v_ref, vs, count)
+        to_plain_rows(places_ref, g_ref, gs, count)
+        kt[...] = jnp.transpose(ks[...].astype(jnp.float32)).astype(jnp.bfloat16)
+        dk[...] = jnp.zeros_like(dk)
+        dv[...] = jnp.zeros_like(dv)
+        for a in range(length // step):
+            n = (a + 1) * step
+            halves = []
+            for h in range(2):
+                query = head_lanes(qs[a * step : n], h)
+                grad = head_lanes(gs[a * step : n], h)
+                scores = lax.dot_general(
+                    ks[0:n], query, (((1,), (1,)), ((), ())), preferred_element_type=jnp.float32
+                )
+                allowed = masked(scores, col_ref[0:n], row_ref[:, a * step : n], a * step)
+                log = log_ref[0, h : h + 1, a * step : n]
+                weights = jnp.exp(jnp.where(allowed, scores * scale - log, masked_score))
+                grad_weights = lax.dot_general(
+                    vs[0:n], grad, (((1,), (1,)), ((), ())), preferred_element_type=jnp.float32
+                )
+                product = weights * grad_weights
+                delta = jnp.sum(product, axis=0, keepdims=True)
+                grad_scores = (product - weights * delta).astype(jnp.bfloat16)
+                dv[0:n] += jnp.dot(
+                    weights.astype(jnp.bfloat16), grad, preferred_element_type=jnp.float32
+                )
+                dk[0:n] += jnp.dot(grad_scores, query, preferred_element_type=jnp.float32)
+                halves.append(
+                    jnp.dot(
+                        kt[h * E : (h + 1) * E, 0:n],
+                        grad_scores,
+                        preferred_element_type=jnp.float32,
+                    )
+                )
+            dq[a * step : n] = jnp.transpose(jnp.concatenate(halves, axis=0))
+
+        sums = [jnp.zeros((1, 128), jnp.float32)] * 3
+        for b in range(count):
+            start = pl.multiple_of(places_ref[1 + b] * rows, rows)
+            cosine = cos_ref[pl.ds(start, rows)]
+            low = low_ref[pl.ds(start, rows)]
+            high = high_ref[pl.ds(start, rows)]
+            for i, (part, out_ref) in enumerate(((dq, dq_ref), (dk, dk_ref), (dv, dv_ref))):
+                block = part[b * rows : (b + 1) * rows]
+                if i < 2:
+                    block = block * scale
+                    block = (
+                        block * cosine
+                        - pltpu.roll(block, 128 - ROT // 2, 1) * low
+                        - pltpu.roll(block, ROT // 2, 1) * high
+                    )
+                block = block.astype(jnp.bfloat16)
+                sums[i] = sums[i] + jnp.sum(block.astype(jnp.float32), axis=0, keepdims=True)
+                out_ref[pl.ds(start, rows)] = block
+        for i in range(3):
+            sums_ref[i] = sums[i]
+
+    def columns(group):
+        return pl.BlockSpec((length, 128), lambda p: (0, group * pairs + p))
+
+    low_scratch = pltpu.VMEM((length, 128), jnp.bfloat16)
+    scratch = pltpu.VMEM((length, 128), jnp.float32)
+    width = heads * E
+    return call(
+        kernel,
+        (pairs,),
+        [
+            smem(),
+            columns(0),
+            columns(1),
+            columns(2),
+            columns(0),
+            pl.BlockSpec((1, 2, length), lambda p: (p, 0, 0)),
+            whole(seg_col),
+            whole(seg_row),
+            whole(tables[0]),
+            whole(tables[1]),
+            whole(tables[2]),
+        ],
+        [columns(0)] * 3 + [pl.BlockSpec((3, 1, 128), lambda p: (0, 0, p))],
+        [sds((length, width), jnp.bfloat16)] * 3 + [sds((3, 1, width), jnp.float32)],
+        [low_scratch] * 4
+        + [pltpu.VMEM((128, length), jnp.bfloat16), scratch, scratch, scratch],
+    )(places, qkv, qkv, qkv, grad_attended, logs, seg_col, seg_row, *tables)
+
+
+def join_rows(places_ref, first, refs, joined):
+    size = refs[0].shape[0]
+    r = 0
+    for ref in refs:
+        if len(ref.shape) == 2:
+            blocks = [ref[...]]
+        else:
+            blocks = [ref[i] for i in range(ref.shape[0])]
+        for block in blocks:
+            start = pl.multiple_of(places_ref[first + r] * size, size)
+            joined[pl.ds(start, size)] = block
+            r += 1
+
+
+def halves_specs(tiles, tile, width):
+    half = tiles // 2
+    rows = pl.BlockSpec((tile, width), lambda m: (lax.rem(m + half, tiles), 0))
+    far = pl.BlockSpec((tile, D), lambda m: (jnp.minimum(m, half - 1), 0))
+    near = pl.BlockSpec((tile, D), lambda m: (jnp.maximum(m - half, 0), 0))
+    return rows, near, far
+
+
+def store_half(value, near_ref, far_ref, half):
+    @pl.when(pl.program_id(0) < half)
+    def _():
+        far_ref[...] = value
+
+    @pl.when(pl.program_id(0) >= half)
+    def _():
+        near_ref[...] = value
+
+
+def out_product(places, left, parts, count):
+    length, depth = left.shape
+    tile = length // 4
+    rows, near, far = halves_specs(4, tile, depth)
+
+    def kernel(places_ref, x_ref, a_ref, b_ref, c_ref, d_ref, near_ref, far_ref, joined):
+        @pl.when(pl.program_id(0) == 0)
+        def _():
+            join_rows(places_ref, 1 + count, (a_ref, b_ref, c_ref, d_ref), joined)
+
+        total = jnp.dot(x_ref[...], joined[...], preferred_element_type=jnp.float32)
+        store_half(total.astype(jnp.bfloat16), near_ref, far_ref, 2)
+
+    shape = sds((length // 2, D), jnp.bfloat16)
+    return call(
+        kernel,
+        (4,),
+        [smem(), rows] + [whole(part) for part in parts],
+        [near, far],
+        [shape, shape],
+        [pltpu.VMEM((depth, D), jnp.bfloat16)],
+    )(places, left, *parts)
+
+
+def grad_out(places, grad, parts, count):
+    length = grad.shape[0]
+    width = parts[0].shape[0] * 2 * (1 + parts[1].shape[0])
+    tile = length // 4
+
+    def kernel(places_ref, x_ref, a_ref, b_ref, c_ref, d_ref, o_ref, joined):
+        @pl.when(pl.program_id(0) == 0)
+        def _():
+            join_rows(places_ref, 1 + count, (a_ref, b_ref, c_ref, d_ref), joined)
+
+        o_ref[...] = lax.dot_general(
+            x_ref[...], joined[...], (((1,), (1,)), ((), ())), preferred_element_type=jnp.float32
+        ).astype(jnp.bfloat16)
+
+    return call(
+        kernel,
+        (4,),
+        [smem(), pl.BlockSpec((tile, D), lambda m: (m, 0))] + [whole(part) for part in parts],
+        pl.BlockSpec((tile, width), lambda m: (m, 0)),
+        sds((length, width), jnp.bfloat16),
+        [pltpu.VMEM((width, D), jnp.bfloat16)],
+    )(places, grad, *parts)
+
+
+def gate_product(normed, parts, depth):
+    length = normed.shape[0]
+    width = parts[0].shape[1]
+    units = width // 2
+    tile = length // 4
+
+    def kernel(x_ref, a_ref, b_ref, c_ref, d_ref, both_ref, activ_ref):
+        both = times_rows(x_ref[...], (a_ref, b_ref, c_ref, d_ref), depth)
+        gate = both[:, :units]
+        both_ref[...] = both.astype(jnp.bfloat16)
+        activ_ref[...] = (gate * jax.nn.sigmoid(gate) * both[:, units:]).astype(jnp.bfloat16)
+
+    return call(
+        kernel,
+        (4,),
+        [pl.BlockSpec((tile, D), lambda m: (m, 0))]
+        + column_specs(parts, depth, width, lambda m: 0),
+        [
+            pl.BlockSpec((tile, width), lambda m: (m, 0)),
+            pl.BlockSpec((tile, units), lambda m: (m, 0)),
+        ],
+        [sds((length, width), jnp.bfloat16), sds((length, units), jnp.bfloat16)],
+        limit=60,
+    )(normed, *parts)
+
+
+def gate_back(places, cotangent, parts, both, count):
+    length = cotangent.shape[0]
+    width = both.shape[1]
+    units = width // 2
+    tile = length // 4
+
+    def kernel(places_ref, x_ref, a_ref, b_ref, c_ref, d_ref, both_ref, o_ref, joined):
+        @pl.when(pl.program_id(0) == 0)
+        def _():
+            join_rows(places_ref, 1 + count, (a_ref, b_ref, c_ref, d_ref), joined)
+
+        grad = lax.dot_general(
+            x_ref[...], joined[...], (((1,), (1,)), ((), ())), preferred_element_type=jnp.float32
+        )
+        gate = both_ref[:, :units].astype(jnp.float32)
+        upward = both_ref[:, units:].astype(jnp.float32)
+        sigma = jax.nn.sigmoid(gate)
+        o_ref[:, :units] = (grad * upward * sigma * (1.0 + gate * (1.0 - sigma))).astype(
+            jnp.bfloat16
+        )
+        o_ref[:, units:] = (grad * (gate * sigma)).astype(jnp.bfloat16)
+
+    spec = pl.BlockSpec((tile, width), lambda m: (m, 0))
+    return call(
+        kernel,
+        (4,),
+        [smem(), pl.BlockSpec((tile, D), lambda m: (m, 0))]
+        + [whole(part) for part in parts]
+        + [spec],
+        spec,
+        sds((length, width), jnp.bfloat16),
+        [pltpu.VMEM((units, D), jnp.bfloat16)],
+        limit=60,
+    )(places, cotangent, *parts, both)
+
+
+def normed_grad(lefts, parts, depth):
+    length = lefts[0].shape[0]
+    width = sum(left.shape[1] for left in lefts)
+    tile = length // 4
+    rows, near, far = halves_specs(4, tile, width)
+
+    def kernel(*refs):
+        left_refs = refs[: len(lefts)]
+        part_refs = refs[len(lefts) : len(lefts) + 4]
+        near_ref, far_ref = refs[-2:]
+        left = jnp.concatenate([ref[...] for ref in left_refs], axis=1)
+        blocks = []
+        for ref in part_refs:
+            block = ref[...]
+            block = block.reshape(-1, block.shape[-1])
+            blocks.append(
+                lax.dot_general(
+                    left, block, (((1,), (1,)), ((), ())), preferred_element_type=jnp.float32
+                ).astype(jnp.bfloat16)
+            )
+        store_half(jnp.concatenate(blocks, axis=1), near_ref, far_ref, 2)
+
+    shape = sds((length // 2, D), jnp.bfloat16)
+    return call(
+        kernel,
+        (4,),
+        [pl.BlockSpec((tile, left.shape[1]), rows.index_map) for left in lefts]
+        + column_specs(parts, depth, width, lambda m: 0),
+        [near, far],
+        [shape, shape],
+        limit=60,
+    )(*lefts, *parts)
+
+
+def line_gather(block):
+    count = lax.axis_size("dp")
+    here = lax.axis_index("dp")
+    ups, downs = [block], [block]
+    for k in range(1, count):
+        ups.append(lax.ppermute(ups[-1], "dp", [(i, i + 1) for i in range(k - 1, count - 1)]))
+        downs.append(lax.ppermute(downs[-1], "dp", [(i, i - 1) for i in range(1, count - k + 1)]))
+    rest = jnp.stack(
+        [jnp.where(here + j < count, downs[j], ups[count - j]) for j in range(1, count)]
+    )
+    return rest, (ups[-1], downs[-1])
+
+
+def line_scatter(block_at):
+    count = lax.axis_size("dp")
+    up = down = None
+    for k in range(count - 1, 0, -1):
+        up_load, down_load = block_at(k), block_at(-k)
+        if up is not None:
+            up_load = (up_load.astype(jnp.float32) + up.astype(jnp.float32)).astype(jnp.bfloat16)
+            down_load = (down_load.astype(jnp.float32) + down.astype(jnp.float32)).astype(
+                jnp.bfloat16
+            )
+        up = lax.ppermute(up_load, "dp", [(i, i + 1) for i in range(count - k)])
+        down = lax.ppermute(down_load, "dp", [(i, i - 1) for i in range(k, count)])
+    total = block_at(0).astype(jnp.float32) + up.astype(jnp.float32) + down.astype(jnp.float32)
+    return total.astype(jnp.bfloat16)
+
+
+def rows_gather(block):
+    bit = lax.axis_size("ctx") // 2
+    while bit >= 1:
+        block = jnp.concatenate([block, swap(block, "ctx", bit)], axis=0)
+        bit //= 2
+    return block
+
+
+def rows_scatter(near, far):
+    count = lax.axis_size("ctx")
+    pieces = [near, swap(far, "ctx", 1)]
+    bit = 2
+    while bit < count:
+        half = pieces[0].shape[0] // 2
+        load = sum(piece[half:].astype(jnp.float32) for piece in pieces).astype(jnp.bfloat16)
+        pieces = [piece[:half] for piece in pieces] + [swap(load, "ctx", bit)]
+        bit *= 2
+    return pieces
+
+
+def blocks_gather(block):
+    near = block[None]
+    bit = lax.axis_size("ctx") // 2
+    while bit >= 2:
+        near = jnp.concatenate([near, swap(near, "ctx", bit)], axis=0)
+        bit //= 2
+    return near, swap(near, "ctx", 1)
+
+
+def fast_body(
+    tokens,
+    segment_ids,
+    cotangent,
+    ln1_gain,
+    ln1_bias,
+    w_qkv,
+    b_qkv,
+    w_out,
+    ln2_gain,
+    ln2_bias,
+    w_gate_up,
+    w_down,
+):
+    rows = tokens.shape[1]
+    count = lax.axis_size("ctx")
+    ctx = lax.axis_index("ctx")
+    far_count = lax.axis_size("dp")
+    here = lax.axis_index("dp")
+    side = lax.axis_index("fsdp")
+    shards = 2 * far_count
+    depth = D // shards
+    heads = H // count
+    width = heads * E
+    length = rows * count
+
+    def reversed_bits(value):
+        result = 0
+        bit, top = 1, count // 2
+        while bit < count:
+            result = result + jnp.where((value & bit) != 0, top, 0)
+            bit, top = bit * 2, top // 2
+        return result
+
+    row_places = [reversed_bits(b ^ ctx) for b in range(count)]
+    shard_of = [
+        ((here + j) % far_count) * 2 + (side ^ r) for r in range(2) for j in range(far_count)
+    ]
+    places = jnp.stack([ctx] + row_places + shard_of).astype(jnp.int32)
+
+    small = jnp.concatenate([ln1_gain, ln1_bias, ln2_gain, ln2_bias, b_qkv])
+    pad = 16
+    qkv_mine = take_columns(places, w_qkv, count, shards, 3, pad)
+    lead = jnp.zeros((pad, 3 * width), jnp.bfloat16)
+    lead = lax.dynamic_update_slice(lead, small[None, : 3 * width], (0, 0))
+    lead = lax.dynamic_update_slice(lead, small[None, 3 * width :], (1, 0))
+    qkv_mine = lax.dynamic_update_slice(qkv_mine, lead, (depth, 0))
+    out_mine = pick(w_out.reshape(count, -1, D), ctx, 0)
+    gate_mine = take_columns(places, w_gate_up, count, shards, 2, 0)
+    down_mine = pick(w_down.reshape(count, -1, D), ctx, 0)
+
+    def weight(block, rest):
+        return (block, rest, swap(block, "fsdp", 1), swap(rest, "fsdp", 1))
+
+    token_rows = rows_gather(tokens[0])
+    qkv_rest, last = line_gather(qkv_mine)
+    qkv_parts = weight(qkv_mine, qkv_rest)
+    out_rest, last = line_gather(tie(out_mine, *last))
+    out_parts = weight(out_mine, out_rest)
+    gate_rest, last = line_gather(tie(gate_mine, *last))
+    gate_parts = weight(gate_mine, gate_rest)
+    down_rest, last = line_gather(tie(down_mine, *last))
+    down_parts = weight(down_mine, down_rest)
+    segments = rows_gather(segment_ids)
+    cot_rows = rows_gather(tie(cotangent[0], token_rows))
+
+    segments = sum(
+        jnp.where(place == jnp.arange(count)[:, None], segments, 0).sum(0)[None, :]
+        * (jnp.arange(count)[:, None] == b)
+        for b, place in enumerate(row_places)
+    )
+    seg_row = segments.reshape(1, length)
+    seg_col = segments.reshape(length, 1)
+    base = jnp.stack([reversed_bits(jnp.int32(p)) ^ ctx for p in range(count)]) * rows
+    positions = (base[:, None] + jnp.arange(rows, dtype=jnp.int32)[None, :]).reshape(length)
+    half = ROT // 2
+    freqs = 10000.0 ** (-jnp.arange(half, dtype=jnp.float32) * 2.0 / ROT)
+    angles = positions.astype(jnp.float32)[:, None] * freqs[None, :]
+    cosine, sine = jnp.cos(angles), jnp.sin(angles)
+    rest_zero = jnp.zeros((length, E - ROT), jnp.float32)
+    zero = jnp.zeros((length, half), jnp.float32)
+    tables = (
+        jnp.concatenate([cosine, cosine, rest_zero + 1.0] * 2, axis=1),
+        jnp.concatenate([-sine, zero, rest_zero] * 2, axis=1),
+        jnp.concatenate([zero, sine, rest_zero] * 2, axis=1),
+    )
+
+    small_rows = [part.reshape(-1, depth + pad, 3 * width)[:, depth : depth + 2] for part in qkv_parts]
+    small_all = jnp.concatenate(small_rows, axis=0).reshape(shards, -1)[:, : small.shape[0]]
+    small_all = small_all.astype(jnp.float32)
+    gain_one, bias_one, gain_two, bias_two = (
+        small_all[:, i * depth : (i + 1) * depth] for i in range(4)
+    )
+    bias_rows = small_all[:, 4 * depth :]
+    bias_plain = sum(
+        (jnp.arange(shards)[:, None] == shard_of[r]) * bias_rows[r][None, :] for r in range(shards)
+    )
+    bias_mine = pick(bias_plain.reshape(3, shards, count, E), ctx, 2).reshape(1, 3 * width)
+
+    normed_one = norm_tokens(places, token_rows, gain_one, bias_one, count)
+    qkv = project(normed_one, qkv_parts, bias_mine, tables, depth)
+    attended, logs = attend(places, qkv, seg_col, seg_row, count, heads)
+    pieces = rows_scatter(*out_product(places, attended, out_parts, count))
+    hidden, normed_two = norm_hidden(places, tokens[0], pieces, gain_two, bias_two, count)
+    normed_two = rows_gather(normed_two)
+    both, activ = gate_product(normed_two, gate_parts, depth)
+
+    def row_grad(left, right):
+        part = contract_rows(left, right).astype(jnp.bfloat16).reshape(far_count, 2, -1, D)
+        arrived = swap(pick(part, 1 - side, 1), "fsdp", 1)
+        total = (pick(part, side, 1).astype(jnp.float32) + arrived.astype(jnp.float32)).astype(
+            jnp.bfloat16
+        )
+
+        def block_at(step):
+            return pick(total, jnp.clip(here + step, 0, far_count - 1), 0)
+
+        return line_scatter(block_at)
+
+    def column_grad(normed, right):
+        load = contract_rows(normed[:, D // 2 :], right).astype(jnp.bfloat16)
+        arrived = swap(load, "fsdp", 1)
+        total = contract_rows(normed[:, : D // 2], right) + arrived.astype(jnp.float32)
+        total = total.astype(jnp.bfloat16).reshape(far_count, depth, -1)
+        return line_scatter(lambda step: total[step % far_count])
+
+    down_grad = row_grad(activ, cot_rows)
+    grad_both = gate_back(places, cot_rows, down_parts, both, count)
+    gate_grad = column_grad(normed_two, grad_both)
+    pieces = rows_scatter(*normed_grad([grad_both], gate_parts, depth))
+    grad_hidden, grad_branch, sums_two = norm_back(
+        places, hidden, pieces, gain_two, cotangent[0], count, True
+    )
+    grad_branch = rows_gather(grad_branch)
+    grad_attended = grad_out(places, grad_branch, out_parts, count)
+    out_grad = row_grad(attended, grad_branch)
+    grad_q, grad_k, grad_v, bias_sums = attend_back(
+        places, qkv, grad_attended, logs, seg_col, seg_row, tables, count, heads
+    )
+    qkv_grad = column_grad(normed_one, jnp.concatenate([grad_q, grad_k, grad_v], axis=1))
+    pieces = rows_scatter(*normed_grad([grad_q, grad_k, grad_v], qkv_parts, depth))
+    input_grad, sums_one = norm_back(
+        places, tokens[0], pieces, gain_one, grad_hidden, count, False
+    )
+
+    mixed_pieces = rows_scatter(*out_product(places, tie(activ, grad_branch), down_parts, count))
+    mixed = hidden + sum(piece[:rows].astype(jnp.float32) for piece in mixed_pieces)
+
+    down_out = spread_rows(places, *blocks_gather(down_grad), count)
+    gate_out = spread_columns(places, *blocks_gather(gate_grad), count, shards, 2)
+    out_out = spread_rows(places, *blocks_gather(out_grad), count)
+    qkv_out = spread_columns(places, *blocks_gather(qkv_grad), count, shards, 3)
+
+    bias_part = jnp.where(
+        jnp.arange(count)[None, None, :, None] == ctx, bias_sums.reshape(3, shards, 1, E), 0.0
+    ).reshape(shards, 3 * depth)
+    small_part = jnp.concatenate(
+        [part.reshape(shards, depth) for part in (*sums_one, *sums_two)] + [bias_part], axis=1
+    ).reshape(far_count, 2, -1)
+    load = pick(small_part, 1 - side, 1).astype(jnp.bfloat16)
+    total = pick(small_part, side, 1) + swap(load, "fsdp", 1).astype(jnp.float32)
+    mine = pick(total, here, 0)
+    low_total = total.astype(jnp.bfloat16)
+    for r in range(1, far_count):
+        mine = mine + swap(pick(low_total, here ^ r, 0), "dp", r).astype(jnp.float32)
+    bit = count // 2
+    while bit >= 1:
+        mine = mine + swap(mine, "ctx", bit)
+        bit //= 2
+
+    return (
+        mixed.astype(jnp.bfloat16)[None],
+        input_grad[None],
+        mine[:depth],
+        mine[depth : 2 * depth],
+        qkv_out,
+        mine[4 * depth :],
+        out_out,
+        mine[2 * depth : 3 * depth],
+        mine[3 * depth : 4 * depth],
+        gate_out,
+        down_out,
+    )
+
+
+def fits(mesh):
+    count, shards = mesh.shape["ctx"], mesh.shape["dp"] * mesh.shape["fsdp"]
+    return (
+        mesh.shape["fsdp"] == 2
+        and count > 1
+        and count & (count - 1) == 0
+        and (H // shards) == count
+        and (FF // shards) % (16 * count) == 0
+        and (FF // count) % 128 == 0
+        and (H // count) % 2 == 0
+    )
+
+
 def solution(mesh):
     shards = ("dp", "fsdp")
     row = P(shards, "ctx", None)
     vector = P(shards)
     matrix = P(shards, None)
     return jax.shard_map(
-        body,
+        fast_body if fits(mesh) else body,
         mesh=mesh,
         in_specs=(
             row,

time: 1630 us -> 1030 us (0.63)
  waiting for transfers between devices: 740 us -> 453 us
  other arithmetic: 302 us -> 79.1 us
  Pallas kernels: 0 us -> 212 us
  matrix products: 219 us -> 41.2 us
  local copies, waits for them, and re-layouts: 246 us -> 83.9 us
  starting transfers between devices: 113 us -> 149 us
    ppermute x99 -> x44, waiting for transfers between devices: 740 us -> 282 us  [swap(): return lax.ppermute(block, axis, [(i, i ^ bit) for i in range(count)])]
    pallas_call x0 -> x20, Pallas kernels: none -> 212 us  [the longest x2 32.1 us: normed_grad(): call(kernel, (4,), [pl.BlockSpec((tile, left.shape[1]), rows.index_map) f...]
    ppermute x0 -> x48, waiting for transfers between devices: none -> 171 us  [the longest x12 119 us: line_gather(): lax.ppermute(downs[-1], 'dp', [(i, i - 1) for i in range(1, count - k + 1)])]
    dot_general x13 -> x0, matrix products: 160 us -> none  [the longest x4 49.5 us: contract_cols(): lax.dot_general(left, right, (((1,), (1,)), ((), ())), preferred_element_...]
    ppermute x0 -> x48, starting transfers between devices: none -> 108 us  [the longest x12 45.3 us: line_scatter(): up = lax.ppermute(up_load, 'dp', [(i, i + 1) for i in range(count - k)])]
    ppermute x99 -> x44, starting transfers between devices: 113 us -> 41.6 us  [swap(): return lax.ppermute(block, axis, [(i, i ^ bit) for i in range(count)])]
    select_n x40 -> x1, other arithmetic: 67.5 us -> 0.08 us  [fast_body(): jnp.where(jnp.arange(count)[None, None, :, None] == ctx, bias_sums.reshap...]
    unnamed x199 -> x149, local copies, waits for them, and re-layouts: 101 us -> 37.4 us
  transfers between devices with their start and end apart: 99 -> 92, of which waited for: 36 -> 24; matrix products, arithmetic and copies ran while one was open for 39% -> 17% of each run, Pallas kernels for 0% -> 19%
where the time goes in v2:
time: 1030 us; the launch traced here: 1020 us
  waiting for transfers between devices  453 us (44%)
  Pallas kernels  212 us (21%)
  starting transfers between devices  149 us (14%)
  local copies, waits for them, and re-layouts  83.9 us (8%)
  other arithmetic  79.1 us (8%)
  matrix products  41.2 us (4%)
    ppermute x44, waiting for transfers between devices, swap(): return lax.ppermute(block, axis, [(i, i ^ bit) for i in range(count)])  282 us
    ppermute x12, waiting for transfers between devices, line_gather(): lax.ppermute(downs[-1], 'dp', [(i, i - 1) for i in range(1, count - k + 1)])  119 us
    ppermute x12, waiting for transfers between devices, line_scatter(): up = lax.ppermute(up_load, 'dp', [(i, i + 1) for i in range(count - k)])  52 us
    ppermute x12, starting transfers between devices, line_scatter(): up = lax.ppermute(up_load, 'dp', [(i, i + 1) for i in range(count - k)])  45.3 us
    ppermute x44, starting transfers between devices, swap(): return lax.ppermute(block, axis, [(i, i ^ bit) for i in range(count)])  41.6 us
    dot_general x6, matrix products, contract_rows(): lax.dot_general(left, right, (((0,), (0,)), ((), ())), preferred_element_...  41.2 us
    unnamed x149, local copies, waits for them, and re-layouts  37.4 us
    pallas_call x2, Pallas kernels, normed_grad(): call(kernel, (4,), [pl.BlockSpec((tile, left.shape[1]), rows.index_map) f...  32.1 us
  transfers between devices with their start and end apart: 92, of which 24 were waited for; matrix products, arithmetic and copies ran while one was open for 17% of the time, Pallas kernels for 19%

profile of v2, /device:TPU:0, one launch (start us, length us, event | category | flops | bytes accessed | tf_op | source)
XLA Modules:
  0.0 1020.3 jit_solution(841549654942126857)
XLA Ops:
  24.1 11.9 %collective-permute-done.2 = bf16[272,1536]{1,0:T(8,128)(2,1)} collective-permute-done((bf16[272,1536]{1,0:T(8,128)(2,1)}, bf16[272,1536]{1,0:T(8,128)(2,1)}, u32[]{:S(2)}, u32[]{:S(2)}) %collective-permute-start.2) | collective-permute-done | bytes 835616 | tf_op jit(solution)/shard_map/ppermute | solution.py:1009
  74.8 19.5 %collective-permute-done.7 = bf16[272,1536]{1,0:T(8,128)(2,1)S(1)} collective-permute-done((bf16[272,1536]{1,0:T(8,128)(2,1)}, bf16[272,1536]{1,0:T(8,128)(2,1)S(1)}, u32[]{:S(2)}, u32[]{:S(2)}) %collective-permute-start.7) | collective-permute-done | bytes 835616 | tf_op jit(solution)/shard_map/ppermute | solution.py:1009
  132.9 18.1 %collective-permute-done.24 = bf16[256,2816]{1,0:T(8,128)(2,1)} collective-permute-done((bf16[256,2816]{1,0:T(8,128)(2,1)S(1)}, bf16[256,2816]{1,0:T(8,128)(2,1)}, u32[]{:S(2)}, u32[]{:S(2)}) %collective-permute-start.24) | collective-permute-done | bytes 1441824 | tf_op jit(solution)/shard_map/ppermute | solution.py:1009
  187.7 16.8 %shard_map.205.q_ref.k_ref.v_ref = bf16[1024,1536]{1,0:T(8,128)(2,1)} custom-call(bf16[1024,2048]{1,0:T(8,128)(2,1)} %copy-done.5, bf16[272,1536]{1,0:T(8,128)(2,1)S(1)} %copy-done.15, bf16[3,272,1536]{2,1,0:T(8,128)(2,1)S(1)} %copy-done.4, bf16[272,1536]{1,0:T(8,128)(2,1)} %collective-permute-done.8.c_ref.refs_5_, bf16[3,272,1536]{2,1,0:T(8,128)(2,1)} %copy-done.39, ...), custom_call_target="tpu_custom_call" | custom-call | flops 1 | bytes 1 | tf_op jit(solution)/shard_map/pallas_call | solution.py:626
  206.4 17.5 %shard_map.206 = (bf16[1024,512]{1,0:T(8,128)(2,1)S(1)}, f32[4,2,1024]{2,1,0:T(2,128)S(1)}) custom-call(s32[13]{0:T(128)S(1)} %stack.116.places_ref, bf16[1024,1536]{1,0:T(8,128)(2,1)S(1)} %copy-done.2, bf16[1024,1536]{1,0:T(8,128)(2,1)S(1)} %copy-done.2, bf16[1024,1536]{1,0:T(8,128)(2,1)S(1)} %copy-done.2, s32[1024,1]{1,0:T(8,128)S(1)} %bitcast.151, ...), custom_call_target="tpu_custom_call" | custom-call | flops 1 | bytes 1 | tf_op jit(solution)/shard_map/pallas_call | solution.py:695
  239.5 27.6 %collective-permute-done.29 = bf16[256,2816]{1,0:T(8,128)(2,1)S(1)} collective-permute-done((bf16[256,2816]{1,0:T(8,128)(2,1)}, bf16[256,2816]{1,0:T(8,128)(2,1)S(1)}, u32[]{:S(2)}, u32[]{:S(2)}) %collective-permute-start.29) | collective-permute-done | bytes 1441824 | tf_op jit(solution)/shard_map/ppermute | solution.py:1009
  291.0 7.3 collective-permute-done.34
  306.6 10.3 %collective-permute-done.38 = bf16[176,2048]{1,0:T(8,128)(2,1)S(1)} collective-permute-done((bf16[176,2048]{1,0:T(8,128)(2,1)}, bf16[176,2048]{1,0:T(8,128)(2,1)S(1)}, u32[]{:S(2)}, u32[]{:S(2)}) %collective-permute-start.38) | collective-permute-done | bytes 720928 | tf_op jit(solution)/shard_map/ppermute | solution.py:1009
  320.8 13.6 %collective-permute-done.39 = bf16[176,2048]{1,0:T(8,128)(2,1)S(1)} collective-permute-done((bf16[176,2048]{1,0:T(8,128)(2,1)S(1)}, bf16[176,2048]{1,0:T(8,128)(2,1)S(1)}, u32[]{:S(2)}, u32[]{:S(2)}) %collective-permute-start.39) | collective-permute-done | bytes 720928 | tf_op jit(solution)/shard_map/ppermute | solution.py:1009
  339.4 59.1 %collective-permute-done.30.c_ref.refs_3_ = bf16[256,2816]{1,0:T(8,128)(2,1)S(1)} collective-permute-done((bf16[256,2816]{1,0:T(8,128)(2,1)S(1)}, bf16[256,2816]{1,0:T(8,128)(2,1)S(1)}, u32[]{:S(2)}, u32[]{:S(2)}) %collective-permute-start.30) | collective-permute-done | bytes 1441824 | tf_op jit(solution)/shard_map/ppermute | solution.py:23
  399.6 18.8 %shard_map.210 = (bf16[1024,2816]{1,0:T(8,128)(2,1)}, bf16[1024,1408]{1,0:T(8,128)(2,1)}) custom-call(bf16[1024,2048]{1,0:T(8,128)(2,1)} %copy-done.44, bf16[256,2816]{1,0:T(8,128)(2,1)} %copy-done.11, bf16[3,256,2816]{2,1,0:T(8,128)(2,1)} %pad_maximum_fusion.b_ref.refs_2_, bf16[256,2816]{1,0:T(8,128)(2,1)} %copy-done.47, ...), custom_call_target="tpu_custom_call" | custom-call | flops 1 | bytes 1 | tf_op jit(solution)/shard_map/pallas_call | solution.py:919
  418.5 8.9 convolution_convert_fusion
  432.8 88.3 %collective-permute-done.40.c_ref = bf16[176,2048]{1,0:T(8,128)(2,1)S(1)} collective-permute-done((bf16[176,2048]{1,0:T(8,128)(2,1)}, bf16[176,2048]{1,0:T(8,128)(2,1)S(1)}, u32[]{:S(2)}, u32[]{:S(2)}) %collective-permute-start.40) | collective-permute-done | bytes 720928 | tf_op jit(solution)/shard_map/ppermute | solution.py:23
  521.9 13.7 %shard_map.211.refs_0_ = bf16[1024,2816]{1,0:T(8,128)(2,1)} custom-call(s32[13]{0:T(128)} %copy-done.34, bf16[1024,2048]{1,0:T(8,128)(2,1)} %constant_dynamic-update-slice_fusion.3.x_ref, bf16[176,2048]{1,0:T(8,128)(2,1)} %dynamic-slice_bitcast_fusion.4.a_ref, bf16[3,176,2048]{2,1,0:T(8,128)(2,1)} %pad_maximum_fusion.4.b_ref, bf16[176,2048]{1,0:T(8,128)(2,1)} %copy-done.27, ...), custom_call_target="tpu_custom_call" | custom-call | flops 1 | bytes 1 | tf_op jit(solution)/shard_map/pallas_call | solution.py:956
  535.7 19.3 %shard_map.212 = (bf16[512,2048]{1,0:T(8,128)(2,1)}, bf16[512,2048]{1,0:T(8,128)(2,1)}) custom-call(bf16[1024,2816]{1,0:T(8,128)(2,1)} %shard_map.211.refs_0_, bf16[256,2816]{1,0:T(8,128)(2,1)} %copy-done.11, bf16[3,256,2816]{2,1,0:T(8,128)(2,1)} %pad_maximum_fusion.b_ref.refs_2_, bf16[256,2816]{1,0:T(8,128)(2,1)} %copy-done.47, ...), custom_call_target="tpu_custom_call" | custom-call | flops 1 | bytes 1 | tf_op jit(solution)/shard_map/pallas_call | solution.py:992
  555.0 11.3 %convolution_convert_fusion.1 = bf16[1024,2816]{1,0:T(8,128)(2,1)} fusion(bf16[1024,2816]{1,0:T(8,128)(2,1)} %shard_map.211.refs_0_, bf16[1024,2048]{1,0:T(8,128)(2,1)} %copy-done.44), kind=kOutput, calls=%fused_computation.5 | convolution fusion | flops 5908463616 | bytes 13631488 | tf_op jit(solution)/shard_map/dot_general | solution.py:137
  577.7 13.4 %collective-permute-done.84 = bf16[176,2048]{1,0:T(8,128)(2,1)} collective-permute-done((bf16[176,2048]{1,0:T(8,128)(2,1)}, bf16[176,2048]{1,0:T(8,128)(2,1)}, u32[]{:S(2)}, u32[]{:S(2)}) %collective-permute-start.84) | collective-permute-done | bytes 720928 | tf_op jit(solution)/shard_map/ppermute | solution.py:1026
  602.7 10.2 collective-permute-done.85
  638.7 16.1 %collective-permute-done.44 = bf16[256,2048]{1,0:T(8,128)(2,1)S(1)} collective-permute-done((bf16[256,2048]{1,0:T(8,128)(2,1)}, bf16[256,2048]{1,0:T(8,128)(2,1)S(1)}, u32[]{:S(2)}, u32[]{:S(2)}) %collective-permute-start.44) | collective-permute-done | bytes 1048608 | tf_op jit(solution)/shard_map/ppermute | solution.py:23
  660.4 32.8 %collective-permute-done.74 = bf16[1024,2816]{1,0:T(8,128)(2,1)} collective-permute-done((bf16[1024,2816]{1,0:T(8,128)(2,1)}, bf16[1024,2816]{1,0:T(8,128)(2,1)}, u32[]{:S(2)}, u32[]{:S(2)}) %collective-permute-start.74) | collective-permute-done | bytes 5767200 | tf_op jit(solution)/shard_map/ppermute | solution.py:23
  693.2 8.6 add_convert_fusion
  723.4 22.1 %shard_map.216 = (bf16[1024,512]{1,0:T(8,128)(2,1)S(1)}, bf16[1024,512]{1,0:T(8,128)(2,1)S(1)}, bf16[1024,512]{1,0:T(8,128)(2,1)S(1)}, f32[3,1,512]{2,1,0:T(1,128)S(1)}) custom-call(s32[13]{0:T(128)S(1)} %copy-done.35, bf16[1024,1536]{1,0:T(8,128)(2,1)} %shard_map.205.q_ref.k_ref.v_ref, bf16[1024,1536]{1,0:T(8,128)(2,1)} %shard_map.205.q_ref.k_ref.v_ref, ...), custom_call_target="tpu_custom_call" | custom-call | flops 1 | bytes 1 | tf_op jit(solution)/shard_map/pallas_call | solution.py:804
  772.0 12.8 %shard_map.217 = (bf16[512,2048]{1,0:T(8,128)(2,1)}, bf16[512,2048]{1,0:T(8,128)(2,1)}) custom-call(bf16[1024,512]{1,0:T(8,128)(2,1)} %copy-done.22, bf16[1024,512]{1,0:T(8,128)(2,1)} %copy-done.23, bf16[1024,512]{1,0:T(8,128)(2,1)} %copy-done.24, bf16[272,1536]{1,0:T(8,128)(2,1)} %constant_dynamic-update-slice_fusion.17.a_ref.refs_3_, ...), custom_call_target="tpu_custom_call" | custom-call | flops 1 | bytes 1 | tf_op jit(solution)/shard_map/pallas_call | solution.py:992
  784.8 10.9 %shard_map.214 = (bf16[512,2048]{1,0:T(8,128)(2,1)S(1)}, bf16[512,2048]{1,0:T(8,128)(2,1)S(1)}) custom-call(s32[13]{0:T(128)S(1)} %copy-done.35, bf16[1024,1408]{1,0:T(8,128)(2,1)} %get-tuple-element.53.x_ref, bf16[176,2048]{1,0:T(8,128)(2,1)} %dynamic-slice_bitcast_fusion.4.a_ref, bf16[3,176,2048]{2,1,0:T(8,128)(2,1)} %pad_maximum_fusion.4.b_ref, ...), custom_call_target="tpu_custom_call" | custom-call | flops 1 | bytes 1 | tf_op jit(solution)/shard_map/pallas_call | solution.py:873
  808.5 7.8 collective-permute-start.77
  816.3 9.2 collective-permute-done.56
  836.6 28.3 %collective-permute-done.57 = bf16[256,1536]{1,0:T(8,128)(2,1)S(1)} collective-permute-done((bf16[256,1536]{1,0:T(8,128)(2,1)S(1)}, bf16[256,1536]{1,0:T(8,128)(2,1)S(1)}, u32[]{:S(2)}, u32[]{:S(2)}) %collective-permute-start.57) | collective-permute-done | bytes 786464 | tf_op jit(solution)/shard_map/ppermute | solution.py:1026
  881.6 10.8 %collective-permute-done.49.refs_2_ = bf16[256,2048]{1,0:T(8,128)(2,1)S(1)} collective-permute-done((bf16[256,2048]{1,0:T(8,128)(2,1)S(1)}, bf16[256,2048]{1,0:T(8,128)(2,1)S(1)}, u32[]{:S(2)}, u32[]{:S(2)}) %collective-permute-start.49) | collective-permute-done | bytes 1048608 | tf_op jit(solution)/shard_map/ppermute | solution.py:23
  908.4 15.0 %collective-permute-done.81 = bf16[1,256,2816]{2,1,0:T(8,128)(2,1)} collective-permute-done((bf16[1,256,2816]{2,1,0:T(8,128)(2,1)}, bf16[1,256,2816]{2,1,0:T(8,128)(2,1)}, u32[]{:S(2)}, u32[]{:S(2)}) %collective-permute-start.81) | collective-permute-done | bytes 1441824 | tf_op jit(solution)/shard_map/ppermute | solution.py:23
  934.5 32.0 %collective-permute-done.72 = bf16[1,64,2048]{2,1,0:T(8,128)(2,1)S(1)} collective-permute-done((bf16[1,64,2048]{2,1,0:T(8,128)(2,1)S(1)}, bf16[1,64,2048]{2,1,0:T(8,128)(2,1)S(1)}, u32[]{:S(2)}, u32[]{:S(2)}) %collective-permute-start.72) | collective-permute-done | bytes 262176 | tf_op jit(solution)/shard_map/ppermute | solution.py:23
  990.0 14.8 %shard_map.219 = f32[256,6144]{1,0:T(8,128)} custom-call(s32[13]{0:T(128)S(1)} %copy-done.35, bf16[2,256,1536]{2,1,0:T(8,128)(2,1)} %pad_maximum_fusion.9.near_ref, bf16[2,256,1536]{2,1,0:T(8,128)(2,1)} %collective-permute-done.64.far_ref), custom_call_target="tpu_custom_call" | custom-call | flops 1 | bytes 1 | tf_op jit(solution)/shard_map/pallas_call | solution.py:435
  1004.8 15.4 %shard_map.221 = f32[256,11264]{1,0:T(8,128)} custom-call(s32[13]{0:T(128)S(1)} %copy-done.35, bf16[2,256,2816]{2,1,0:T(8,128)(2,1)} %pad_maximum_fusion.2.near_ref, bf16[2,256,2816]{2,1,0:T(8,128)(2,1)} %collective-permute-done.82.far_ref), custom_call_target="tpu_custom_call" | custom-call | flops 1 | bytes 1 | tf_op jit(solution)/shard_map/pallas_call | solution.py:435
  (492 shorter events, 395.6 us)
Async XLA Ops:
  19.9 85.7 %collective-permute-start.8 = (bf16[272,1536]{1,0:T(8,128)(2,1)}, bf16[272,1536]{1,0:T(8,128)(2,1)}, u32[]{:S(2)}, u32[]{:S(2)}) collective-permute-start(bf16[272,1536]{1,0:T(8,128)(2,1)} %constant_dynamic-update-slice_fusion.17.a_ref.refs_3_), channel_id=1, source_target_pairs={{0,1},{1,0},{2,3},{3,2},{4,5},{5,4},{6,7},{7,6},{8,9},{9,8},{10,11... | collective-permute-start | bytes 2506760 | tf_op jit(solution)/shard_map/ppermute | solution.py:23
  21.8 49.4 %collective-permute-start = (bf16[256,2048]{1,0:T(8,128)(2,1)}, bf16[256,2048]{1,0:T(8,128)(2,1)}, u32[]{:S(2)}, u32[]{:S(2)}) collective-permute-start(bf16[256,2048]{1,0:T(8,128)(2,1)} %bitcast.145), channel_id=1, source_target_pairs={{0,4},{2,6},{4,0},{6,2},{1,5},{3,7},{5,1},{7,3},{8,12},{10,14},{12... | collective-permute-start | bytes 3145736 | tf_op jit(solution)/shard_map/ppermute | solution.py:23
  23.4 47.7 %collective-permute-start.10 = (s32[1,256]{1,0:T(1,128)S(1)}, s32[1,256]{1,0:T(1,128)S(1)}, u32[]{:S(2)}, u32[]{:S(2)}) collective-permute-start(s32[1,256]{1,0:T(1,128)S(1)} %copy-done.58), channel_id=1, source_target_pairs={{0,4},{2,6},{4,0},{6,2},{1,5},{3,7},{5,1},{7,3},{8,12},{10,14},{12... | collective-permute-start | bytes 3080 | tf_op jit(solution)/shard_map/ppermute | solution.py:23
  73.0 53.9 %collective-permute-start.1 = (bf16[512,2048]{1,0:T(8,128)(2,1)S(1)}, bf16[512,2048]{1,0:T(8,128)(2,1)S(1)}, u32[]{:S(2)}, u32[]{:S(2)}) collective-permute-start(bf16[512,2048]{1,0:T(8,128)(2,1)S(1)} %pad_maximum_fusion.5), channel_id=1, source_target_pairs={{0,2},{2,0},{4,6},{6,4},{1,3},{3,1},{5,7},{7,5},{8,10},{10,8},{12,... | collective-permute-start | bytes 6291464 | tf_op jit(solution)/shard_map/ppermute | solution.py:23
  101.8 57.4 %collective-permute-start.9 = (bf16[3,272,1536]{2,1,0:T(8,128)(2,1)S(1)}, bf16[3,272,1536]{2,1,0:T(8,128)(2,1)S(1)}, u32[]{:S(2)}, u32[]{:S(2)}) collective-permute-start(bf16[3,272,1536]{2,1,0:T(8,128)(2,1)S(1)} %pad_maximum_fusion.3.b_ref.refs_4_), channel_id=1, source_target_pairs={{0,1},{1,0},{2,3},{3,2},{4,5},{5,4},{6,7},{7,6},{8,9},{9,8},{10,11... | collective-permute-start | bytes 7520264 | tf_op jit(solution)/shard_map/ppermute | solution.py:23
  105.6 118.3 %collective-permute-start.18 = (bf16[64,2048]{1,0:T(8,128)(2,1)}, bf16[64,2048]{1,0:T(8,128)(2,1)}, u32[]{:S(2)}, u32[]{:S(2)}) collective-permute-start(bf16[64,2048]{1,0:T(8,128)(2,1)} %dynamic-slice_bitcast_fusion.7.a_ref), channel_id=1, source_target_pairs={{0,1},{1,0},{2,3},{3,2},{4,5},{5,4},{6,7},{7,6},{8,9},{9,8},{10,11... | collective-permute-start | bytes 786440 | tf_op jit(solution)/shard_map/ppermute | solution.py:23
  130.2 101.4 %collective-permute-start.32 = (bf16[256,2048]{1,0:T(8,128)(2,1)}, bf16[256,2048]{1,0:T(8,128)(2,1)}, u32[]{:S(2)}, u32[]{:S(2)}) collective-permute-start(bf16[256,2048]{1,0:T(8,128)(2,1)} %bitcast.30.added_ref), channel_id=1, source_target_pairs={{0,4},{2,6},{4,0},{6,2},{1,5},{3,7},{5,1},{7,3},{8,12},{10,14},{12... | collective-permute-start | bytes 3145736 | tf_op jit(solution)/shard_map/ppermute | solution.py:23
  150.9 73.0 %collective-permute-start.19 = (bf16[3,64,2048]{2,1,0:T(8,128)(2,1)}, bf16[3,64,2048]{2,1,0:T(8,128)(2,1)}, u32[]{:S(2)}, u32[]{:S(2)}) collective-permute-start(bf16[3,64,2048]{2,1,0:T(8,128)(2,1)} %pad_maximum_fusion.11.b_ref), channel_id=1, source_target_pairs={{0,1},{1,0},{2,3},{3,2},{4,5},{5,4},{6,7},{7,6},{8,9},{9,8},{10,11... | collective-permute-start | bytes 2359304 | tf_op jit(solution)/shard_map/ppermute | solution.py:23
  151.9 78.5 %collective-permute-start.28 = (bf16[256,2816]{1,0:T(8,128)(2,1)}, bf16[256,2816]{1,0:T(8,128)(2,1)}, u32[]{:S(2)}, u32[]{:S(2)}) collective-permute-start(bf16[256,2816]{1,0:T(8,128)(2,1)} %collective-permute-done.24), channel_id=1, source_target_pairs={{8,0},{16,8},{9,1},{17,9},{10,2},{18,10},{11,3},{19,11},{12,4},{20... | collective-permute-start | bytes 4325384 | tf_op jit(solution)/shard_map/ppermute | solution.py:1009
  159.2 76.1 %collective-permute-start.26 = (bf16[256,2816]{1,0:T(8,128)(2,1)}, bf16[256,2816]{1,0:T(8,128)(2,1)}, u32[]{:S(2)}, u32[]{:S(2)}) collective-permute-start(bf16[256,2816]{1,0:T(8,128)(2,1)} %collective-permute-done.25), channel_id=1, source_target_pairs={{8,16},{16,24},{9,17},{17,25},{10,18},{18,26},{11,19},{19,27},{12,... | collective-permute-start | bytes 4325384 | tf_op jit(solution)/shard_map/ppermute | solution.py:1008
  234.8 55.3 %collective-permute-start.33 = (bf16[512,2048]{1,0:T(8,128)(2,1)}, bf16[512,2048]{1,0:T(8,128)(2,1)}, u32[]{:S(2)}, u32[]{:S(2)}) collective-permute-start(bf16[512,2048]{1,0:T(8,128)(2,1)} %pad_maximum_fusion.7), channel_id=1, source_target_pairs={{0,2},{2,0},{4,6},{6,4},{1,3},{3,1},{5,7},{7,5},{8,10},{10,8},{12,... | collective-permute-start | bytes 6291464 | tf_op jit(solution)/shard_map/ppermute | solution.py:23
  271.1 127.4 %collective-permute-start.31 = (bf16[3,256,2816]{2,1,0:T(8,128)(2,1)}, bf16[3,256,2816]{2,1,0:T(8,128)(2,1)}, u32[]{:S(2)}, u32[]{:S(2)}) collective-permute-start(bf16[3,256,2816]{2,1,0:T(8,128)(2,1)} %pad_maximum_fusion.b_ref.refs_2_), channel_id=1, source_target_pairs={{0,1},{1,0},{2,3},{3,2},{4,5},{5,4},{6,7},{7,6},{8,9},{9,8},{10,11... | collective-permute-start | bytes 12976136 | tf_op jit(solution)/shard_map/ppermute | solution.py:23
  290.1 108.4 %collective-permute-start.30 = (bf16[256,2816]{1,0:T(8,128)(2,1)S(1)}, bf16[256,2816]{1,0:T(8,128)(2,1)S(1)}, u32[]{:S(2)}, u32[]{:S(2)}) collective-permute-start(bf16[256,2816]{1,0:T(8,128)(2,1)S(1)} %copy-done.13), channel_id=1, source_target_pairs={{0,1},{1,0},{2,3},{3,2},{4,5},{5,4},{6,7},{7,6},{8,9},{9,8},{10,11... | collective-permute-start | bytes 4325384 | tf_op jit(solution)/shard_map/ppermute | solution.py:23
  337.3 183.7 %collective-permute-start.41 = (bf16[3,176,2048]{2,1,0:T(8,128)(2,1)}, bf16[3,176,2048]{2,1,0:T(8,128)(2,1)}, u32[]{:S(2)}, u32[]{:S(2)}) collective-permute-start(bf16[3,176,2048]{2,1,0:T(8,128)(2,1)} %pad_maximum_fusion.4.b_ref), channel_id=1, source_target_pairs={{0,1},{1,0},{2,3},{3,2},{4,5},{5,4},{6,7},{7,6},{8,9},{9,8},{10,11... | collective-permute-start | bytes 6488072 | tf_op jit(solution)/shard_map/ppermute | solution.py:23
  430.7 137.1 %collective-permute-start.83 = (bf16[4,176,2048]{2,1,0:T(8,128)(2,1)}, bf16[4,176,2048]{2,1,0:T(8,128)(2,1)}, u32[]{:S(2)}, u32[]{:S(2)}) collective-permute-start(bf16[4,176,2048]{2,1,0:T(8,128)(2,1)} %dynamic-slice_bitcast_fusion), channel_id=1, source_target_pairs={{0,1},{1,0},{2,3},{3,2},{4,5},{5,4},{6,7},{7,6},{8,9},{9,8},{10,11... | collective-permute-start | bytes 8650760 | tf_op jit(solution)/shard_map/ppermute | solution.py:23
  432.2 88.8 %collective-permute-start.40 = (bf16[176,2048]{1,0:T(8,128)(2,1)}, bf16[176,2048]{1,0:T(8,128)(2,1)S(1)}, u32[]{:S(2)}, u32[]{:S(2)}) collective-permute-start(bf16[176,2048]{1,0:T(8,128)(2,1)} %dynamic-slice_bitcast_fusion.4.a_ref), channel_id=1, source_target_pairs={{0,1},{1,0},{2,3},{3,2},{4,5},{5,4},{6,7},{7,6},{8,9},{9,8},{10,11... | collective-permute-start | bytes 2162696 | tf_op jit(solution)/shard_map/ppermute | solution.py:23
  555.0 43.6 %collective-permute-start.42 = (bf16[512,2048]{1,0:T(8,128)(2,1)}, bf16[512,2048]{1,0:T(8,128)(2,1)}, u32[]{:S(2)}, u32[]{:S(2)}) collective-permute-start(bf16[512,2048]{1,0:T(8,128)(2,1)} %get-tuple-element.51), channel_id=1, source_target_pairs={{0,2},{2,0},{4,6},{6,4},{1,3},{3,1},{5,7},{7,5},{8,10},{10,8},{12,... | collective-permute-start | bytes 6291464 | tf_op jit(solution)/shard_map/ppermute | solution.py:23
  566.3 126.9 %collective-permute-start.74 = (bf16[1024,2816]{1,0:T(8,128)(2,1)}, bf16[1024,2816]{1,0:T(8,128)(2,1)}, u32[]{:S(2)}, u32[]{:S(2)}) collective-permute-start(bf16[1024,2816]{1,0:T(8,128)(2,1)} %convolution_convert_fusion.1), channel_id=1, source_target_pairs={{0,1},{1,0},{2,3},{3,2},{4,5},{5,4},{6,7},{7,6},{8,9},{9,8},{10,11... | collective-permute-start | bytes 17301512 | tf_op jit(solution)/shard_map/ppermute | solution.py:23
  656.2 45.6 %collective-permute-start.45 = (bf16[512,2048]{1,0:T(8,128)(2,1)S(1)}, bf16[512,2048]{1,0:T(8,128)(2,1)S(1)}, u32[]{:S(2)}, u32[]{:S(2)}) collective-permute-start(bf16[512,2048]{1,0:T(8,128)(2,1)S(1)} %pad_maximum_fusion.8), channel_id=1, source_target_pairs={{0,2},{2,0},{4,6},{6,4},{1,3},{3,1},{5,7},{7,5},{8,10},{10,8},{12,... | collective-permute-start | bytes 6291464 | tf_op jit(solution)/shard_map/ppermute | solution.py:23
  658.9 139.7 %collective-permute-start.90 = (bf16[1,176,2048]{2,1,0:T(8,128)(2,1)}, bf16[1,176,2048]{2,1,0:T(8,128)(2,1)}, u32[]{:S(2)}, u32[]{:S(2)}) collective-permute-start(bf16[1,176,2048]{2,1,0:T(8,128)(2,1)} %fusion.19), channel_id=1, source_target_pairs={{0,4},{2,6},{4,0},{6,2},{1,5},{3,7},{5,1},{7,3},{8,12},{10,14},{12... | collective-permute-start | bytes 2162696 | tf_op jit(solution)/shard_map/ppermute | solution.py:23
  707.4 39.8 %collective-permute-start.65 = (bf16[4,64,2048]{2,1,0:T(8,128)(2,1)}, bf16[4,64,2048]{2,1,0:T(8,128)(2,1)}, u32[]{:S(2)}, u32[]{:S(2)}) collective-permute-start(bf16[4,64,2048]{2,1,0:T(8,128)(2,1)} %dynamic-slice_bitcast_fusion.1), channel_id=1, source_target_pairs={{0,1},{1,0},{2,3},{3,2},{4,5},{5,4},{6,7},{7,6},{8,9},{9,8},{10,11... | collective-permute-start | bytes 3145736 | tf_op jit(solution)/shard_map/ppermute | solution.py:23
  710.6 46.8 %collective-permute-start.75 = (bf16[256,2816]{1,0:T(8,128)(2,1)}, bf16[256,2816]{1,0:T(8,128)(2,1)}, u32[]{:S(2)}, u32[]{:S(2)}) collective-permute-start(bf16[256,2816]{1,0:T(8,128)(2,1)} %get-tuple-element.92), channel_id=1, source_target_pairs={{0,8},{1,9},{2,10},{3,11},{4,12},{5,13},{6,14},{7,15}} | collective-permute-start | bytes 4325384 | tf_op jit(solution)/shard_map/ppermute | solution.py:1026
  714.7 46.8 %collective-permute-start.78 = (bf16[256,2816]{1,0:T(8,128)(2,1)}, bf16[256,2816]{1,0:T(8,128)(2,1)}, u32[]{:S(2)}, u32[]{:S(2)}) collective-permute-start(bf16[256,2816]{1,0:T(8,128)(2,1)} %get-tuple-element.93), channel_id=1, source_target_pairs={{24,16},{25,17},{26,18},{27,19},{28,20},{29,21},{30,22},{31,23}} | collective-permute-start | bytes 4325384 | tf_op jit(solution)/shard_map/ppermute | solution.py:1027
  756.2 69.3 %collective-permute-start.56 = (bf16[1024,1536]{1,0:T(8,128)(2,1)}, bf16[1024,1536]{1,0:T(8,128)(2,1)}, u32[]{:S(2)}, u32[]{:S(2)}) collective-permute-start(bf16[1024,1536]{1,0:T(8,128)(2,1)} %convolution_convert_fusion.2), channel_id=1, source_target_pairs={{0,1},{1,0},{2,3},{3,2},{4,5},{5,4},{6,7},{7,6},{8,9},{9,8},{10,11... | collective-permute-start | bytes 9437192 | tf_op jit(solution)/shard_map/ppermute | solution.py:23
  765.4 38.2 %collective-permute-start.76 = (bf16[256,2816]{1,0:T(8,128)(2,1)}, bf16[256,2816]{1,0:T(8,128)(2,1)}, u32[]{:S(2)}, u32[]{:S(2)}) collective-permute-start(bf16[256,2816]{1,0:T(8,128)(2,1)} %get-tuple-element.90), channel_id=1, source_target_pairs={{0,8},{8,16},{1,9},{9,17},{2,10},{10,18},{3,11},{11,19},{4,12},{12... | collective-permute-start | bytes 4325384 | tf_op jit(solution)/shard_map/ppermute | solution.py:1026
  807.1 62.2 %collective-permute-start.80 = (bf16[256,2816]{1,0:T(8,128)(2,1)S(1)}, bf16[256,2816]{1,0:T(8,128)(2,1)S(1)}, u32[]{:S(2)}, u32[]{:S(2)}) collective-permute-start(bf16[256,2816]{1,0:T(8,128)(2,1)S(1)} %get-tuple-element.89), channel_id=1, source_target_pairs={{8,0},{16,8},{24,16},{9,1},{17,9},{25,17},{10,2},{18,10},{26,18},{... | collective-permute-start | bytes 4325384 | tf_op jit(solution)/shard_map/ppermute | solution.py:1027
  808.5 66.7 %collective-permute-start.77 = (bf16[256,2816]{1,0:T(8,128)(2,1)S(1)}, bf16[256,2816]{1,0:T(8,128)(2,1)S(1)}, u32[]{:S(2)}, u32[]{:S(2)}) collective-permute-start(bf16[256,2816]{1,0:T(8,128)(2,1)S(1)} %get-tuple-element.88), channel_id=1, source_target_pairs={{0,8},{8,16},{16,24},{1,9},{9,17},{17,25},{2,10},{10,18},{18,26},{... | collective-permute-start | bytes 4325384 | tf_op jit(solution)/shard_map/ppermute | solution.py:1026
  833.9 46.0 %collective-permute-start.68 = (bf16[64,2048]{1,0:T(8,128)(2,1)S(1)}, bf16[64,2048]{1,0:T(8,128)(2,1)S(1)}, u32[]{:S(2)}, u32[]{:S(2)}) collective-permute-start(bf16[64,2048]{1,0:T(8,128)(2,1)S(1)} %get-tuple-element.104), channel_id=1, source_target_pairs={{0,8},{8,16},{16,24},{1,9},{9,17},{17,25},{2,10},{10,18},{18,26},{... | collective-permute-start | bytes 786440 | tf_op jit(solution)/shard_map/ppermute | solution.py:1026
  879.9 96.2 %collective-permute-start.91 = (bf16[2,176,2048]{2,1,0:T(8,128)(2,1)}, bf16[2,176,2048]{2,1,0:T(8,128)(2,1)}, u32[]{:S(2)}, u32[]{:S(2)}) collective-permute-start(bf16[2,176,2048]{2,1,0:T(8,128)(2,1)} %pad_maximum_fusion.10.near_ref), channel_id=1, source_target_pairs={{0,2},{2,0},{4,6},{6,4},{1,3},{3,1},{5,7},{7,5},{8,10},{10,8},{12,... | collective-permute-start | bytes 4325384 | tf_op jit(solution)/shard_map/ppermute | solution.py:23
  879.9 43.5 %collective-permute-start.81 = (bf16[1,256,2816]{2,1,0:T(8,128)(2,1)}, bf16[1,256,2816]{2,1,0:T(8,128)(2,1)}, u32[]{:S(2)}, u32[]{:S(2)}) collective-permute-start(bf16[1,256,2816]{2,1,0:T(8,128)(2,1)} %fusion.10), channel_id=1, source_target_pairs={{0,4},{2,6},{4,0},{6,2},{1,5},{3,7},{5,1},{7,3},{8,12},{10,14},{12... | collective-permute-start | bytes 4325384 | tf_op jit(solution)/shard_map/ppermute | solution.py:23
  892.4 93.5 %collective-permute-start.47 = (bf16[256,2048]{1,0:T(8,128)(2,1)}, bf16[256,2048]{1,0:T(8,128)(2,1)}, u32[]{:S(2)}, u32[]{:S(2)}) collective-permute-start(bf16[256,2048]{1,0:T(8,128)(2,1)} %add_convert_fusion.7), channel_id=1, source_target_pairs={{0,4},{2,6},{4,0},{6,2},{1,5},{3,7},{5,1},{7,3},{8,12},{10,14},{12... | collective-permute-start | bytes 3145736 | tf_op jit(solution)/shard_map/ppermute | solution.py:23
  927.1 77.7 %collective-permute-start.82 = (bf16[2,256,2816]{2,1,0:T(8,128)(2,1)}, bf16[2,256,2816]{2,1,0:T(8,128)(2,1)}, u32[]{:S(2)}, u32[]{:S(2)}) collective-permute-start(bf16[2,256,2816]{2,1,0:T(8,128)(2,1)} %pad_maximum_fusion.2.near_ref), channel_id=1, source_target_pairs={{0,2},{2,0},{4,6},{6,4},{1,3},{3,1},{5,7},{7,5},{8,10},{10,8},{12,... | collective-permute-start | bytes 8650760 | tf_op jit(solution)/shard_map/ppermute | solution.py:23
  (124 other events, 2629.7 us)

commit v3 on v1

--- a/solution.py
+++ b/solution.py
@@ -1,6 +1,11 @@
+import math
+
 import jax
 import jax.numpy as jnp
+import numpy as np
 from jax import lax
+from jax.experimental import pallas as pl
+from jax.experimental.pallas import tpu as pltpu
 from jax.sharding import PartitionSpec as P
 
 D = 2048
@@ -353,13 +358,1156 @@
     )
 
 
+def call(kernel, grid, in_specs, out_specs, out_shape, scratch=(), limit=48, after=(), aliases=()):
+    inputs = len(in_specs)
+
+    def body_of(places_ref, *refs):
+        kernel(places_ref, *refs[:inputs], *refs[inputs + len(after) :])
+
+    run = pl.pallas_call(
+        body_of,
+        grid_spec=pltpu.PrefetchScalarGridSpec(
+            num_scalar_prefetch=1,
+            grid=grid,
+            in_specs=in_specs + [anywhere()] * len(after),
+            out_specs=out_specs,
+            scratch_shapes=list(scratch),
+        ),
+        out_shape=out_shape,
+        input_output_aliases=dict(aliases),
+        compiler_params=pltpu.CompilerParams(vmem_limit_bytes=limit * 1024 * 1024),
+        cost_estimate=pl.CostEstimate(flops=1, bytes_accessed=1, transcendentals=0),
+    )
+    return lambda *operands: run(*operands, *after)
+
+
+def anywhere():
+    return pl.BlockSpec(memory_space=pl.ANY)
+
+
+def hold(places, value, *after):
+    def kernel(places_ref, value_ref, o_ref):
+        pass
+
+    return call(
+        kernel,
+        (1,),
+        [anywhere()],
+        anywhere(),
+        sds(value.shape, value.dtype),
+        limit=1,
+        after=after,
+        aliases=((1, 0),),
+    )(places, value)
+
+
+def sds(shape, dtype):
+    return jax.ShapeDtypeStruct(shape, dtype)
+
+
+def whole(array):
+    zeros = (0,) * array.ndim
+    return pl.BlockSpec(array.shape, lambda *_: zeros)
+
+
+def quarters(shape):
+    if shape[0] % 64 == 0:
+        return (shape[0] // 4, shape[1]), lambda m: (m, 0)
+    return (shape[0], shape[1] // 4), lambda m: (0, m)
+
+
+def add(places, terms, after=()):
+    shape = terms[0][0].shape[len(terms[0][1]) :]
+    steps = 4 if shape[0] % 64 == 0 else 1
+    tile = shape[0] // steps
+
+    def spec(at):
+        return pl.BlockSpec((None,) * len(at) + (tile, shape[1]), lambda m, _: at + (m, 0))
+
+    def kernel(places_ref, *refs):
+        total = refs[0][...].astype(jnp.float32)
+        for ref in refs[1:-1]:
+            total = total + ref[...].astype(jnp.float32)
+        refs[-1][...] = total.astype(jnp.bfloat16)
+
+    return call(
+        kernel,
+        (steps,),
+        [spec(at) for _, at in terms],
+        spec(()),
+        sds(shape, jnp.bfloat16),
+        after=after,
+    )(places, *[array for array, _ in terms])
+
+
+def contract(left, right):
+    return lax.dot_general(
+        left, right, (((0,), (0,)), ((), ())), preferred_element_type=jnp.float32
+    )
+
+
+def take_columns(places, w, count, shards, groups, group, copies, pad, after=()):
+    depth = w.shape[0]
+    each = w.shape[1] // groups
+    unit = each // (shards * count)
+    tile = depth // 4
+
+    def kernel(places_ref, w_ref, o_ref):
+        for i in range(count):
+
+            @pl.when(places_ref[0] == i)
+            def _():
+                block = jnp.concatenate(
+                    [
+                        w_ref[:, (s * count + i) * unit : (s * count + i + 1) * unit]
+                        for s in range(shards)
+                    ],
+                    axis=1,
+                )
+                for copy in range(copies):
+                    o_ref[copy] = block
+
+    return call(
+        kernel,
+        (4,),
+        [pl.BlockSpec((tile, each), lambda m, _: (m, group))],
+        pl.BlockSpec((copies, tile, each // count), lambda m, _: (0, m, 0)),
+        sds((copies, depth + pad, each // count), jnp.bfloat16),
+        after=after,
+    )(places, w)
+
+
+def take_pairs(places, w, count, shards, after=()):
+    depth = w.shape[0]
+    each = w.shape[1] // 2
+    unit = each // (shards * count)
+    tile = depth // 4
+
+    def kernel(places_ref, gate_ref, up_ref, o_ref):
+        for i in range(count):
+
+            @pl.when(places_ref[0] == i)
+            def _():
+                for part, ref in enumerate((gate_ref, up_ref)):
+                    block = jnp.concatenate(
+                        [
+                            ref[:, (s * count + i) * unit : (s * count + i + 1) * unit]
+                            for s in range(shards)
+                        ],
+                        axis=1,
+                    )
+                    for n in range(each // count // 128):
+                        at = (2 * n + part) * 128
+                        o_ref[:, at : at + 128] = block[:, n * 128 : (n + 1) * 128]
+
+    return call(
+        kernel,
+        (4,),
+        [
+            pl.BlockSpec((tile, each), lambda m, _: (m, 0)),
+            pl.BlockSpec((tile, each), lambda m, _: (m, 1)),
+        ],
+        pl.BlockSpec((tile, 2 * each // count), lambda m, _: (m, 0)),
+        sds((depth, 2 * each // count), jnp.bfloat16),
+        after=after,
+    )(places, w, w)
+
+
+def interleave(blocks, shards):
+    unit = blocks[0].shape[1] // shards
+    return [
+        jnp.concatenate([block[:, s * unit : (s + 1) * unit] for block in blocks], axis=1)
+        for s in range(shards)
+    ]
+
+
+def spread_pairs(places, gathered, count, shards, after=()):
+    depth = gathered.shape[0] // count
+    width = gathered.shape[1]
+    each = width // 2
+    unit = each // shards * count
+    tile = depth // 8
+
+    def kernel(places_ref, x_ref, o_ref):
+        for part in range(2):
+            blocks = []
+            for i in range(count):
+                tiles = [
+                    x_ref[i][:, (2 * n + part) * 128 : (2 * n + part + 1) * 128]
+                    for n in range(each // 128)
+                ]
+                blocks.append(jnp.concatenate(tiles, axis=1).astype(jnp.float32))
+            for s, block in enumerate(interleave(blocks, shards)):
+                at = part * each * count + s * unit
+                o_ref[:, at : at + unit] = block
+
+    return call(
+        kernel,
+        (8,),
+        [pl.BlockSpec((count, tile, width), lambda m, _: (0, m, 0))],
+        pl.BlockSpec((tile, width * count), lambda m, _: (m, 0)),
+        sds((depth, width * count), jnp.float32),
+        after=after,
+    )(places, gathered.reshape(count, depth, width))
+
+
+def spread_columns(places, pieces, count, shards, after=()):
+    groups = len(pieces)
+    depth, each = pieces[0][0].shape
+    unit = each // shards * count
+    tile = depth // 4
+    flat = [piece for group in pieces for piece in group]
+
+    def kernel(places_ref, *refs):
+        o_ref = refs[-1]
+        for g in range(groups):
+            values = [refs[g * count + p][...].astype(jnp.float32) for p in range(count)]
+            blocks = []
+            for i in range(count):
+                block = values[0]
+                for p in range(1, count):
+                    block = jnp.where(places_ref[1 + i] == p, values[p], block)
+                blocks.append(block)
+            for s, block in enumerate(interleave(blocks, shards)):
+                at = g * each * count + s * unit
+                o_ref[:, at : at + unit] = block
+
+    spec = pl.BlockSpec((tile, each), lambda m, _: (m, 0))
+    return call(
+        kernel,
+        (4,),
+        [spec] * len(flat),
+        pl.BlockSpec((tile, groups * each * count), lambda m, _: (m, 0)),
+        sds((depth, groups * each * count), jnp.float32),
+        after=after,
+    )(places, *flat)
+
+
+def norm_stats(values):
+    average = jnp.mean(values, axis=-1, keepdims=True)
+    centred = values - average
+    inverse = lax.rsqrt(jnp.mean(centred * centred, axis=-1, keepdims=True) + epsilon)
+    return centred * inverse, inverse
+
+
+def norm_tokens(places, tokens, gain, bias, count, after=()):
+    length = tokens.shape[0]
+    tile = length // count // 2
+    shards, depth = gain.shape
+
+    def kernel(places_ref, x_ref, gain_ref, bias_ref, o_ref, plain_ref):
+        plain_ref[...], _ = norm_stats(x_ref[...].astype(jnp.float32))
+        for r in range(shards):
+            start = pl.multiple_of(places_ref[1 + count + r] * depth, depth)
+            block = plain_ref[:, pl.ds(start, depth)]
+            o_ref[:, r * depth : (r + 1) * depth] = (
+                block * gain_ref[r : r + 1] + bias_ref[r : r + 1]
+            ).astype(jnp.bfloat16)
+
+    return call(
+        kernel,
+        (count, 2),
+        [
+            pl.BlockSpec((tile, D), lambda b, h, p: (p[1 + b] * 2 + h, 0)),
+            whole(gain),
+            whole(bias),
+        ],
+        pl.BlockSpec((tile, D), lambda b, h, _: (b * 2 + h, 0)),
+        sds((length, D), jnp.bfloat16),
+        [pltpu.VMEM((tile, D), jnp.float32)],
+        after=after,
+    )(places, tokens, gain, bias)
+
+
+def norm_hidden(places, tokens, pieces, gain, bias, after=()):
+    rows = tokens.shape[0]
+    tile = rows // 4
+
+    def kernel(places_ref, x_ref, *refs):
+        gain_ref, bias_ref, hidden_ref, o_ref = refs[-4:]
+        hidden = x_ref[...].astype(jnp.float32)
+        for ref in refs[:-4]:
+            hidden = hidden + ref[...].astype(jnp.float32)
+        hidden_ref[...] = hidden
+        normal, _ = norm_stats(hidden)
+        o_ref[...] = (normal * gain_ref[...] + bias_ref[...]).astype(jnp.bfloat16)
+
+    spec = pl.BlockSpec((tile, D), lambda m, _: (m, 0))
+    return call(
+        kernel,
+        (4,),
+        [spec] * (1 + len(pieces)) + [whole(gain), whole(bias)],
+        [spec, spec],
+        [sds((rows, D), jnp.float32), sds((rows, D), jnp.bfloat16)],
+        after=after,
+    )(places, tokens, *pieces, gain, bias)
+
+
+def norm_back(places, source, pieces, gain, added, first, low, after=()):
+    rows = source.shape[0]
+    tile = rows // 4
+    shards, depth = gain.shape
+
+    def kernel(places_ref, x_ref, added_ref, gain_ref, *refs):
+        piece_refs = refs[: len(pieces)]
+        out_refs = refs[len(pieces) : -2]
+        sums_ref = out_refs[-1]
+        grad_ref, gain_plain = refs[-2:]
+        for r in range(shards):
+            start = pl.multiple_of(places_ref[first + r] * depth, depth) if shards > 1 else 0
+            at = slice(r * depth, (r + 1) * depth)
+            block = piece_refs[0][:, at].astype(jnp.float32)
+            for ref in piece_refs[1:]:
+                block = block + ref[:, at].astype(jnp.float32)
+            grad_ref[:, pl.ds(start, depth)] = block
+            gain_plain[:, pl.ds(start, depth)] = jnp.broadcast_to(gain_ref[r : r + 1], (8, depth))
+        normal, inverse = norm_stats(x_ref[...].astype(jnp.float32))
+        grad = grad_ref[...]
+
+        @pl.when(pl.program_id(0) == 0)
+        def _():
+            sums_ref[...] = jnp.zeros_like(sums_ref)
+
+        sums_ref[0:1] += jnp.sum(grad * normal, axis=0, keepdims=True)
+        sums_ref[1:2] += jnp.sum(grad, axis=0, keepdims=True)
+        scaled = grad * gain_plain[0:1]
+        mean = jnp.mean(scaled, axis=-1, keepdims=True)
+        second = jnp.mean(scaled * normal, axis=-1, keepdims=True)
+        total = added_ref[...].astype(jnp.float32) + inverse * (scaled - mean - normal * second)
+        out_refs[0][...] = total
+        if low:
+            out_refs[1][...] = total.astype(jnp.bfloat16)
+
+    spec = pl.BlockSpec((tile, D), lambda m, _: (m, 0))
+    sums = pl.BlockSpec((2, D), lambda m, _: (0, 0))
+    return call(
+        kernel,
+        (4,),
+        [spec, spec, whole(gain)] + [spec] * len(pieces),
+        [spec] + [spec] * low + [sums],
+        [sds((rows, D), jnp.float32)]
+        + [sds((rows, D), jnp.bfloat16)] * low
+        + [sds((2, D), jnp.float32)],
+        [pltpu.VMEM((tile, D), jnp.float32), pltpu.VMEM((8, D), jnp.float32)],
+        after=after,
+    )(places, source, added, gain, *pieces)
+
+
+def project(places, normed, near, far, bias, tables, after=()):
+    length = normed.shape[0]
+    width = bias.shape[1]
+    tile = min(width, 256)
+    blocks = near.shape[0]
+    depth = D // blocks // 2
+
+    def kernel(places_ref, x_ref, near_ref, far_ref, bias_ref, *refs):
+        o_ref = refs[-1]
+        total = bias_ref[...]
+        for i, ref in enumerate((near_ref, far_ref)):
+            weight = ref[...].reshape(D // 2, tile)
+            left = x_ref[:, i * (D // 2) : (i + 1) * (D // 2)]
+            total = total + jnp.dot(left, weight, preferred_element_type=jnp.float32)
+        if tables:
+            cosine, low, high = (
+                jnp.concatenate([ref[...]] * (tile // 128), axis=1) for ref in refs[:3]
+            )
+            total = (
+                total * cosine
+                + pltpu.roll(total, tile - ROT // 2, 1) * low
+                + pltpu.roll(total, ROT // 2, 1) * high
+            )
+        o_ref[...] = total.astype(jnp.bfloat16)
+
+    weight = pl.BlockSpec((blocks, depth, tile), lambda n, _: (0, 0, n))
+    return call(
+        kernel,
+        (width // tile,),
+        [whole(normed), weight, weight, pl.BlockSpec((1, tile), lambda n, _: (0, n))]
+        + [whole(table) for table in tables],
+        pl.BlockSpec((length, tile), lambda n, _: (0, n)),
+        sds((length, width), jnp.bfloat16),
+        after=after,
+    )(places, normed, near, far, bias, *tables)
+
+
+def head_lanes(values, head):
+    lanes = lax.broadcasted_iota(jnp.int32, values.shape, 1)
+    return jnp.where((lanes >= head * E) & (lanes < (head + 1) * E), values, jnp.zeros_like(values))
+
+
+def to_plain_rows(places_ref, source_ref, target_ref, count):
+    rows = target_ref.shape[0] // count
+    for b in range(count):
+        start = pl.multiple_of(places_ref[1 + b] * rows, rows)
+        target_ref[b * rows : (b + 1) * rows] = source_ref[pl.ds(start, rows)]
+
+
+def masked(scores, keys_seg, query_seg, first):
+    ks = lax.broadcasted_iota(jnp.int32, scores.shape, 0)
+    qs = lax.broadcasted_iota(jnp.int32, scores.shape, 1) + first
+    return (ks <= qs) & (keys_seg == query_seg)
+
+
+def attend(places, qkv, seg_col, seg_row, count, heads, after=()):
+    length = qkv[0].shape[0]
+    pairs = heads // 2
+    step = math.gcd(length, 256)
+    rows = length // count
+
+    def kernel(places_ref, q_ref, k_ref, v_ref, col_ref, row_ref, o_ref, log_ref, vt, os):
+        vt[...] = jnp.transpose(v_ref[...].astype(jnp.float32)).astype(jnp.bfloat16)
+        for a in range(length // step):
+            n = (a + 1) * step
+            halves = []
+            for h in range(2):
+                query = head_lanes(q_ref[a * step : n], h)
+                scores = lax.dot_general(
+                    k_ref[0:n], query, (((1,), (1,)), ((), ())), preferred_element_type=jnp.float32
+                )
+                allowed = masked(scores, col_ref[0:n], row_ref[:, a * step : n], a * step)
+                scores = jnp.where(allowed, scores * scale, masked_score)
+                top = jnp.max(scores, axis=0, keepdims=True)
+                weights = jnp.exp(scores - top)
+                total = jnp.sum(weights, axis=0, keepdims=True)
+                out = jnp.dot(
+                    vt[h * E : (h + 1) * E, 0:n],
+                    weights.astype(jnp.bfloat16),
+                    preferred_element_type=jnp.float32,
+                )
+                halves.append(out / total)
+                log_ref[0, h : h + 1, a * step : n] = top + jnp.log(total)
+            os[a * step : n] = jnp.transpose(jnp.concatenate(halves, axis=0)).astype(jnp.bfloat16)
+        for b in range(count):
+            start = pl.multiple_of(places_ref[1 + b] * rows, rows)
+            o_ref[pl.ds(start, rows)] = os[b * rows : (b + 1) * rows]
+
+    def columns(group):
+        return pl.BlockSpec((length, 128), lambda p, _: (0, group * pairs + p))
+
+    scratch = pltpu.VMEM((length, 128), jnp.bfloat16)
+    return call(
+        kernel,
+        (pairs,),
+        [columns(0), columns(0), columns(0), whole(seg_col), whole(seg_row)],
+        [columns(0), pl.BlockSpec((1, 2, length), lambda p, _: (p, 0, 0))],
+        [
+            sds((length, heads * E), jnp.bfloat16),
+            sds((pairs, 2, length), jnp.float32),
+        ],
+        [pltpu.VMEM((128, length), jnp.bfloat16), scratch],
+        after=after,
+    )(places, *qkv, seg_col, seg_row)
+
+
+def attend_back(
+    places, qkv, grad_attended, logs, seg_col, seg_row, tables, count, heads, after=()
+):
+    length = qkv[0].shape[0]
+    pairs = heads // 2
+    step = math.gcd(length, 256)
+    rows = length // count
+
+    def kernel(
+        places_ref,
+        q_ref,
+        k_ref,
+        v_ref,
+        g_ref,
+        log_ref,
+        col_ref,
+        row_ref,
+        cos_ref,
+        low_ref,
+        high_ref,
+        dq_ref,
+        dk_ref,
+        dv_ref,
+        sums_ref,
+        gs,
+        kt,
+        dq,
+        dk,
+        dv,
+    ):
+        to_plain_rows(places_ref, g_ref, gs, count)
+        kt[...] = jnp.transpose(k_ref[...].astype(jnp.float32)).astype(jnp.bfloat16)
+        dk[...] = jnp.zeros_like(dk)
+        dv[...] = jnp.zeros_like(dv)
+        for a in range(length // step):
+            n = (a + 1) * step
+            halves = []
+            for h in range(2):
+                query = head_lanes(q_ref[a * step : n], h)
+                grad = head_lanes(gs[a * step : n], h)
+                scores = lax.dot_general(
+                    k_ref[0:n], query, (((1,), (1,)), ((), ())), preferred_element_type=jnp.float32
+                )
+                allowed = masked(scores, col_ref[0:n], row_ref[:, a * step : n], a * step)
+                log = log_ref[0, h : h + 1, a * step : n]
+                weights = jnp.exp(jnp.where(allowed, scores * scale - log, masked_score))
+                grad_weights = lax.dot_general(
+                    v_ref[0:n], grad, (((1,), (1,)), ((), ())), preferred_element_type=jnp.float32
+                )
+                product = weights * grad_weights
+                delta = jnp.sum(product, axis=0, keepdims=True)
+                grad_scores = (product - weights * delta).astype(jnp.bfloat16)
+                dv[0:n] += jnp.dot(
+                    weights.astype(jnp.bfloat16), grad, preferred_element_type=jnp.float32
+                )
+                dk[0:n] += jnp.dot(grad_scores, query, preferred_element_type=jnp.float32)
+                halves.append(
+                    jnp.dot(
+                        kt[h * E : (h + 1) * E, 0:n],
+                        grad_scores,
+                        preferred_element_type=jnp.float32,
+                    )
+                )
+            dq[a * step : n] = jnp.transpose(jnp.concatenate(halves, axis=0))
+
+        sums = [jnp.zeros((1, 128), jnp.float32)] * 3
+        for b in range(count):
+            at = slice(b * rows, (b + 1) * rows)
+            cosine, low, high = cos_ref[at], low_ref[at], high_ref[at]
+            for i, (part, out_ref) in enumerate(((dq, dq_ref), (dk, dk_ref), (dv, dv_ref))):
+                block = part[at]
+                if i < 2:
+                    block = block * scale
+                    block = (
+                        block * cosine
+                        - pltpu.roll(block, 128 - ROT // 2, 1) * low
+                        - pltpu.roll(block, ROT // 2, 1) * high
+                    )
+                block = block.astype(jnp.bfloat16)
+                sums[i] = sums[i] + jnp.sum(block.astype(jnp.float32), axis=0, keepdims=True)
+                out_ref[at] = block
+        for i in range(3):
+            sums_ref[i] = sums[i]
+
+    def columns(group):
+        return pl.BlockSpec((length, 128), lambda p, _: (0, group * pairs + p))
+
+    low_scratch = pltpu.VMEM((length, 128), jnp.bfloat16)
+    scratch = pltpu.VMEM((length, 128), jnp.float32)
+    width = heads * E
+    return call(
+        kernel,
+        (pairs,),
+        [
+            columns(0),
+            columns(0),
+            columns(0),
+            columns(0),
+            pl.BlockSpec((1, 2, length), lambda p, _: (p, 0, 0)),
+            whole(seg_col),
+            whole(seg_row),
+            whole(tables[0]),
+            whole(tables[1]),
+            whole(tables[2]),
+        ],
+        [columns(0)] * 3 + [pl.BlockSpec((3, 1, 128), lambda p, _: (0, 0, p))],
+        [sds((length, width), jnp.bfloat16)] * 3 + [sds((3, 1, width), jnp.float32)],
+        [low_scratch]
+        + [pltpu.VMEM((128, length), jnp.bfloat16), scratch, scratch, scratch],
+        after=after,
+    )(places, *qkv, grad_attended, logs, seg_col, seg_row, *tables)
+
+
+def join_rows(places_ref, first, refs, joined):
+    r = 0
+    for ref in refs:
+        blocks, size, _ = ref.shape
+        for i in range(blocks):
+            start = pl.multiple_of(places_ref[first + r] * size, size)
+            joined[pl.ds(start, size)] = ref[i]
+            r += 1
+
+
+def row_product(places, left, near, far, count, after=()):
+    length, depth = left.shape
+    tile = D // 4
+
+    def kernel(places_ref, x_ref, a_ref, b_ref, near_ref, far_ref, joined):
+        @pl.when(pl.program_id(0) == 0)
+        def _():
+            join_rows(places_ref, 1 + count, (a_ref, b_ref), joined)
+
+        start = pl.multiple_of(pl.program_id(0) * tile, tile)
+        total = jnp.dot(
+            x_ref[...], joined[:, pl.ds(start, tile)], preferred_element_type=jnp.float32
+        ).astype(jnp.bfloat16)
+        near_ref[...] = total[: length // 2]
+        far_ref[...] = total[length // 2 :]
+
+    spec = pl.BlockSpec((length // 2, tile), lambda n, _: (0, n))
+    shape = sds((length // 2, D), jnp.bfloat16)
+    return call(
+        kernel,
+        (4,),
+        [whole(left), whole(near), whole(far)],
+        [spec, spec],
+        [shape, shape],
+        [pltpu.VMEM((depth, D), jnp.bfloat16)],
+        after=after,
+    )(places, left, near, far)
+
+
+def grad_out(places, pieces, near, far, count, after=()):
+    rows = pieces[0].shape[0]
+    width = near.shape[0] * near.shape[1] * 2
+    tile = rows
+
+    def kernel(places_ref, *refs):
+        piece_refs = refs[:count]
+        a_ref, b_ref, o_ref, all_ref, joined = refs[count:]
+
+        @pl.when(pl.program_id(0) == 0)
+        def _():
+            join_rows(places_ref, 1 + count, (a_ref, b_ref), joined)
+
+        for p, ref in enumerate(piece_refs):
+
+            @pl.when(pl.program_id(0) == p)
+            def _():
+                all_ref[...] = ref[...]
+                o_ref[...] = lax.dot_general(
+                    ref[...],
+                    joined[...],
+                    (((1,), (1,)), ((), ())),
+                    preferred_element_type=jnp.float32,
+                ).astype(jnp.bfloat16)
+
+    return call(
+        kernel,
+        (count,),
+        [whole(piece) for piece in pieces] + [whole(near), whole(far)],
+        [
+            pl.BlockSpec((tile, width), lambda m, _: (m, 0)),
+            pl.BlockSpec((tile, D), lambda m, _: (m, 0)),
+        ],
+        [sds((rows * count, width), jnp.bfloat16), sds((rows * count, D), jnp.bfloat16)],
+        [pltpu.VMEM((width, D), jnp.bfloat16)],
+        after=after,
+    )(places, *pieces, near, far)
+
+
+def gate_product(places, pieces, weight, after=()):
+    rows = pieces[0].shape[0]
+    length = rows * len(pieces)
+    width = weight.shape[1]
+
+    def kernel(places_ref, *refs):
+        *piece_refs, w_ref, all_ref, both_ref, activ_ref = refs
+
+        @pl.when(pl.program_id(0) == 0)
+        def _():
+            for p, ref in enumerate(piece_refs):
+                all_ref[p * rows : (p + 1) * rows] = ref[...]
+
+        both = jnp.dot(all_ref[...], w_ref[...], preferred_element_type=jnp.float32)
+        gate = both[:, :128]
+        both_ref[...] = both.astype(jnp.bfloat16)
+        activ_ref[...] = (gate * jax.nn.sigmoid(gate) * both[:, 128:]).astype(jnp.bfloat16)
+
+    return call(
+        kernel,
+        (width // 256,),
+        [whole(piece) for piece in pieces] + [pl.BlockSpec((D, 256), lambda n, _: (0, n))],
+        [
+            pl.BlockSpec((length, D), lambda n, _: (0, 0)),
+            pl.BlockSpec((length, 256), lambda n, _: (0, n)),
+            pl.BlockSpec((length, 128), lambda n, _: (0, n)),
+        ],
+        [
+            sds((length, D), jnp.bfloat16),
+            sds((length, width), jnp.bfloat16),
+            sds((length, width // 2), jnp.bfloat16),
+        ],
+        limit=56,
+        after=after,
+    )(places, *pieces, weight)
+
+
+def gate_back(places, cotangent, near, far, both, count, after=()):
+    length, width = both.shape
+    units = width // 2
+    steps = -(-units // 256)
+
+    def kernel(places_ref, x_ref, a_ref, b_ref, both_ref, o_ref, joined):
+        @pl.when(pl.program_id(0) == 0)
+        def _():
+            join_rows(places_ref, 1 + count, (a_ref, b_ref), joined)
+
+        start = pl.multiple_of(pl.program_id(0) * 256, 256)
+        grad = lax.dot_general(
+            x_ref[...],
+            joined[pl.ds(start, 256)],
+            (((1,), (1,)), ((), ())),
+            preferred_element_type=jnp.float32,
+        )
+        for i in range(2):
+            part = grad[:, i * 128 : (i + 1) * 128]
+            gate = both_ref[:, i * 256 : i * 256 + 128].astype(jnp.float32)
+            upward = both_ref[:, i * 256 + 128 : (i + 1) * 256].astype(jnp.float32)
+            sigma = jax.nn.sigmoid(gate)
+            grad_gate = part * upward * sigma * (1.0 + gate * (1.0 - sigma))
+            o_ref[:, i * 256 : i * 256 + 128] = grad_gate.astype(jnp.bfloat16)
+            o_ref[:, i * 256 + 128 : (i + 1) * 256] = (part * (gate * sigma)).astype(jnp.bfloat16)
+
+    spec = pl.BlockSpec((length, 512), lambda n, _: (0, n))
+    return call(
+        kernel,
+        (steps,),
+        [whole(cotangent), whole(near), whole(far), spec],
+        spec,
+        sds((length, width), jnp.bfloat16),
+        [pltpu.VMEM((steps * 256, D), jnp.bfloat16)],
+        limit=56,
+        after=after,
+    )(places, cotangent, near, far, both)
+
+
+def normed_grad(places, left, weight, after=()):
+    length, width = left.shape
+
+    def kernel(places_ref, x_ref, w_ref, near_ref, far_ref):
+        total = lax.dot_general(
+            x_ref[...], w_ref[...], (((1,), (1,)), ((), ())), preferred_element_type=jnp.float32
+        ).astype(jnp.bfloat16)
+        near_ref[...] = total[: length // 2]
+        far_ref[...] = total[length // 2 :]
+
+    spec = pl.BlockSpec((length // 2, 256), lambda n, _: (0, n))
+    shape = sds((length // 2, D), jnp.bfloat16)
+    return call(
+        kernel,
+        (D // 256,),
+        [whole(left), pl.BlockSpec((256, width), lambda n, _: (n, 0))],
+        [spec, spec],
+        [shape, shape],
+        limit=56,
+        after=after,
+    )(places, left, weight)
+
+
+def normed_grad_parts(places, lefts, parts, count, after=()):
+    length, width = lefts[0].shape
+    rows = length // count
+    blocks, depth = parts[0][0].shape[0], D // parts[0][0].shape[0] // 2
+    total_width = width * len(lefts)
+
+    def kernel(places_ref, *refs):
+        left_refs = refs[: len(lefts)]
+        near_refs = refs[len(lefts) : 2 * len(lefts)]
+        far_refs = refs[2 * len(lefts) : 3 * len(lefts)]
+        near_ref, far_ref, joined = refs[3 * len(lefts) :]
+
+        @pl.when(pl.program_id(0) == 0)
+        def _():
+            for b in range(count):
+                start = pl.multiple_of(places_ref[1 + b] * rows, rows)
+                for i, ref in enumerate(left_refs):
+                    joined[pl.ds(start, rows), i * width : (i + 1) * width] = ref[
+                        b * rows : (b + 1) * rows
+                    ]
+
+        def run(weight_refs):
+            weight = jnp.concatenate([ref[0] for ref in weight_refs], axis=1)
+            total = lax.dot_general(
+                joined[...], weight, (((1,), (1,)), ((), ())), preferred_element_type=jnp.float32
+            ).astype(jnp.bfloat16)
+            near_ref[...] = total[: length // 2]
+            far_ref[...] = total[length // 2 :]
+
+        @pl.when(pl.program_id(0) < blocks)
+        def _():
+            run(near_refs)
+
+        @pl.when(pl.program_id(0) >= blocks)
+        def _():
+            run(far_refs)
+
+    near_spec = pl.BlockSpec((1, depth, width), lambda n, _: (jnp.minimum(n, blocks - 1), 0, 0))
+    far_spec = pl.BlockSpec((1, depth, width), lambda n, _: (jnp.maximum(n - blocks, 0), 0, 0))
+    spec = pl.BlockSpec((length // 2, depth), lambda n, _: (0, n))
+    shape = sds((length // 2, D), jnp.bfloat16)
+    return call(
+        kernel,
+        (2 * blocks,),
+        [whole(left) for left in lefts] + [near_spec] * len(lefts) + [far_spec] * len(lefts),
+        [spec, spec],
+        [shape, shape],
+        [pltpu.VMEM((length, total_width), jnp.bfloat16)],
+        after=after,
+    )(places, *lefts, *[near for near, _ in parts], *[far for _, far in parts])
+
+
+def turn(source_ref, first, columns, target_ref):
+    step = math.gcd(columns, 256)
+    for at in range(0, columns, step):
+        block = source_ref[:, first + at : first + at + step].astype(jnp.float32)
+        target_ref[at : at + step] = jnp.transpose(block).astype(jnp.bfloat16)
+
+
+def pairs_grad(places, normed, right, after=()):
+    length, width = right.shape
+
+    def kernel(places_ref, x_ref, g_ref, o_ref, turned):
+        @pl.when(pl.program_id(0) == 0)
+        def _():
+            turn(x_ref, 0, D, turned)
+
+        o_ref[...] = jnp.dot(
+            turned[...], g_ref[...], preferred_element_type=jnp.float32
+        ).astype(jnp.bfloat16)
+
+    return call(
+        kernel,
+        (width // 256,),
+        [whole(normed), pl.BlockSpec((length, 256), lambda n, _: (0, n))],
+        pl.BlockSpec((D, 256), lambda n, _: (0, n)),
+        sds((D, width), jnp.bfloat16),
+        [pltpu.VMEM((D, length), jnp.bfloat16)],
+        after=after,
+    )(places, normed, right)
+
+
+def column_loads(places, normed, rights, after=()):
+    length, width = rights[0].shape
+    count = len(rights)
+    rows = D // 2
+
+    def kernel(places_ref, x_ref, *refs):
+        right_refs, out_refs = refs[:count], refs[count : 2 * count]
+        turned_ref, turned = refs[2 * count :]
+        step = pl.program_id(0)
+
+        @pl.when(step == 0)
+        def _():
+            turn(x_ref, rows, rows, turned)
+
+        for i in range(count):
+
+            @pl.when(step == i)
+            def _():
+                out_refs[i][...] = jnp.dot(
+                    turned[...], right_refs[i][...], preferred_element_type=jnp.float32
+                ).astype(jnp.bfloat16)
+
+        @pl.when(step == count - 1)
+        def _():
+            turn(x_ref, 0, rows, turned_ref)
+
+    shape = sds((rows, width), jnp.bfloat16)
+    own = sds((rows, length), jnp.bfloat16)
+    return call(
+        kernel,
+        (count,),
+        [whole(normed)] + [whole(right) for right in rights],
+        [whole(shape)] * count + [whole(own)],
+        [shape] * count + [own],
+        [pltpu.VMEM((rows, length), jnp.bfloat16)],
+        after=after,
+    )(places, normed, *rights)
+
+
+def column_keep(places, turned, right, arrived, after=()):
+    rows, length = turned.shape
+    width = right.shape[1]
+    tile = width // 2
+
+    def kernel(places_ref, x_ref, g_ref, arrived_ref, o_ref):
+        total = jnp.dot(x_ref[...], g_ref[...], preferred_element_type=jnp.float32)
+        o_ref[...] = (total + arrived_ref[...].astype(jnp.float32)).astype(jnp.bfloat16)
+
+    spec = pl.BlockSpec((rows, tile), lambda n, _: (0, n))
+    return call(
+        kernel,
+        (2,),
+        [whole(turned), pl.BlockSpec((length, tile), lambda n, _: (0, n)), spec],
+        spec,
+        sds((rows, width), jnp.bfloat16),
+        after=after,
+    )(places, turned, right, arrived)
+
+
+def row_grad(places, left, right, size, count, stacked, after=()):
+    length, width = left.shape
+    tile = D // 4
+    blocks = width // size // 2
+
+    def kernel(places_ref, x_ref, g_ref, *refs):
+        total_ref = refs[-1]
+        total_ref[...] = contract(x_ref[...], g_ref[...])
+        for side in range(2):
+            for r in range(blocks):
+                place = places_ref[1 + count + side * blocks + r]
+                start = pl.multiple_of(place * size, size)
+                refs[side][r] = total_ref[pl.ds(start, size)].astype(jnp.bfloat16)
+
+    block = (blocks, size, tile)
+    if stacked:
+        spec = pl.BlockSpec(block, lambda n, _: (0, n, 0))
+        shape = sds((blocks, 4 * size, tile), jnp.bfloat16)
+    else:
+        spec = pl.BlockSpec(block, lambda n, _: (0, 0, n))
+        shape = sds((blocks, size, D), jnp.bfloat16)
+    return call(
+        kernel,
+        (4,),
+        [whole(left), pl.BlockSpec((length, tile), lambda n, _: (0, n))],
+        [spec, spec],
+        [shape, shape],
+        [pltpu.VMEM((width, tile), jnp.float32)],
+        after=after,
+    )(places, left, right)
+
+
+def to_line(blocks):
+    return lax.all_to_all(blocks, "dp", split_axis=0, concat_axis=0)
+
+
+def rows_gather(own):
+    pieces = [own]
+    bit = lax.axis_size("ctx") // 2
+    while bit >= 1:
+        pieces = pieces + [swap(piece, "ctx", bit) for piece in pieces]
+        bit //= 2
+    return pieces
+
+
+def rows_scatter(places, near, far, after=()):
+    count = lax.axis_size("ctx")
+    pieces = [near, swap(far, "ctx", 1)]
+    bit = 2
+    while bit < count:
+        pieces = [piece.reshape(2, -1, D) for piece in pieces]
+        load = add(places, [(piece, (1,)) for piece in pieces], after if 2 * bit == count else ())
+        pieces = [piece[0] for piece in pieces] if 2 * bit < count else [
+            piece.reshape(-1, D) for piece in pieces
+        ]
+        pieces.append(swap(load, "ctx", bit))
+        bit *= 2
+    return pieces
+
+
+def fast_body(
+    tokens,
+    segment_ids,
+    cotangent,
+    ln1_gain,
+    ln1_bias,
+    w_qkv,
+    b_qkv,
+    w_out,
+    ln2_gain,
+    ln2_bias,
+    w_gate_up,
+    w_down,
+):
+    rows = tokens.shape[1]
+    count = lax.axis_size("ctx")
+    ctx = lax.axis_index("ctx")
+    line = lax.axis_size("dp")
+    here = lax.axis_index("dp")
+    side = lax.axis_index("fsdp")
+    shards = 2 * line
+    depth = D // shards
+    heads = H // count
+    width = heads * E
+    length = rows * count
+
+    def reversed_bits(value):
+        return sum(
+            jnp.where((value >> i) & 1, count >> (i + 1), 0) for i in range(count.bit_length() - 1)
+        )
+
+    row_places = [reversed_bits(b ^ ctx) for b in range(count)]
+    shard_of = [(r % line) * 2 + (side ^ (r // line)) for r in range(shards)]
+    places = jnp.stack([jnp.asarray(i, jnp.int32) for i in [ctx] + row_places + shard_of])
+
+    small = jnp.concatenate([ln1_gain, ln1_bias, ln2_gain, ln2_bias, b_qkv])
+    pad = 16
+    q_mine = take_columns(places, w_qkv, count, shards, 3, 0, line, pad)
+    lines = -(-small.shape[0] // width)
+    lead = jnp.pad(small, (0, pad * width - small.shape[0])).reshape(1, pad, width)
+    q_mine = lax.dynamic_update_slice(
+        q_mine, jnp.broadcast_to(lead, (line, pad, width)), (0, depth, 0)
+    )
+
+    def weight(blocks):
+        near = to_line(blocks)
+        return near, swap(near, "fsdp", 1)
+
+    def row_copies(w, *after):
+        block = hold(places, pick(w.reshape(count, -1, D), ctx, 0), *after)
+        return jnp.broadcast_to(block[None], (line,) + block.shape)
+
+    token_rows = jnp.concatenate(rows_gather(tokens[0]), axis=0)
+    cot_rows = jnp.concatenate(
+        rows_gather(hold(places, cotangent[0], token_rows)), axis=0
+    )
+    q_parts = weight(q_mine)
+    k_mine = take_columns(
+        places, w_qkv, count, shards, 3, 1, line, 0, q_parts[:1]
+    )
+    k_parts = weight(k_mine)
+    gate_mine = take_pairs(places, w_gate_up, count, shards, (k_parts[0], token_rows))
+    gate_up = lax.all_gather(gate_mine, ("dp", "fsdp"), axis=0, tiled=True)
+    v_mine = take_columns(
+        places, w_qkv, count, shards, 3, 2, line, 0, (k_parts[0], q_parts[1], token_rows)
+    )
+    v_parts = weight(v_mine)
+    qkv_parts = [q_parts, k_parts, v_parts]
+    out_parts = weight(row_copies(w_out, v_parts[0], k_parts[1], cot_rows))
+    seg_row = lax.all_gather(segment_ids, "ctx", axis=1, tiled=True)
+    seg_col = seg_row.reshape(length, 1)
+
+    half = ROT // 2
+    angles = np.arange(length)[:, None] * 10000.0 ** (-np.arange(half) * 2.0 / ROT)[None, :]
+    cosine, sine = np.cos(angles), np.sin(angles)
+    flat = np.zeros((length, E - ROT))
+    zero = np.zeros((length, half))
+    tables = [
+        jnp.asarray(np.concatenate(parts * 2, axis=1), jnp.float32)
+        for parts in ([cosine, cosine, flat + 1.0], [-sine, zero, flat], [zero, sine, flat])
+    ]
+
+    small_rows = [part[:, depth : depth + lines] for part in qkv_parts[0]]
+    small_all = jnp.concatenate(small_rows, axis=0).reshape(shards, -1)[:, : small.shape[0]]
+    small_all = small_all.astype(jnp.float32)
+    small_plain = sum(
+        (jnp.arange(shards)[:, None] == shard_of[r]) * small_all[r][None, :] for r in range(shards)
+    )
+    gain_one, bias_one = small_all[:, :depth], small_all[:, depth : 2 * depth]
+    gain_two = small_plain[:, 2 * depth : 3 * depth].reshape(1, D)
+    bias_two = small_plain[:, 3 * depth : 4 * depth].reshape(1, D)
+    bias_plain = small_plain[:, 4 * depth :]
+    bias_mine = pick(bias_plain.reshape(3, shards, count, E), ctx, 2).reshape(3, 1, width)
+
+    normed_one = norm_tokens(places, token_rows, gain_one, bias_one, count, (seg_row,))
+    qkv = []
+    for i, parts in enumerate(qkv_parts):
+        turns = tables if i < 2 else []
+        qkv.append(project(places, normed_one, *parts, bias_mine[i], turns, qkv[-1:]))
+    down_near = to_line(row_copies(w_down, out_parts[0], qkv[2]))
+    attended, logs = attend(places, qkv, seg_col, seg_row, count, heads)
+    pieces = rows_scatter(places, *row_product(places, attended, *out_parts, count))
+    hidden, normed_two = norm_hidden(places, tokens[0], pieces, gain_two, bias_two)
+    down_near = hold(places, down_near, hidden)
+    down_parts = (down_near, swap(down_near, "fsdp", 1))
+    normed_two, both, activ = gate_product(places, rows_gather(normed_two), gate_up)
+
+    def line_sum(blocks, after=()):
+        arrived = to_line(blocks).reshape(line, -1, blocks.shape[-1])
+        return add(places, [(arrived, (i,)) for i in range(line)], after)
+
+    def both_sides(kept, arrived):
+        return (kept.astype(jnp.float32) + arrived.astype(jnp.float32)).astype(jnp.bfloat16)
+
+    down_keep, down_load = row_grad(
+        places, activ, cot_rows, down_parts[0].shape[1], count, False
+    )
+    down_arrived = swap(down_load, "fsdp", 1)
+    grad_both = gate_back(places, cot_rows, *down_parts, both, count, (down_load,))
+    gate_part = pairs_grad(places, normed_two, grad_both)
+    gate_grad = lax.psum_scatter(gate_part, ("dp", "fsdp"), scatter_dimension=0, tiled=True)
+    pieces = rows_scatter(places, *normed_grad(places, grad_both, gate_up, (gate_part,)))
+    down_total = both_sides(down_keep, hold(places, down_arrived, pieces[1]))
+    down_pieces = row_product(places, activ, *down_parts, count, (down_total,))
+    grad_hidden, grad_branch, sums_two = norm_back(
+        places, hidden, pieces, gain_two, cotangent[0], 0, True, (down_pieces[0],)
+    )
+    down_pieces = rows_scatter(places, *down_pieces, (grad_branch,))
+    grad_attended, grad_branch = grad_out(places, rows_gather(grad_branch), *out_parts, count)
+    out_keep, out_load = row_grad(places, attended, grad_branch, out_parts[0].shape[1], count, True)
+    out_arrived = swap(out_load, "fsdp", 1)
+    grads = attend_back(
+        places, qkv, grad_attended, logs, seg_col, seg_row, tables, count, heads, (out_load,)
+    )
+    grads, bias_sums = grads[:3], grads[3]
+    *loads, turned = column_loads(places, normed_one, grads)
+    arrivals = [swap(load, "fsdp", 1) for load in loads]
+    mixed = hidden + sum(piece[:rows].astype(jnp.float32) for piece in down_pieces)
+    mixed = mixed.astype(jnp.bfloat16)
+    down_grad = line_sum(down_total, (loads[2],))
+
+    def ctx_rows(block):
+        return lax.all_gather(block, "ctx", axis=0, tiled=True)
+
+    def keep(i, *after):
+        total = column_keep(places, turned, grads[i], arrivals[i], after)
+        return total.reshape(line, depth, width)
+
+    out_total = both_sides(out_keep, out_arrived)
+    totals = [jnp.concatenate([keep(0, down_grad), out_total], axis=1)]
+    near, far = normed_grad_parts(places, grads, qkv_parts, count, (totals[0],))
+    gate_out = spread_pairs(places, ctx_rows(gate_grad), count, shards)
+    down_out = ctx_rows(down_grad).astype(jnp.float32)
+    totals.append(keep(1, gate_out))
+    pieces = rows_scatter(places, near, far, (totals[1],))
+    q_sum = line_sum(totals[0], (mixed,))
+    totals.append(keep(2, down_out))
+    input_grad, sums_one = norm_back(
+        places, tokens[0], pieces, gain_one, grad_hidden, 1 + count, False, (totals[2],)
+    )
+    out_out = ctx_rows(q_sum[depth:]).reshape(count, 4, -1, D // 4)
+    out_out = out_out.transpose(0, 2, 1, 3).reshape(-1, D).astype(jnp.float32)
+    sums = [q_sum[:depth], line_sum(totals[1]), line_sum(totals[2], (out_out,))]
+    qkv_grads = [rows_gather(total) for total in sums]
+    qkv_out = spread_columns(places, qkv_grads, count, shards)
+
+    bias_part = jnp.where(
+        jnp.arange(count)[None, None, :, None] == ctx, bias_sums.reshape(3, shards, 1, E), 0.0
+    ).reshape(shards, 3 * depth)
+    small_part = jnp.concatenate(
+        [part.reshape(shards, depth) for part in (*sums_one, *sums_two)] + [bias_part], axis=1
+    ).reshape(line, 2, -1)
+    load = pick(small_part, 1 - side, 1).astype(jnp.bfloat16)
+    total = pick(small_part, side, 1) + swap(load, "fsdp", 1).astype(jnp.float32)
+    low_total = total.astype(jnp.bfloat16)
+    mine = pick(total, here, 0)
+    for r in range(1, line):
+        mine = mine + swap(pick(low_total, here ^ r, 0), "dp", r).astype(jnp.float32)
+    bit = count // 2
+    while bit >= 1:
+        mine = mine + swap(mine, "ctx", bit)
+        bit //= 2
+
+    return (
+        mixed[None],
+        input_grad[None],
+        mine[:depth],
+        mine[depth : 2 * depth],
+        qkv_out,
+        mine[4 * depth :],
+        out_out,
+        mine[2 * depth : 3 * depth],
+        mine[3 * depth : 4 * depth],
+        gate_out,
+        down_out,
+    )
+
+
+def fits(mesh):
+    count, shards = mesh.shape["ctx"], mesh.shape["dp"] * mesh.shape["fsdp"]
+    return (
+        mesh.shape["fsdp"] == 2
+        and count > 1
+        and count & (count - 1) == 0
+        and (H // shards) == count
+        and (FF // shards) % (16 * count) == 0
+        and (FF // count) % 128 == 0
+        and (H // count) % 2 == 0
+    )
+
+
 def solution(mesh):
     shards = ("dp", "fsdp")
     row = P(shards, "ctx", None)
     vector = P(shards)
     matrix = P(shards, None)
     return jax.shard_map(
-        body,
+        fast_body if fits(mesh) else body,
         mesh=mesh,
         in_specs=(
             row,

time: 1630 us -> 880 us (0.54)
  waiting for transfers between devices: 740 us -> 400 us
  other arithmetic: 302 us -> 22.9 us
  Pallas kernels: 0 us -> 266 us
  matrix products: 219 us -> 0 us
  local copies, waits for them, and re-layouts: 246 us -> 78.3 us
  starting transfers between devices: 113 us -> 81.3 us
    ppermute x99 -> x45, waiting for transfers between devices: 740 us -> 296 us  [swap(): return lax.ppermute(block, axis, [(i, i ^ bit) for i in range(count)])]
    pallas_call x0 -> x42, Pallas kernels: none -> 266 us  [call(): return lambda *operands: run(*operands, *after)]
    dot_general x17 -> x0, matrix products: 199 us -> none  [the longest x4 49.5 us: contract_cols(): lax.dot_general(left, right, (((1,), (1,)), ((), ())), preferred_element_...]
    all_to_all x0 -> x9, waiting for transfers between devices: none -> 100 us  [to_line(): return lax.all_to_all(blocks, 'dp', split_axis=0, concat_axis=0)]
    ppermute x99 -> x45, starting transfers between devices: 113 us -> 42.3 us  [swap(): return lax.ppermute(block, axis, [(i, i ^ bit) for i in range(count)])]
    select_n x40 -> x1, other arithmetic: 67.5 us -> 0.08 us  [fast_body(): jnp.where(jnp.arange(count)[None, None, :, None] == ctx, bias_sums.reshap...]
    convert_element_type x14 -> x11, other arithmetic: 78.7 us -> 14 us  [the longest x1 5.27 us: fast_body(): down_out = ctx_rows(down_grad).astype(jnp.float32)]
    concatenate x35 -> x3, other arithmetic: 68.8 us -> 8.61 us  [the longest x1 3.71 us: fast_body(): jnp.concatenate(rows_gather(hold(places, cotangent[0], token_rows)), axis=0)]
  transfers between devices with their start and end apart: 99 -> 59, of which waited for: 36 -> 32; matrix products, arithmetic and copies ran while one was open for 39% -> 4% of each run, Pallas kernels for 0% -> 25%
where the time goes in v3:
time: 880 us; the launch traced here: 869 us
  waiting for transfers between devices  400 us (45%)
  Pallas kernels  266 us (30%)
  starting transfers between devices  81.3 us (9%)
  local copies, waits for them, and re-layouts  78.3 us (9%)
  other arithmetic  22.9 us (3%)
  between operations  15.4 us (2%)
    ppermute x45, waiting for transfers between devices, swap(): return lax.ppermute(block, axis, [(i, i ^ bit) for i in range(count)])  296 us
    pallas_call x42, Pallas kernels, call(): return lambda *operands: run(*operands, *after)  266 us
    all_to_all x9, waiting for transfers between devices, to_line(): return lax.all_to_all(blocks, 'dp', split_axis=0, concat_axis=0)  100 us
    unnamed x201, local copies, waits for them, and re-layouts  66 us
    ppermute x45, starting transfers between devices, swap(): return lax.ppermute(block, axis, [(i, i ^ bit) for i in range(count)])  42.3 us
    all_to_all x9, starting transfers between devices, to_line(): return lax.all_to_all(blocks, 'dp', split_axis=0, concat_axis=0)  38.8 us
  transfers between devices with their start and end apart: 59, of which 32 were waited for; matrix products, arithmetic and copies ran while one was open for 4% of the time, Pallas kernels for 25%

profile of v3, /device:TPU:0, one launch (start us, length us, event | category | flops | bytes accessed | tf_op | source)
XLA Modules:
  0.0 869.1 jit_solution(4890557126109128822)
XLA Ops:
  16.6 6.3 all-to-all-start
  24.4 25.7 %all-to-all-done.refs_1_.refs_3_ = bf16[4,272,512]{2,1,0:T(8,128)(2,1)} async-done(((bf16[4,272,512]{2,1,0:T(8,128)(2,1)}), bf16[4,272,512]{2,1,0:T(8,128)(2,1)}, u32[]{:S(2)}, u32[]{:S(2)}) %all-to-all-start) | async-done | bytes 1114144 | tf_op jit(solution)/shard_map/all_to_all | solution.py:1266
  66.4 17.4 %all-to-all-done.1.refs_1_.refs_2_.refs_4_ = bf16[4,256,512]{2,1,0:T(8,128)(2,1)} async-done(((bf16[4,256,512]{2,1,0:T(8,128)(2,1)}), bf16[4,256,512]{2,1,0:T(8,128)(2,1)}, u32[]{:S(2)}, u32[]{:S(2)}) %all-to-all-start.1) | async-done | bytes 1048608 | tf_op jit(solution)/shard_map/all_to_all | solution.py:1266
  97.3 33.1 %collective-permute-done.3.refs_2_.refs_6_ = bf16[4,272,512]{2,1,0:T(8,128)(2,1)S(1)} collective-permute-done((bf16[4,272,512]{2,1,0:T(8,128)(2,1)}, bf16[4,272,512]{2,1,0:T(8,128)(2,1)S(1)}, u32[]{:S(2)}, u32[]{:S(2)}) %collective-permute-start.3) | collective-permute-done | bytes 1114144 | tf_op jit(solution)/shard_map/ppermute | solution.py:24
  153.3 19.2 %collective-permute-done.4.refs_2_.refs_7_ = bf16[4,256,512]{2,1,0:T(8,128)(2,1)S(1)} collective-permute-done((bf16[4,256,512]{2,1,0:T(8,128)(2,1)}, bf16[4,256,512]{2,1,0:T(8,128)(2,1)S(1)}, u32[]{:S(2)}, u32[]{:S(2)}) %collective-permute-start.4) | collective-permute-done | bytes 1048608 | tf_op jit(solution)/shard_map/ppermute | solution.py:24
  173.5 10.5 %all-to-all-done.2.refs_1_.refs_5_ = bf16[4,256,512]{2,1,0:T(8,128)(2,1)} async-done(((bf16[4,256,512]{2,1,0:T(8,128)(2,1)}), bf16[4,256,512]{2,1,0:T(8,128)(2,1)}, u32[]{:S(2)}, u32[]{:S(2)}) %all-to-all-start.2) | async-done | bytes 1048608 | tf_op jit(solution)/shard_map/all_to_all | solution.py:1266
  195.0 7.2 shard_map.231.refs_0_
  207.8 6.3 shard_map.232.refs_7_.refs_0_
  218.8 6.2 shard_map.234.refs_4_.refs_1_
  225.1 15.0 %collective-permute-done.5.refs_2_.refs_8_ = bf16[4,256,512]{2,1,0:T(8,128)(2,1)} collective-permute-done((bf16[4,256,512]{2,1,0:T(8,128)(2,1)}, bf16[4,256,512]{2,1,0:T(8,128)(2,1)}, u32[]{:S(2)}, u32[]{:S(2)}) %collective-permute-start.5) | collective-permute-done | bytes 1048608 | tf_op jit(solution)/shard_map/ppermute | solution.py:24
  259.8 18.0 %shard_map.237 = (bf16[1024,512]{1,0:T(8,128)(2,1)S(1)}, f32[4,2,1024]{2,1,0:T(2,128)S(1)}) custom-call(s32[13]{0:T(128)S(1)} %stack.55.places_ref, bf16[1024,512]{1,0:T(8,128)(2,1)S(1)} %copy-done.20, bf16[1024,512]{1,0:T(8,128)(2,1)S(1)} %copy-done.22, bf16[1024,512]{1,0:T(8,128)(2,1)S(1)} %copy-done.16, s32[1024,1]{1,0:T(8,128)S(1)} %copy.42.refs_3_.refs_5_, ...), custom_call_target="tpu_custom_call" | custom-call | flops 1 | bytes 1 | tf_op jit(solution)/shard_map/pallas_call | solution.py:381
  290.3 23.8 %collective-permute-done.11.refs_3_ = bf16[256,2048]{1,0:T(8,128)(2,1)S(1)} collective-permute-done((bf16[256,2048]{1,0:T(8,128)(2,1)S(1)}, bf16[256,2048]{1,0:T(8,128)(2,1)S(1)}, u32[]{:S(2)}, u32[]{:S(2)}) %collective-permute-start.11) | collective-permute-done | bytes 1048608 | tf_op jit(solution)/shard_map/ppermute | solution.py:24
  320.1 30.2 %all-to-all-done.4.refs_0_ = bf16[4,176,2048]{2,1,0:T(8,128)(2,1)S(1)} async-done(((bf16[4,176,2048]{2,1,0:T(8,128)(2,1)}), bf16[4,176,2048]{2,1,0:T(8,128)(2,1)S(1)}, u32[]{:S(2)}, u32[]{:S(2)}) %all-to-all-start.4) | async-done | bytes 2883616 | tf_op jit(solution)/shard_map/all_to_all | solution.py:1266
  355.4 23.1 %collective-permute-done.12.refs_1_ = bf16[256,2048]{1,0:T(8,128)(2,1)S(1)} collective-permute-done((bf16[256,2048]{1,0:T(8,128)(2,1)S(1)}, bf16[256,2048]{1,0:T(8,128)(2,1)S(1)}, u32[]{:S(2)}, u32[]{:S(2)}) %collective-permute-start.12) | collective-permute-done | bytes 1048608 | tf_op jit(solution)/shard_map/ppermute | solution.py:24
  381.3 19.8 %shard_map.244 = (bf16[1024,2048]{1,0:T(8,128)(2,1)}, bf16[1024,2816]{1,0:T(8,128)(2,1)}, bf16[1024,1408]{1,0:T(8,128)(2,1)}) custom-call(s32[13]{0:T(128)} %copy-done.81, bf16[256,2048]{1,0:T(8,128)(2,1)} %copy-done.78, bf16[256,2048]{1,0:T(8,128)(2,1)} %copy-done.87, bf16[256,2048]{1,0:T(8,128)(2,1)} %copy-done.88, ...), custom_call_target="tpu_custom_call" | custom-call | flops 1 | bytes 1 | tf_op jit(solution)/shard_map/pallas_call | solution.py:381
  401.2 11.2 %shard_map.247 = (bf16[4,176,2048]{2,1,0:T(8,128)(2,1)S(1)}, bf16[4,176,2048]{2,1,0:T(8,128)(2,1)}) custom-call(s32[13]{0:T(128)S(1)} %copy-done.82, bf16[1024,1408]{1,0:T(8,128)(2,1)} %get-tuple-element.50.refs_0_, bf16[1024,2048]{1,0:T(8,128)(2,1)} %pad_maximum_fusion.1.refs_3_.refs_1_.refs_0_), custom_call_target="tpu_custom_call" | custom-call | flops 1 | bytes 1 | tf_op jit(solution)/shard_map/pallas_call | solution.py:381
  416.6 15.9 %shard_map.248.refs_1_.refs_0_ = bf16[1024,2816]{1,0:T(8,128)(2,1)} custom-call(s32[13]{0:T(128)} %copy-done.81, bf16[1024,2048]{1,0:T(8,128)(2,1)} %pad_maximum_fusion.1.refs_3_.refs_1_.refs_0_, bf16[4,176,2048]{2,1,0:T(8,128)(2,1)} %copy-done.5, bf16[4,176,2048]{2,1,0:T(8,128)(2,1)} %collective-permute-done.15.refs_2_, ...), custom_call_target="tpu_custom_call" | custom-call | flops 1 | bytes 1 | tf_op jit(solution)/shard_map/pallas_call | solution.py:381
  432.6 18.4 %shard_map.249.refs_2_ = bf16[2048,2816]{1,0:T(8,128)(2,1)} custom-call(s32[13]{0:T(128)S(1)} %copy-done.83, bf16[1024,2048]{1,0:T(8,128)(2,1)S(1)} %copy-done.68, bf16[1024,2816]{1,0:T(8,128)(2,1)} %shard_map.248.refs_1_.refs_0_), custom_call_target="tpu_custom_call" | custom-call | flops 1 | bytes 1 | tf_op jit(solution)/shard_map/pallas_call | solution.py:381
  452.8 18.3 %shard_map.250 = (bf16[512,2048]{1,0:T(8,128)(2,1)}, bf16[512,2048]{1,0:T(8,128)(2,1)}) custom-call(s32[13]{0:T(128)} %copy-done.81, bf16[1024,2816]{1,0:T(8,128)(2,1)} %shard_map.248.refs_1_.refs_0_, bf16[2048,2816]{1,0:T(8,128)(2,1)} %all-gather.5.cloned.1.call-done.refs_4_.refs_1_, bf16[2048,2816]{1,0:T(8,128)(2,1)} %shard_map.249.refs_2_), custom_call_target="tpu_custom_call" | custom-call | flops 1 | bytes 1 | tf_op jit(solution)/shard_map/pallas_call | solution.py:381
  475.4 70.0 %collective-permute-done.16.refs_0_ = bf16[4,176,2048]{2,1,0:T(8,128)(2,1)S(1)} collective-permute-done((bf16[4,176,2048]{2,1,0:T(8,128)(2,1)}, bf16[4,176,2048]{2,1,0:T(8,128)(2,1)S(1)}, u32[]{:S(2)}, u32[]{:S(2)}) %collective-permute-start.16) | collective-permute-done | bytes 2883616 | tf_op jit(solution)/shard_map/ppermute | solution.py:24
  558.3 12.0 %shard_map.252 = (bf16[512,2048]{1,0:T(8,128)(2,1)S(1)}, bf16[512,2048]{1,0:T(8,128)(2,1)S(1)}) custom-call(s32[13]{0:T(128)S(1)} %copy-done.84, bf16[1024,1408]{1,0:T(8,128)(2,1)} %get-tuple-element.50.refs_0_, bf16[4,176,2048]{2,1,0:T(8,128)(2,1)} %copy-done.5, bf16[4,176,2048]{2,1,0:T(8,128)(2,1)} %collective-permute-done.15.refs_2_, ...), custom_call_target="tpu_custom_call" | custom-call | flops 1 | bytes 1 | tf_op jit(solution)/shard_map/pallas_call | solution.py:381
  573.1 6.9 collective-permute-done.19.refs_5_
  588.2 20.9 %collective-permute-done.21.refs_1_ = bf16[256,2048]{1,0:T(8,128)(2,1)S(1)} collective-permute-done((bf16[256,2048]{1,0:T(8,128)(2,1)S(1)}, bf16[256,2048]{1,0:T(8,128)(2,1)S(1)}, u32[]{:S(2)}, u32[]{:S(2)}) %collective-permute-start.21) | collective-permute-done | bytes 1048608 | tf_op jit(solution)/shard_map/ppermute | solution.py:24
  611.8 6.7 shard_map.256
  626.0 22.5 %shard_map.258 = (bf16[1024,512]{1,0:T(8,128)(2,1)S(1)}, bf16[1024,512]{1,0:T(8,128)(2,1)S(1)}, bf16[1024,512]{1,0:T(8,128)(2,1)S(1)}, f32[3,1,512]{2,1,0:T(1,128)S(1)}) custom-call(s32[13]{0:T(128)S(1)} %copy-done.84, bf16[1024,512]{1,0:T(8,128)(2,1)} %copy-done.19, bf16[1024,512]{1,0:T(8,128)(2,1)} %copy-done.21, bf16[1024,512]{1,0:T(8,128)(2,1)} %copy-done.15, ...), custom_call_target="tpu_custom_call" | custom-call | flops 1 | bytes 1 | tf_op jit(solution)/shard_map/pallas_call | solution.py:381
  649.5 9.0 %shard_map.259 = (bf16[1024,512]{1,0:T(8,128)(2,1)S(1)}, bf16[1024,512]{1,0:T(8,128)(2,1)}, bf16[1024,512]{1,0:T(8,128)(2,1)S(1)}, bf16[1024,1024]{1,0:T(8,128)(2,1)}) custom-call(s32[13]{0:T(128)S(1)} %copy-done.84, bf16[1024,2048]{1,0:T(8,128)(2,1)} %copy-done.2, bf16[1024,512]{1,0:T(8,128)(2,1)S(1)} %get-tuple-element.65.refs_1_.refs_0_, ...), custom_call_target="tpu_custom_call" | custom-call | flops 1 | bytes 1 | tf_op jit(solution)/shard_map/pallas_call | solution.py:381
  671.6 24.2 %collective-permute-done.25 = bf16[4,256,512]{2,1,0:T(8,128)(2,1)S(1)} collective-permute-done((bf16[4,256,512]{2,1,0:T(8,128)(2,1)}, bf16[4,256,512]{2,1,0:T(8,128)(2,1)S(1)}, u32[]{:S(2)}, u32[]{:S(2)}) %collective-permute-start.25) | collective-permute-done | bytes 1048608 | tf_op jit(solution)/shard_map/ppermute | solution.py:24
  697.3 20.1 %collective-permute-done.24.refs_2_ = bf16[1024,512]{1,0:T(8,128)(2,1)S(1)} collective-permute-done((bf16[1024,512]{1,0:T(8,128)(2,1)}, bf16[1024,512]{1,0:T(8,128)(2,1)S(1)}, u32[]{:S(2)}, u32[]{:S(2)}) %collective-permute-start.24) | collective-permute-done | bytes 1048608 | tf_op jit(solution)/shard_map/ppermute | solution.py:24
  733.7 12.1 %shard_map.262 = (bf16[512,2048]{1,0:T(8,128)(2,1)}, bf16[512,2048]{1,0:T(8,128)(2,1)}) custom-call(s32[13]{0:T(128)S(1)} %copy-done.84, bf16[1024,512]{1,0:T(8,128)(2,1)S(1)} %copy-done.34, bf16[1024,512]{1,0:T(8,128)(2,1)S(1)} %copy-done.28, bf16[1024,512]{1,0:T(8,128)(2,1)S(1)} %copy-done.38, bf16[4,272,512]{2,1,0:T(8,128)(2,1)} %all-to-all-done.refs_1_.refs_3_, ...), custom_call_target="tpu_custom_call" | custom-call | flops 1 | bytes 1 | tf_op jit(solution)/shard_map/pallas_call | solution.py:381
  756.8 15.9 %all-to-all-done.6.refs_0_.refs_1_.refs_2_.refs_3_ = bf16[4,512,512]{2,1,0:T(8,128)(2,1)S(1)} async-done(((bf16[4,512,512]{2,1,0:T(8,128)(2,1)}), bf16[4,512,512]{2,1,0:T(8,128)(2,1)S(1)}, u32[]{:S(2)}, u32[]{:S(2)}) %all-to-all-start.6) | async-done | bytes 2097184 | tf_op jit(solution)/shard_map/all_to_all | solution.py:1266
  783.9 7.7 shard_map.263.refs_3_
  813.6 12.3 %collective-permute-done.28.refs_5_ = bf16[256,2048]{1,0:T(8,128)(2,1)} collective-permute-done((bf16[256,2048]{1,0:T(8,128)(2,1)}, bf16[256,2048]{1,0:T(8,128)(2,1)}, u32[]{:S(2)}, u32[]{:S(2)}) %collective-permute-start.28) | collective-permute-done | bytes 1048608 | tf_op jit(solution)/shard_map/ppermute | solution.py:24
  (395 shorter events, 287.9 us)
Async XLA Ops:
  16.6 33.6 %all-to-all-start = ((bf16[4,272,512]{2,1,0:T(8,128)(2,1)}), bf16[4,272,512]{2,1,0:T(8,128)(2,1)}, u32[]{:S(2)}, u32[]{:S(2)}) async-start(bf16[4,272,512]{2,1,0:T(8,128)(2,1)} %broadcast_dynamic-update-slice_fusion), calls=%async_computation | async-start | bytes 2228224 | tf_op jit(solution)/shard_map/all_to_all | solution.py:1266
  22.9 35.7 %collective-permute-start = (bf16[256,2048]{1,0:T(8,128)(2,1)}, bf16[256,2048]{1,0:T(8,128)(2,1)}, u32[]{:S(2)}, u32[]{:S(2)}) collective-permute-start(bf16[256,2048]{1,0:T(8,128)(2,1)} %bitcast.78), channel_id=1, source_target_pairs={{0,4},{2,6},{4,0},{6,2},{1,5},{3,7},{5,1},{7,3},{8,12},{10,14},{12... | collective-permute-start | bytes 3145736 | tf_op jit(solution)/shard_map/ppermute | solution.py:24
  54.2 29.5 %all-to-all-start.1 = ((bf16[4,256,512]{2,1,0:T(8,128)(2,1)}), bf16[4,256,512]{2,1,0:T(8,128)(2,1)}, u32[]{:S(2)}, u32[]{:S(2)}) async-start(bf16[4,256,512]{2,1,0:T(8,128)(2,1)} %copy-done.67), calls=%async_computation.1 | async-start | bytes 2097152 | tf_op jit(solution)/shard_map/all_to_all | solution.py:1266
  58.5 322.9 %all-gather.5.cloned.1.call-start = ((), (), s32[]{:S(2)}) async-start(), calls=%async_computation.10 | async-start | bytes 12976128 | tf_op jit(solution)/shard_map/all_gather | solution.py:1355
  89.1 41.3 %collective-permute-start.3 = (bf16[4,272,512]{2,1,0:T(8,128)(2,1)}, bf16[4,272,512]{2,1,0:T(8,128)(2,1)S(1)}, u32[]{:S(2)}, u32[]{:S(2)}) collective-permute-start(bf16[4,272,512]{2,1,0:T(8,128)(2,1)} %all-to-all-done.refs_1_.refs_3_), channel_id=1, source_target_pairs={{0,1},{1,0},{2,3},{3,2},{4,5},{5,4},{6,7},{7,6},{8,9},{9,8},{10,11... | collective-permute-start | bytes 3342344 | tf_op jit(solution)/shard_map/ppermute | solution.py:24
  95.7 43.9 %collective-permute-start.6 = (bf16[256,2048]{1,0:T(8,128)(2,1)}, bf16[256,2048]{1,0:T(8,128)(2,1)}, u32[]{:S(2)}, u32[]{:S(2)}) collective-permute-start(bf16[256,2048]{1,0:T(8,128)(2,1)} %shard_map.238), channel_id=1, source_target_pairs={{0,4},{2,6},{4,0},{6,2},{1,5},{3,7},{5,1},{7,3},{8,12},{10,14},{12... | collective-permute-start | bytes 3145736 | tf_op jit(solution)/shard_map/ppermute | solution.py:24
  135.3 48.7 %all-to-all-start.2 = ((bf16[4,256,512]{2,1,0:T(8,128)(2,1)}), bf16[4,256,512]{2,1,0:T(8,128)(2,1)}, u32[]{:S(2)}, u32[]{:S(2)}) async-start(bf16[4,256,512]{2,1,0:T(8,128)(2,1)} %copy-done.69), calls=%async_computation.2 | async-start | bytes 2097152 | tf_op jit(solution)/shard_map/all_to_all | solution.py:1266
  145.2 27.3 %collective-permute-start.4 = (bf16[4,256,512]{2,1,0:T(8,128)(2,1)}, bf16[4,256,512]{2,1,0:T(8,128)(2,1)S(1)}, u32[]{:S(2)}, u32[]{:S(2)}) collective-permute-start(bf16[4,256,512]{2,1,0:T(8,128)(2,1)} %all-to-all-done.1.refs_1_.refs_2_.refs_4_), channel_id=1, source_target_pairs={{0,1},{1,0},{2,3},{3,2},{4,5},{5,4},{6,7},{7,6},{8,9},{9,8},{10,11... | collective-permute-start | bytes 3145736 | tf_op jit(solution)/shard_map/ppermute | solution.py:24
  189.0 57.8 %all-to-all-start.3 = ((bf16[4,64,2048]{2,1,0:T(8,128)(2,1)}), bf16[4,64,2048]{2,1,0:T(8,128)(2,1)S(1)}, u32[]{:S(2)}, u32[]{:S(2)}) async-start(bf16[4,64,2048]{2,1,0:T(8,128)(2,1)} %broadcast_in_dim.58), calls=%async_computation.3 | async-start | bytes 2097152 | tf_op jit(solution)/shard_map/all_to_all | solution.py:1266
  193.4 46.7 %collective-permute-start.5 = (bf16[4,256,512]{2,1,0:T(8,128)(2,1)}, bf16[4,256,512]{2,1,0:T(8,128)(2,1)}, u32[]{:S(2)}, u32[]{:S(2)}) collective-permute-start(bf16[4,256,512]{2,1,0:T(8,128)(2,1)} %all-to-all-done.2.refs_1_.refs_5_), channel_id=1, source_target_pairs={{0,1},{1,0},{2,3},{3,2},{4,5},{5,4},{6,7},{7,6},{8,9},{9,8},{10,11... | collective-permute-start | bytes 3145736 | tf_op jit(solution)/shard_map/ppermute | solution.py:24
  249.3 100.9 %all-to-all-start.4 = ((bf16[4,176,2048]{2,1,0:T(8,128)(2,1)}), bf16[4,176,2048]{2,1,0:T(8,128)(2,1)S(1)}, u32[]{:S(2)}, u32[]{:S(2)}) async-start(bf16[4,176,2048]{2,1,0:T(8,128)(2,1)} %broadcast_in_dim.59), calls=%async_computation.4 | async-start | bytes 5767168 | tf_op jit(solution)/shard_map/all_to_all | solution.py:1266
  254.3 415.2 %reduce-scatter.2.cloned.1.call-start = ((), (), s32[]{:S(2)}) async-start(), calls=%async_computation.11 | async-start | bytes 12976128 | tf_op jit(solution)/shard_map/reduce_scatter | solution.py:1413
  352.4 64.2 %collective-permute-start.15 = (bf16[4,176,2048]{2,1,0:T(8,128)(2,1)S(1)}, bf16[4,176,2048]{2,1,0:T(8,128)(2,1)}, u32[]{:S(2)}, u32[]{:S(2)}) collective-permute-start(bf16[4,176,2048]{2,1,0:T(8,128)(2,1)S(1)} %shard_map.246.refs_1_), channel_id=1, source_target_pairs={{0,1},{1,0},{2,3},{3,2},{4,5},{5,4},{6,7},{7,6},{8,9},{9,8},{10,11... | collective-permute-start | bytes 8650760 | tf_op jit(solution)/shard_map/ppermute | solution.py:24
  451.0 94.4 %collective-permute-start.16 = (bf16[4,176,2048]{2,1,0:T(8,128)(2,1)}, bf16[4,176,2048]{2,1,0:T(8,128)(2,1)S(1)}, u32[]{:S(2)}, u32[]{:S(2)}) collective-permute-start(bf16[4,176,2048]{2,1,0:T(8,128)(2,1)} %get-tuple-element.52.refs_4_), channel_id=1, source_target_pairs={{0,1},{1,0},{2,3},{3,2},{4,5},{5,4},{6,7},{7,6},{8,9},{9,8},{10,11... | collective-permute-start | bytes 8650760 | tf_op jit(solution)/shard_map/ppermute | solution.py:24
  549.0 113.6 %all-to-all-start.5 = ((bf16[4,176,2048]{2,1,0:T(8,128)(2,1)}), bf16[4,176,2048]{2,1,0:T(8,128)(2,1)S(1)}, u32[]{:S(2)}, u32[]{:S(2)}) async-start(bf16[4,176,2048]{2,1,0:T(8,128)(2,1)} %add_convert_fusion.refs_3_), calls=%async_computation.5 | async-start | bytes 5767168 | tf_op jit(solution)/shard_map/all_to_all | solution.py:1266
  552.7 194.7 %all-gather.9.cloned.1.call-start = ((), (), s32[]{:S(2)}) async-start(), calls=%async_computation.13 | async-start | bytes 3604480 | tf_op jit(solution)/shard_map/all_gather | solution.py:1435
  665.6 115.6 %all-gather.7.cloned.1.call-start = ((), (), s32[]{:S(2)}) async-start(), calls=%async_computation.12 | async-start | bytes 7208960 | tf_op jit(solution)/shard_map/all_gather | solution.py:1435
  669.5 26.3 %collective-permute-start.25 = (bf16[4,256,512]{2,1,0:T(8,128)(2,1)}, bf16[4,256,512]{2,1,0:T(8,128)(2,1)S(1)}, u32[]{:S(2)}, u32[]{:S(2)}) collective-permute-start(bf16[4,256,512]{2,1,0:T(8,128)(2,1)} %copy-done.77), channel_id=1, source_target_pairs={{0,1},{1,0},{2,3},{3,2},{4,5},{5,4},{6,7},{7,6},{8,9},{9,8},{10,11... | collective-permute-start | bytes 3145736 | tf_op jit(solution)/shard_map/ppermute | solution.py:24
  670.1 47.3 %collective-permute-start.24 = (bf16[1024,512]{1,0:T(8,128)(2,1)}, bf16[1024,512]{1,0:T(8,128)(2,1)S(1)}, u32[]{:S(2)}, u32[]{:S(2)}) collective-permute-start(bf16[1024,512]{1,0:T(8,128)(2,1)} %copy-done.86), channel_id=1, source_target_pairs={{0,1},{1,0},{2,3},{3,2},{4,5},{5,4},{6,7},{7,6},{8,9},{9,8},{10,11... | collective-permute-start | bytes 3145736 | tf_op jit(solution)/shard_map/ppermute | solution.py:24
  671.6 53.7 %collective-permute-start.18 = (bf16[512,2048]{1,0:T(8,128)(2,1)}, bf16[512,2048]{1,0:T(8,128)(2,1)}, u32[]{:S(2)}, u32[]{:S(2)}) collective-permute-start(bf16[512,2048]{1,0:T(8,128)(2,1)} %copy-done.85), channel_id=1, source_target_pairs={{0,2},{2,0},{4,6},{6,4},{1,3},{3,1},{5,7},{7,5},{8,10},{10,8},{12,... | collective-permute-start | bytes 6291464 | tf_op jit(solution)/shard_map/ppermute | solution.py:24
  721.1 51.6 %all-to-all-start.6 = ((bf16[4,512,512]{2,1,0:T(8,128)(2,1)}), bf16[4,512,512]{2,1,0:T(8,128)(2,1)S(1)}, u32[]{:S(2)}, u32[]{:S(2)}) async-start(bf16[4,512,512]{2,1,0:T(8,128)(2,1)} %pad_maximum_fusion.2.refs_9_), calls=%async_computation.7 | async-start | bytes 4194304 | tf_op jit(solution)/shard_map/all_to_all | solution.py:1266
  724.7 27.9 %collective-permute-start.29 = (bf16[1024,512]{1,0:T(8,128)(2,1)}, bf16[1024,512]{1,0:T(8,128)(2,1)}, u32[]{:S(2)}, u32[]{:S(2)}) collective-permute-start(bf16[1024,512]{1,0:T(8,128)(2,1)} %copy-done.74), channel_id=1, source_target_pairs={{0,1},{1,0},{2,3},{3,2},{4,5},{5,4},{6,7},{7,6},{8,9},{9,8},{10,11... | collective-permute-start | bytes 3145736 | tf_op jit(solution)/shard_map/ppermute | solution.py:24
  732.3 44.0 %collective-permute-start.20 = (bf16[256,2048]{1,0:T(8,128)(2,1)}, bf16[256,2048]{1,0:T(8,128)(2,1)}, u32[]{:S(2)}, u32[]{:S(2)}) collective-permute-start(bf16[256,2048]{1,0:T(8,128)(2,1)} %shard_map.255), channel_id=1, source_target_pairs={{0,4},{2,6},{4,0},{6,2},{1,5},{3,7},{5,1},{7,3},{8,12},{10,14},{12... | collective-permute-start | bytes 3145736 | tf_op jit(solution)/shard_map/ppermute | solution.py:24
  745.8 49.6 %collective-permute-start.26 = (bf16[512,2048]{1,0:T(8,128)(2,1)}, bf16[512,2048]{1,0:T(8,128)(2,1)}, u32[]{:S(2)}, u32[]{:S(2)}) collective-permute-start(bf16[512,2048]{1,0:T(8,128)(2,1)} %get-tuple-element.73), channel_id=1, source_target_pairs={{0,2},{2,0},{4,6},{6,4},{1,3},{3,1},{5,7},{7,5},{8,10},{10,8},{12,... | collective-permute-start | bytes 6291464 | tf_op jit(solution)/shard_map/ppermute | solution.py:24
  745.9 45.7 %collective-permute-start.27 = (bf16[1024,512]{1,0:T(8,128)(2,1)}, bf16[1024,512]{1,0:T(8,128)(2,1)}, u32[]{:S(2)}, u32[]{:S(2)}) collective-permute-start(bf16[1024,512]{1,0:T(8,128)(2,1)} %get-tuple-element.74), channel_id=1, source_target_pairs={{0,1},{1,0},{2,3},{3,2},{4,5},{5,4},{6,7},{7,6},{8,9},{9,8},{10,11... | collective-permute-start | bytes 3145736 | tf_op jit(solution)/shard_map/ppermute | solution.py:24
  772.7 28.7 %all-to-all-start.8 = ((bf16[4,256,512]{2,1,0:T(8,128)(2,1)}), bf16[4,256,512]{2,1,0:T(8,128)(2,1)S(1)}, u32[]{:S(2)}, u32[]{:S(2)}) async-start(bf16[4,256,512]{2,1,0:T(8,128)(2,1)} %bitcast.83), calls=%async_computation.9 | async-start | bytes 2097152 | tf_op jit(solution)/shard_map/all_to_all | solution.py:1266
  776.2 31.0 %all-gather.11.cloned.1.call-start = ((), (), s32[]{:S(2)}) async-start(), calls=%async_computation.14 | async-start | bytes 1310720 | tf_op jit(solution)/shard_map/all_gather | solution.py:1435
  799.5 26.4 %collective-permute-start.28 = (bf16[256,2048]{1,0:T(8,128)(2,1)}, bf16[256,2048]{1,0:T(8,128)(2,1)}, u32[]{:S(2)}, u32[]{:S(2)}) collective-permute-start(bf16[256,2048]{1,0:T(8,128)(2,1)} %shard_map.265), channel_id=1, source_target_pairs={{0,4},{2,6},{4,0},{6,2},{1,5},{3,7},{5,1},{7,3},{8,12},{10,14},{12... | collective-permute-start | bytes 3145736 | tf_op jit(solution)/shard_map/ppermute | solution.py:24
  801.4 31.1 %all-to-all-start.7 = ((bf16[4,256,512]{2,1,0:T(8,128)(2,1)}), bf16[4,256,512]{2,1,0:T(8,128)(2,1)S(1)}, u32[]{:S(2)}, u32[]{:S(2)}) async-start(bf16[4,256,512]{2,1,0:T(8,128)(2,1)} %bitcast.31.refs_2_), calls=%async_computation.8 | async-start | bytes 2097152 | tf_op jit(solution)/shard_map/all_to_all | solution.py:1266
  806.5 46.5 %collective-permute-start.36 = (bf16[256,512]{1,0:T(8,128)(2,1)S(1)}, bf16[256,512]{1,0:T(8,128)(2,1)}, u32[]{:S(2)}, u32[]{:S(2)}) collective-permute-start(bf16[256,512]{1,0:T(8,128)(2,1)S(1)} %get-tuple-element.97.refs_0_), channel_id=1, source_target_pairs={{0,4},{2,6},{4,0},{6,2},{1,5},{3,7},{5,1},{7,3},{8,12},{10,14},{12... | collective-permute-start | bytes 786440 | tf_op jit(solution)/shard_map/ppermute | solution.py:24
  807.2 46.3 %collective-permute-start.37 = (bf16[256,512]{1,0:T(8,128)(2,1)S(1)}, bf16[256,512]{1,0:T(8,128)(2,1)}, u32[]{:S(2)}, u32[]{:S(2)}) collective-permute-start(bf16[256,512]{1,0:T(8,128)(2,1)S(1)} %get-tuple-element.97.refs_0_), channel_id=1, source_target_pairs={{0,2},{2,0},{4,6},{6,4},{1,3},{3,1},{5,7},{7,5},{8,10},{10,8},{12,... | collective-permute-start | bytes 786440 | tf_op jit(solution)/shard_map/ppermute | solution.py:24
  812.2 41.5 %collective-permute-start.42 = (bf16[256,512]{1,0:T(8,128)(2,1)}, bf16[256,512]{1,0:T(8,128)(2,1)}, u32[]{:S(2)}, u32[]{:S(2)}) collective-permute-start(bf16[256,512]{1,0:T(8,128)(2,1)} %shard_map.270.refs_8_), channel_id=1, source_target_pairs={{0,4},{2,6},{4,0},{6,2},{1,5},{3,7},{5,1},{7,3},{8,12},{10,14},{12... | collective-permute-start | bytes 786440 | tf_op jit(solution)/shard_map/ppermute | solution.py:24
  (120 other events, 1778.0 us)
Sparse Core Ops, SparseCore 0:
  89.2 252.2 all-gather.4
  451.2 218.2 reduce-scatter.1
  671.1 25.0 all-gather.8
  697.6 48.2 all-gather.6
  781.3 17.1 all-gather.10

commit v4 on v3

--- a/solution.py
+++ b/solution.py
@@ -446,7 +446,7 @@
     )
 
 
-def take_columns(places, w, count, shards, groups, group, copies, pad, after=()):
+def take_columns(places, w, count, shards, groups, copies, pad, after=()):
     depth = w.shape[0]
     each = w.shape[1] // groups
     unit = each // (shards * count)
@@ -469,10 +469,10 @@
 
     return call(
         kernel,
-        (4,),
-        [pl.BlockSpec((tile, each), lambda m, _: (m, group))],
-        pl.BlockSpec((copies, tile, each // count), lambda m, _: (0, m, 0)),
-        sds((copies, depth + pad, each // count), jnp.bfloat16),
+        (groups, 4),
+        [pl.BlockSpec((tile, each), lambda g, m, _: (m, g))],
+        pl.BlockSpec((copies, tile, each // count), lambda g, m, _: (0, m, g)),
+        sds((copies, depth + pad, w.shape[1] // count), jnp.bfloat16),
         after=after,
     )(places, w)
 
@@ -693,7 +693,7 @@
     )(places, source, added, gain, *pieces)
 
 
-def project(places, normed, near, far, bias, tables, after=()):
+def project(places, normed, near, far, group, bias, tables, after=()):
     length = normed.shape[0]
     width = bias.shape[1]
     tile = min(width, 256)
@@ -718,10 +718,11 @@
             )
         o_ref[...] = total.astype(jnp.bfloat16)
 
-    weight = pl.BlockSpec((blocks, depth, tile), lambda n, _: (0, 0, n))
-    return call(
-        kernel,
-        (width // tile,),
+    steps = width // tile
+    weight = pl.BlockSpec((blocks, depth, tile), lambda n, _: (0, 0, group * steps + n))
+    return call(
+        kernel,
+        (steps,),
         [whole(normed), weight, weight, pl.BlockSpec((1, tile), lambda n, _: (0, n))]
         + [whole(table) for table in tables],
         pl.BlockSpec((length, tile), lambda n, _: (0, n)),
@@ -742,9 +743,9 @@
         target_ref[b * rows : (b + 1) * rows] = source_ref[pl.ds(start, rows)]
 
 
-def masked(scores, keys_seg, query_seg, first):
-    ks = lax.broadcasted_iota(jnp.int32, scores.shape, 0)
-    qs = lax.broadcasted_iota(jnp.int32, scores.shape, 1) + first
+def masked(shape, keys_seg, query_seg, first):
+    ks = lax.broadcasted_iota(jnp.int32, shape, 0)
+    qs = lax.broadcasted_iota(jnp.int32, shape, 1) + first
     return (ks <= qs) & (keys_seg == query_seg)
 
 
@@ -759,13 +760,13 @@
         for a in range(length // step):
             n = (a + 1) * step
             halves = []
+            allowed = masked((n, step), col_ref[0:n], row_ref[:, a * step : n], a * step)
             for h in range(2):
-                query = head_lanes(q_ref[a * step : n], h)
+                query = head_lanes(q_ref[a * step : n], h) * scale
                 scores = lax.dot_general(
                     k_ref[0:n], query, (((1,), (1,)), ((), ())), preferred_element_type=jnp.float32
                 )
-                allowed = masked(scores, col_ref[0:n], row_ref[:, a * step : n], a * step)
-                scores = jnp.where(allowed, scores * scale, masked_score)
+                scores = jnp.where(allowed, scores, masked_score)
                 top = jnp.max(scores, axis=0, keepdims=True)
                 weights = jnp.exp(scores - top)
                 total = jnp.sum(weights, axis=0, keepdims=True)
@@ -836,15 +837,15 @@
         for a in range(length // step):
             n = (a + 1) * step
             halves = []
+            allowed = masked((n, step), col_ref[0:n], row_ref[:, a * step : n], a * step)
             for h in range(2):
-                query = head_lanes(q_ref[a * step : n], h)
+                query = head_lanes(q_ref[a * step : n], h) * scale
                 grad = head_lanes(gs[a * step : n], h)
                 scores = lax.dot_general(
                     k_ref[0:n], query, (((1,), (1,)), ((), ())), preferred_element_type=jnp.float32
                 )
-                allowed = masked(scores, col_ref[0:n], row_ref[:, a * step : n], a * step)
                 log = log_ref[0, h : h + 1, a * step : n]
-                weights = jnp.exp(jnp.where(allowed, scores * scale - log, masked_score))
+                weights = jnp.exp(jnp.where(allowed, scores - log, masked_score))
                 grad_weights = lax.dot_general(
                     v_ref[0:n], grad, (((1,), (1,)), ((), ())), preferred_element_type=jnp.float32
                 )
@@ -870,8 +871,9 @@
             cosine, low, high = cos_ref[at], low_ref[at], high_ref[at]
             for i, (part, out_ref) in enumerate(((dq, dq_ref), (dk, dk_ref), (dv, dv_ref))):
                 block = part[at]
+                if i == 0:
+                    block = block * scale
                 if i < 2:
-                    block = block * scale
                     block = (
                         block * cosine
                         - pltpu.roll(block, 128 - ROT // 2, 1) * low
@@ -913,23 +915,26 @@
 
 
 def join_rows(places_ref, first, refs, joined):
-    r = 0
-    for ref in refs:
+    halves = len(refs) // 2
+    width = refs[0].shape[-1]
+    for at, ref in enumerate(refs):
         blocks, size, _ = ref.shape
+        columns = slice(at % halves * width, (at % halves + 1) * width)
         for i in range(blocks):
-            start = pl.multiple_of(places_ref[first + r] * size, size)
-            joined[pl.ds(start, size)] = ref[i]
-            r += 1
-
-
-def row_product(places, left, near, far, count, after=()):
+            place = places_ref[first + at // halves * blocks + i]
+            joined[pl.ds(pl.multiple_of(place * size, size), size), columns] = ref[i]
+
+
+def row_product(places, left, parts, count, after=()):
     length, depth = left.shape
     tile = D // 4
 
-    def kernel(places_ref, x_ref, a_ref, b_ref, near_ref, far_ref, joined):
+    def kernel(places_ref, x_ref, *refs):
+        near_ref, far_ref, joined = refs[-3:]
+
         @pl.when(pl.program_id(0) == 0)
         def _():
-            join_rows(places_ref, 1 + count, (a_ref, b_ref), joined)
+            join_rows(places_ref, 1 + count, refs[:-3], joined)
 
         start = pl.multiple_of(pl.program_id(0) * tile, tile)
         total = jnp.dot(
@@ -943,12 +948,12 @@
     return call(
         kernel,
         (4,),
-        [whole(left), whole(near), whole(far)],
+        [whole(left)] + [whole(part) for part in parts],
         [spec, spec],
         [shape, shape],
         [pltpu.VMEM((depth, D), jnp.bfloat16)],
         after=after,
-    )(places, left, near, far)
+    )(places, left, *parts)
 
 
 def grad_out(places, pieces, near, far, count, after=()):
@@ -1027,15 +1032,17 @@
     )(places, *pieces, weight)
 
 
-def gate_back(places, cotangent, near, far, both, count, after=()):
+def gate_back(places, cotangent, parts, both, count, after=()):
     length, width = both.shape
     units = width // 2
     steps = -(-units // 256)
 
-    def kernel(places_ref, x_ref, a_ref, b_ref, both_ref, o_ref, joined):
+    def kernel(places_ref, x_ref, both_ref, *refs):
+        o_ref, joined = refs[-2:]
+
         @pl.when(pl.program_id(0) == 0)
         def _():
-            join_rows(places_ref, 1 + count, (a_ref, b_ref), joined)
+            join_rows(places_ref, 1 + count, refs[:-2], joined)
 
         start = pl.multiple_of(pl.program_id(0) * 256, 256)
         grad = lax.dot_general(
@@ -1057,13 +1064,13 @@
     return call(
         kernel,
         (steps,),
-        [whole(cotangent), whole(near), whole(far), spec],
+        [whole(cotangent), spec] + [whole(part) for part in parts],
         spec,
         sds((length, width), jnp.bfloat16),
         [pltpu.VMEM((steps * 256, D), jnp.bfloat16)],
         limit=56,
         after=after,
-    )(places, cotangent, near, far, both)
+    )(places, cotangent, both, *parts)
 
 
 def normed_grad(places, left, weight, after=()):
@@ -1092,14 +1099,13 @@
 def normed_grad_parts(places, lefts, parts, count, after=()):
     length, width = lefts[0].shape
     rows = length // count
-    blocks, depth = parts[0][0].shape[0], D // parts[0][0].shape[0] // 2
+    blocks = parts[0].shape[0]
+    depth = D // blocks // 2
     total_width = width * len(lefts)
 
     def kernel(places_ref, *refs):
         left_refs = refs[: len(lefts)]
-        near_refs = refs[len(lefts) : 2 * len(lefts)]
-        far_refs = refs[2 * len(lefts) : 3 * len(lefts)]
-        near_ref, far_ref, joined = refs[3 * len(lefts) :]
+        near_part, far_part, near_ref, far_ref, joined = refs[len(lefts) :]
 
         @pl.when(pl.program_id(0) == 0)
         def _():
@@ -1110,35 +1116,38 @@
                         b * rows : (b + 1) * rows
                     ]
 
-        def run(weight_refs):
-            weight = jnp.concatenate([ref[0] for ref in weight_refs], axis=1)
+        def run(weight_ref):
             total = lax.dot_general(
-                joined[...], weight, (((1,), (1,)), ((), ())), preferred_element_type=jnp.float32
+                joined[...], weight_ref[0], (((1,), (1,)), ((), ())), preferred_element_type=jnp.float32
             ).astype(jnp.bfloat16)
             near_ref[...] = total[: length // 2]
             far_ref[...] = total[length // 2 :]
 
         @pl.when(pl.program_id(0) < blocks)
         def _():
-            run(near_refs)
+            run(near_part)
 
         @pl.when(pl.program_id(0) >= blocks)
         def _():
-            run(far_refs)
-
-    near_spec = pl.BlockSpec((1, depth, width), lambda n, _: (jnp.minimum(n, blocks - 1), 0, 0))
-    far_spec = pl.BlockSpec((1, depth, width), lambda n, _: (jnp.maximum(n - blocks, 0), 0, 0))
+            run(far_part)
+
+    near_spec = pl.BlockSpec(
+        (1, depth, total_width), lambda n, _: (jnp.minimum(n, blocks - 1), 0, 0)
+    )
+    far_spec = pl.BlockSpec(
+        (1, depth, total_width), lambda n, _: (jnp.maximum(n - blocks, 0), 0, 0)
+    )
     spec = pl.BlockSpec((length // 2, depth), lambda n, _: (0, n))
     shape = sds((length // 2, D), jnp.bfloat16)
     return call(
         kernel,
         (2 * blocks,),
-        [whole(left) for left in lefts] + [near_spec] * len(lefts) + [far_spec] * len(lefts),
+        [whole(left) for left in lefts] + [near_spec, far_spec],
         [spec, spec],
         [shape, shape],
         [pltpu.VMEM((length, total_width), jnp.bfloat16)],
         after=after,
-    )(places, *lefts, *[near for near, _ in parts], *[far for _, far in parts])
+    )(places, *lefts, *parts)
 
 
 def turn(source_ref, first, columns, target_ref):
@@ -1238,25 +1247,33 @@
     def kernel(places_ref, x_ref, g_ref, *refs):
         total_ref = refs[-1]
         total_ref[...] = contract(x_ref[...], g_ref[...])
-        for side in range(2):
-            for r in range(blocks):
-                place = places_ref[1 + count + side * blocks + r]
-                start = pl.multiple_of(place * size, size)
-                refs[side][r] = total_ref[pl.ds(start, size)].astype(jnp.bfloat16)
+        halves = 1 if stacked else 2
+        for half in range(halves):
+
+            @pl.when(pl.program_id(0) // 2 == half if halves > 1 else pl.program_id(0) >= 0)
+            def _():
+                for side in range(2):
+                    for r in range(blocks):
+                        place = places_ref[1 + count + side * blocks + r]
+                        start = pl.multiple_of(place * size, size)
+                        block = total_ref[pl.ds(start, size)].astype(jnp.bfloat16)
+                        refs[side * halves + half][r] = block
 
     block = (blocks, size, tile)
     if stacked:
-        spec = pl.BlockSpec(block, lambda n, _: (0, n, 0))
-        shape = sds((blocks, 4 * size, tile), jnp.bfloat16)
+        specs = [pl.BlockSpec(block, lambda n, _: (0, n, 0))] * 2
+        shapes = [sds((blocks, 4 * size, tile), jnp.bfloat16)] * 2
     else:
-        spec = pl.BlockSpec(block, lambda n, _: (0, 0, n))
-        shape = sds((blocks, size, D), jnp.bfloat16)
+        first = pl.BlockSpec(block, lambda n, _: (0, 0, jnp.minimum(n, 1)))
+        second = pl.BlockSpec(block, lambda n, _: (0, 0, jnp.maximum(n - 2, 0)))
+        specs = [first, second] * 2
+        shapes = [sds((blocks, size, D // 2), jnp.bfloat16)] * 4
     return call(
         kernel,
         (4,),
         [whole(left), pl.BlockSpec((length, tile), lambda n, _: (0, n))],
-        [spec, spec],
-        [shape, shape],
+        specs,
+        shapes,
         [pltpu.VMEM((width, tile), jnp.float32)],
         after=after,
     )(places, left, right)
@@ -1318,20 +1335,26 @@
 
     def reversed_bits(value):
         return sum(
-            jnp.where((value >> i) & 1, count >> (i + 1), 0) for i in range(count.bit_length() - 1)
+            ((value >> i) & 1) * (count >> (i + 1)) for i in range(count.bit_length() - 1)
         )
 
-    row_places = [reversed_bits(b ^ ctx) for b in range(count)]
     shard_of = [(r % line) * 2 + (side ^ (r // line)) for r in range(shards)]
-    places = jnp.stack([jnp.asarray(i, jnp.int32) for i in [ctx] + row_places + shard_of])
+    index = jnp.arange(1 + count + shards, dtype=jnp.int32)
+    r = jnp.maximum(index - 1 - count, 0)
+    places = jnp.where(
+        index <= count,
+        reversed_bits(jnp.clip(index - 1, 0, count - 1) ^ ctx),
+        lax.rem(r, line) * 2 + (side ^ lax.div(r, line)),
+    )
+    places = jnp.where(index == 0, ctx, places).astype(jnp.int32)
 
     small = jnp.concatenate([ln1_gain, ln1_bias, ln2_gain, ln2_bias, b_qkv])
     pad = 16
-    q_mine = take_columns(places, w_qkv, count, shards, 3, 0, line, pad)
-    lines = -(-small.shape[0] // width)
-    lead = jnp.pad(small, (0, pad * width - small.shape[0])).reshape(1, pad, width)
-    q_mine = lax.dynamic_update_slice(
-        q_mine, jnp.broadcast_to(lead, (line, pad, width)), (0, depth, 0)
+    qkv_mine = take_columns(places, w_qkv, count, shards, 3, line, pad)
+    lead = jnp.pad(small, (0, 2 * 3 * width - small.shape[0])).reshape(1, 2, 3 * width)
+    lead = jnp.pad(lead, ((0, 0), (0, pad - 2), (0, 0)))
+    qkv_mine = lax.dynamic_update_slice(
+        qkv_mine, jnp.broadcast_to(lead, (line, pad, 3 * width)), (0, depth, 0)
     )
 
     def weight(blocks):
@@ -1346,19 +1369,10 @@
     cot_rows = jnp.concatenate(
         rows_gather(hold(places, cotangent[0], token_rows)), axis=0
     )
-    q_parts = weight(q_mine)
-    k_mine = take_columns(
-        places, w_qkv, count, shards, 3, 1, line, 0, q_parts[:1]
-    )
-    k_parts = weight(k_mine)
-    gate_mine = take_pairs(places, w_gate_up, count, shards, (k_parts[0], token_rows))
+    qkv_parts = weight(qkv_mine)
+    gate_mine = take_pairs(places, w_gate_up, count, shards, (qkv_parts[0], token_rows))
     gate_up = lax.all_gather(gate_mine, ("dp", "fsdp"), axis=0, tiled=True)
-    v_mine = take_columns(
-        places, w_qkv, count, shards, 3, 2, line, 0, (k_parts[0], q_parts[1], token_rows)
-    )
-    v_parts = weight(v_mine)
-    qkv_parts = [q_parts, k_parts, v_parts]
-    out_parts = weight(row_copies(w_out, v_parts[0], k_parts[1], cot_rows))
+    out_parts = weight(row_copies(w_out, qkv_parts[0], cot_rows))
     seg_row = lax.all_gather(segment_ids, "ctx", axis=1, tiled=True)
     seg_col = seg_row.reshape(length, 1)
 
@@ -1372,7 +1386,7 @@
         for parts in ([cosine, cosine, flat + 1.0], [-sine, zero, flat], [zero, sine, flat])
     ]
 
-    small_rows = [part[:, depth : depth + lines] for part in qkv_parts[0]]
+    small_rows = [part[:, depth : depth + 2] for part in qkv_parts]
     small_all = jnp.concatenate(small_rows, axis=0).reshape(shards, -1)[:, : small.shape[0]]
     small_all = small_all.astype(jnp.float32)
     small_plain = sum(
@@ -1386,16 +1400,29 @@
 
     normed_one = norm_tokens(places, token_rows, gain_one, bias_one, count, (seg_row,))
     qkv = []
-    for i, parts in enumerate(qkv_parts):
+    for i in range(3):
         turns = tables if i < 2 else []
-        qkv.append(project(places, normed_one, *parts, bias_mine[i], turns, qkv[-1:]))
-    down_near = to_line(row_copies(w_down, out_parts[0], qkv[2]))
+        qkv.append(
+            project(places, normed_one, *qkv_parts, i, bias_mine[i], turns, qkv[-1:])
+        )
+    down_copies = row_copies(w_down, out_parts[0])
+    size = down_copies.shape[1]
+    down_left = to_line(down_copies[..., : D // 2])
+    down_right = to_line(hold(places, down_copies[..., D // 2 :], down_left))
     attended, logs = attend(places, qkv, seg_col, seg_row, count, heads)
-    pieces = rows_scatter(places, *row_product(places, attended, *out_parts, count))
+    product = row_product(places, attended, out_parts, count)
+    pieces = rows_scatter(places, *product)
     hidden, normed_two = norm_hidden(places, tokens[0], pieces, gain_two, bias_two)
-    down_near = hold(places, down_near, hidden)
-    down_parts = (down_near, swap(down_near, "fsdp", 1))
-    normed_two, both, activ = gate_product(places, rows_gather(normed_two), gate_up)
+    normed_pieces = rows_gather(normed_two)
+    down_left = hold(places, down_left, product[0])
+    down_right = hold(places, down_right, normed_pieces[1])
+    down_parts = (
+        down_left,
+        down_right,
+        swap(down_left, "fsdp", 1),
+        swap(down_right, "fsdp", 1),
+    )
+    normed_two, both, activ = gate_product(places, normed_pieces, gate_up)
 
     def line_sum(blocks, after=()):
         arrived = to_line(blocks).reshape(line, -1, blocks.shape[-1])
@@ -1404,32 +1431,50 @@
     def both_sides(kept, arrived):
         return (kept.astype(jnp.float32) + arrived.astype(jnp.float32)).astype(jnp.bfloat16)
 
-    down_keep, down_load = row_grad(
-        places, activ, cot_rows, down_parts[0].shape[1], count, False
-    )
-    down_arrived = swap(down_load, "fsdp", 1)
-    grad_both = gate_back(places, cot_rows, *down_parts, both, count, (down_load,))
+    keep_left, keep_right, load_left, load_right = row_grad(
+        places, activ, cot_rows, size, count, False
+    )
+    left_arrived = swap(load_left, "fsdp", 1)
+    right_arrived = swap(load_right, "fsdp", 1)
+    grad_both = gate_back(places, cot_rows, down_parts, both, count, (load_right,))
     gate_part = pairs_grad(places, normed_two, grad_both)
     gate_grad = lax.psum_scatter(gate_part, ("dp", "fsdp"), scatter_dimension=0, tiled=True)
     pieces = rows_scatter(places, *normed_grad(places, grad_both, gate_up, (gate_part,)))
-    down_total = both_sides(down_keep, hold(places, down_arrived, pieces[1]))
-    down_pieces = row_product(places, activ, *down_parts, count, (down_total,))
+    down_pieces = row_product(places, activ, down_parts, count, (pieces[1],))
+    left_total = both_sides(keep_left, hold(places, left_arrived, pieces[1]))
     grad_hidden, grad_branch, sums_two = norm_back(
-        places, hidden, pieces, gain_two, cotangent[0], 0, True, (down_pieces[0],)
+        places, hidden, pieces, gain_two, cotangent[0], 0, True, (down_pieces[0], left_total,)
     )
     down_pieces = rows_scatter(places, *down_pieces, (grad_branch,))
-    grad_attended, grad_branch = grad_out(places, rows_gather(grad_branch), *out_parts, count)
-    out_keep, out_load = row_grad(places, attended, grad_branch, out_parts[0].shape[1], count, True)
+    branch_pieces = rows_gather(grad_branch)
+    down_total = both_sides(keep_right, hold(places, right_arrived, branch_pieces[1]))
+    grad_attended, grad_branch = grad_out(
+        places, branch_pieces, *out_parts, count, ( down_total,)
+    )
+    out_keep, out_load = row_grad(
+        places, attended, grad_branch, out_parts[0].shape[1], count, True, ()
+    )
     out_arrived = swap(out_load, "fsdp", 1)
     grads = attend_back(
-        places, qkv, grad_attended, logs, seg_col, seg_row, tables, count, heads, (out_load,)
+        places,
+        qkv,
+        grad_attended,
+        logs,
+        seg_col,
+        seg_row,
+        tables,
+        count,
+        heads,
+        (out_load, down_pieces[-1]),
     )
     grads, bias_sums = grads[:3], grads[3]
-    *loads, turned = column_loads(places, normed_one, grads)
+    out_total = both_sides(out_keep, out_arrived)
+    *loads, turned = column_loads(places, normed_one, grads, ())
     arrivals = [swap(load, "fsdp", 1) for load in loads]
     mixed = hidden + sum(piece[:rows].astype(jnp.float32) for piece in down_pieces)
     mixed = mixed.astype(jnp.bfloat16)
-    down_grad = line_sum(down_total, (loads[2],))
+    left_grad = line_sum(left_total, (loads[2],))
+    down_grad = jnp.concatenate([left_grad, line_sum(down_total, (loads[2],))], axis=1)
 
     def ctx_rows(block):
         return lax.all_gather(block, "ctx", axis=0, tiled=True)
@@ -1438,21 +1483,22 @@
         total = column_keep(places, turned, grads[i], arrivals[i], after)
         return total.reshape(line, depth, width)
 
-    out_total = both_sides(out_keep, out_arrived)
     totals = [jnp.concatenate([keep(0, down_grad), out_total], axis=1)]
     near, far = normed_grad_parts(places, grads, qkv_parts, count, (totals[0],))
-    gate_out = spread_pairs(places, ctx_rows(gate_grad), count, shards)
-    down_out = ctx_rows(down_grad).astype(jnp.float32)
+    gate_grad = hold(places, gate_grad, loads[0])
+    gate_rows = ctx_rows(gate_grad)
+    gate_out = spread_pairs(places, gate_rows, count, shards)
+    down_out = ctx_rows(hold(places, down_grad, totals[0])).astype(jnp.float32)
     totals.append(keep(1, gate_out))
-    pieces = rows_scatter(places, near, far, (totals[1],))
+    pieces = rows_scatter(places, near, far, (totals[0],))
     q_sum = line_sum(totals[0], (mixed,))
     totals.append(keep(2, down_out))
     input_grad, sums_one = norm_back(
-        places, tokens[0], pieces, gain_one, grad_hidden, 1 + count, False, (totals[2],)
+        places, tokens[0], pieces, gain_one, grad_hidden, 1 + count, False, ()
     )
     out_out = ctx_rows(q_sum[depth:]).reshape(count, 4, -1, D // 4)
     out_out = out_out.transpose(0, 2, 1, 3).reshape(-1, D).astype(jnp.float32)
-    sums = [q_sum[:depth], line_sum(totals[1]), line_sum(totals[2], (out_out,))]
+    sums = [q_sum[:depth], line_sum(totals[1], ()), line_sum(totals[2], (out_out, down_out, gate_out))]
     qkv_grads = [rows_gather(total) for total in sums]
     qkv_out = spread_columns(places, qkv_grads, count, shards)
 

time: 880 us -> 820 us (0.932)
  waiting for transfers between devices: 400 us -> 349 us
  Pallas kernels: 266 us -> 281 us
  local copies, waits for them, and re-layouts: 78.3 us -> 66.4 us
    ppermute x45, waiting for transfers between devices: 296 us -> 202 us  [swap(): return lax.ppermute(block, axis, [(i, i ^ bit) for i in range(count)])]
    all_to_all x9, waiting for transfers between devices: 100 us -> 139 us  [to_line(): return lax.all_to_all(blocks, 'dp', split_axis=0, concat_axis=0)]
    pallas_call x42 -> x46, Pallas kernels: 266 us -> 281 us  [call(): return lambda *operands: run(*operands, *after)]
    unnamed x201 -> x191, local copies, waits for them, and re-layouts: 66 us -> 52 us
    ppermute x45, starting transfers between devices: 42.3 us -> 30.5 us  [swap(): return lax.ppermute(block, axis, [(i, i ^ bit) for i in range(count)])]
  transfers between devices with their start and end apart: 59 -> 59, of which waited for: 32 -> 29; matrix products, arithmetic and copies ran while one was open for 4% -> 4% of each run, Pallas kernels for 25% -> 28%
where the time goes in v4:
time: 820 us; the launch traced here: 813 us
  waiting for transfers between devices  349 us (43%)
  Pallas kernels  281 us (34%)
  starting transfers between devices  77.6 us (9%)
  local copies, waits for them, and re-layouts  66.4 us (8%)
  other arithmetic  19.2 us (2%)
  between operations  15.1 us (2%)
    pallas_call x46, Pallas kernels, call(): return lambda *operands: run(*operands, *after)  281 us
    ppermute x45, waiting for transfers between devices, swap(): return lax.ppermute(block, axis, [(i, i ^ bit) for i in range(count)])  202 us
    all_to_all x9, waiting for transfers between devices, to_line(): return lax.all_to_all(blocks, 'dp', split_axis=0, concat_axis=0)  139 us
    unnamed x191, local copies, waits for them, and re-layouts  52 us
    all_to_all x9, starting transfers between devices, to_line(): return lax.all_to_all(blocks, 'dp', split_axis=0, concat_axis=0)  46.4 us
    ppermute x45, starting transfers between devices, swap(): return lax.ppermute(block, axis, [(i, i ^ bit) for i in range(count)])  30.5 us
  transfers between devices with their start and end apart: 59, of which 29 were waited for; matrix products, arithmetic and copies ran while one was open for 4% of the time, Pallas kernels for 28%

profile of v4, /device:TPU:0, one launch (start us, length us, event | category | flops | bytes accessed | tf_op | source)
XLA Modules:
  0.0 813.2 jit_solution(401595192323307295)
XLA Ops:
  19.8 6.3 all-to-all-start
  27.7 23.3 %collective-permute-done = bf16[256,2048]{1,0:T(8,128)(2,1)S(1)} collective-permute-done((bf16[256,2048]{1,0:T(8,128)(2,1)}, bf16[256,2048]{1,0:T(8,128)(2,1)S(1)}, u32[]{:S(2)}, u32[]{:S(2)}) %collective-permute-start) | collective-permute-done | bytes 1048608 | tf_op jit(solution)/shard_map/ppermute | solution.py:24
  57.0 44.2 %all-to-all-done.refs_1_.refs_2_.refs_3_ = bf16[4,272,1536]{2,1,0:T(8,128)(2,1)} async-done(((bf16[4,272,1536]{2,1,0:T(8,128)(2,1)}), bf16[4,272,1536]{2,1,0:T(8,128)(2,1)}, u32[]{:S(2)}, u32[]{:S(2)}) %all-to-all-start) | async-done | bytes 3342368 | tf_op jit(solution)/shard_map/all_to_all | solution.py:1283
  114.7 21.2 %collective-permute-done.4 = bf16[256,2048]{1,0:T(8,128)(2,1)} collective-permute-done((bf16[256,2048]{1,0:T(8,128)(2,1)}, bf16[256,2048]{1,0:T(8,128)(2,1)}, u32[]{:S(2)}, u32[]{:S(2)}) %collective-permute-start.4) | collective-permute-done | bytes 1048608 | tf_op jit(solution)/shard_map/ppermute | solution.py:24
  155.6 38.4 %all-to-all-done.1.refs_1_.refs_4_ = bf16[4,64,2048]{2,1,0:T(8,128)(2,1)} async-done(((bf16[4,64,2048]{2,1,0:T(8,128)(2,1)}), bf16[4,64,2048]{2,1,0:T(8,128)(2,1)}, u32[]{:S(2)}, u32[]{:S(2)}) %all-to-all-start.1) | async-done | bytes 1048608 | tf_op jit(solution)/shard_map/all_to_all | solution.py:1283
  209.6 7.3 shard_map.231.refs_0_
  219.1 6.4 shard_map.232.refs_7_.refs_0_
  228.0 6.4 shard_map.233.refs_4_.refs_1_
  243.4 17.4 %shard_map.235 = (bf16[1024,512]{1,0:T(8,128)(2,1)S(1)}, f32[4,2,1024]{2,1,0:T(2,128)S(1)}) custom-call(s32[13]{0:T(128)S(1)} %compare_select_fusion.1.places_ref, bf16[1024,512]{1,0:T(8,128)(2,1)S(1)} %copy-done.14, bf16[1024,512]{1,0:T(8,128)(2,1)S(1)} %copy-done.16, bf16[1024,512]{1,0:T(8,128)(2,1)S(1)} %shard_map.234.refs_2_, s32[1024,1]{1,0:T(8,128)S(1)} %copy-done.49, ...), custom_call_target="tpu_custom_call" | custom-call | flops 1 | bytes 1 | tf_op jit(solution)/shard_map/pallas_call | solution.py:381
  268.2 8.3 %all-to-all-done.2.refs_0_.refs_1_ = bf16[4,176,1024]{2,1,0:T(8,128)(2,1)} async-done(((bf16[4,176,1024]{2,1,0:T(8,128)(2,1)}), bf16[4,176,1024]{2,1,0:T(8,128)(2,1)}, u32[]{:S(2)}, u32[]{:S(2)}) %all-to-all-start.2) | async-done | bytes 1441824 | tf_op jit(solution)/shard_map/all_to_all | solution.py:1283
  278.4 6.7 all-to-all-start.3
  288.1 21.9 %collective-permute-done.9.refs_3_ = bf16[256,2048]{1,0:T(8,128)(2,1)S(1)} collective-permute-done((bf16[256,2048]{1,0:T(8,128)(2,1)S(1)}, bf16[256,2048]{1,0:T(8,128)(2,1)S(1)}, u32[]{:S(2)}, u32[]{:S(2)}) %collective-permute-start.9) | collective-permute-done | bytes 1048608 | tf_op jit(solution)/shard_map/ppermute | solution.py:24
  317.6 30.4 %all-to-all-done.3.refs_0_ = bf16[4,176,1024]{2,1,0:T(8,128)(2,1)} async-done(((bf16[4,176,1024]{2,1,0:T(8,128)(2,1)}), bf16[4,176,1024]{2,1,0:T(8,128)(2,1)}, u32[]{:S(2)}, u32[]{:S(2)}) %all-to-all-start.3) | async-done | bytes 1441824 | tf_op jit(solution)/shard_map/all_to_all | solution.py:1283
  354.9 19.8 %shard_map.242 = (bf16[1024,2048]{1,0:T(8,128)(2,1)}, bf16[1024,2816]{1,0:T(8,128)(2,1)}, bf16[1024,1408]{1,0:T(8,128)(2,1)}) custom-call(s32[13]{0:T(128)} %copy-done.66, bf16[256,2048]{1,0:T(8,128)(2,1)} %get-tuple-element.51.refs_0_, bf16[256,2048]{1,0:T(8,128)(2,1)} %collective-permute-done.10.refs_1_, bf16[256,2048]{1,0:T(8,128)(2,1)} %copy-done.85, ...), custom_call_target="tpu_custom_call" | custom-call | flops 1 | bytes 1 | tf_op jit(solution)/shard_map/pallas_call | solution.py:381
  374.7 10.7 %shard_map.247 = (bf16[4,176,1024]{2,1,0:T(8,128)(2,1)S(1)}, bf16[4,176,1024]{2,1,0:T(8,128)(2,1)S(1)}, bf16[4,176,1024]{2,1,0:T(8,128)(2,1)S(1)}, bf16[4,176,1024]{2,1,0:T(8,128)(2,1)S(1)}) custom-call(s32[13]{0:T(128)S(1)} %copy-done.67, bf16[1024,1408]{1,0:T(8,128)(2,1)} %get-tuple-element.52.refs_0_, bf16[1024,2048]{1,0:T(8,128)(2,1)} %copy-done.3), custom_call_target="tpu_custom_call" | custom-call | flops 1 | bytes 1 | tf_op jit(solution)/shard_map/pallas_call | solution.py:381
  387.6 16.7 %shard_map.248.refs_1_.refs_0_ = bf16[1024,2816]{1,0:T(8,128)(2,1)} custom-call(s32[13]{0:T(128)} %copy-done.66, bf16[1024,2048]{1,0:T(8,128)(2,1)} %copy-done.3, bf16[1024,2816]{1,0:T(8,128)(2,1)} %get-tuple-element.53.refs_1_, bf16[4,176,1024]{2,1,0:T(8,128)(2,1)} %shard_map.244.refs_2_.refs_1_, bf16[4,176,1024]{2,1,0:T(8,128)(2,1)} %shard_map.246.refs_3_.refs_2_, ...), custom_call_target="tpu_custom_call" | custom-call | flops 1 | bytes 1 | tf_op jit(solution)/shard_map/pallas_call | solution.py:381
  404.4 18.4 %shard_map.249.refs_2_ = bf16[2048,2816]{1,0:T(8,128)(2,1)} custom-call(s32[13]{0:T(128)S(1)} %copy-done.68, bf16[1024,2048]{1,0:T(8,128)(2,1)S(1)} %copy-done.55, bf16[1024,2816]{1,0:T(8,128)(2,1)} %shard_map.248.refs_1_.refs_0_), custom_call_target="tpu_custom_call" | custom-call | flops 1 | bytes 1 | tf_op jit(solution)/shard_map/pallas_call | solution.py:381
  422.9 18.2 %shard_map.250 = (bf16[512,2048]{1,0:T(8,128)(2,1)}, bf16[512,2048]{1,0:T(8,128)(2,1)}) custom-call(s32[13]{0:T(128)} %copy-done.66, bf16[1024,2816]{1,0:T(8,128)(2,1)} %shard_map.248.refs_1_.refs_0_, bf16[2048,2816]{1,0:T(8,128)(2,1)} %all-gather.5.cloned.1.call-done.refs_4_.refs_1_, bf16[2048,2816]{1,0:T(8,128)(2,1)} %shard_map.249.refs_2_), custom_call_target="tpu_custom_call" | custom-call | flops 1 | bytes 1 | tf_op jit(solution)/shard_map/pallas_call | solution.py:381
  451.6 33.8 %collective-permute-done.18.refs_0_ = bf16[4,176,1024]{2,1,0:T(8,128)(2,1)S(1)} collective-permute-done((bf16[4,176,1024]{2,1,0:T(8,128)(2,1)S(1)}, bf16[4,176,1024]{2,1,0:T(8,128)(2,1)S(1)}, u32[]{:S(2)}, u32[]{:S(2)}) %collective-permute-start.18) | collective-permute-done | bytes 1441824 | tf_op jit(solution)/shard_map/ppermute | solution.py:24
  487.7 6.1 all-to-all-start.4
  493.8 12.8 %shard_map.251 = (bf16[512,2048]{1,0:T(8,128)(2,1)}, bf16[512,2048]{1,0:T(8,128)(2,1)}) custom-call(s32[13]{0:T(128)S(1)} %copy-done.69, bf16[1024,1408]{1,0:T(8,128)(2,1)} %get-tuple-element.52.refs_0_, bf16[4,176,1024]{2,1,0:T(8,128)(2,1)} %shard_map.244.refs_2_.refs_1_, bf16[4,176,1024]{2,1,0:T(8,128)(2,1)} %shard_map.246.refs_3_.refs_2_, ...), custom_call_target="tpu_custom_call" | custom-call | flops 1 | bytes 1 | tf_op jit(solution)/shard_map/pallas_call | solution.py:381
  507.7 6.9 shard_map.254
  515.7 24.4 %collective-permute-done.20.refs_1_ = bf16[256,2048]{1,0:T(8,128)(2,1)} collective-permute-done((bf16[256,2048]{1,0:T(8,128)(2,1)}, bf16[256,2048]{1,0:T(8,128)(2,1)}, u32[]{:S(2)}, u32[]{:S(2)}) %collective-permute-start.20) | collective-permute-done | bytes 1048608 | tf_op jit(solution)/shard_map/ppermute | solution.py:24
  545.4 11.9 %all-to-all-done.4.refs_0_.refs_1_.refs_2_.refs_3_ = bf16[4,176,1024]{2,1,0:T(8,128)(2,1)} async-done(((bf16[4,176,1024]{2,1,0:T(8,128)(2,1)}), bf16[4,176,1024]{2,1,0:T(8,128)(2,1)}, u32[]{:S(2)}, u32[]{:S(2)}) %all-to-all-start.4) | async-done | bytes 1441824 | tf_op jit(solution)/shard_map/all_to_all | solution.py:1283
  566.4 8.3 %shard_map.257 = (bf16[1024,512]{1,0:T(8,128)(2,1)S(1)}, bf16[1024,2048]{1,0:T(8,128)(2,1)}) custom-call(s32[13]{0:T(128)S(1)} %copy-done.69, bf16[256,2048]{1,0:T(8,128)(2,1)} %get-tuple-element.62.refs_2_.refs_0_, bf16[256,2048]{1,0:T(8,128)(2,1)} %collective-permute-done.20.refs_1_, bf16[256,2048]{1,0:T(8,128)(2,1)} %collective-permute-done.21.refs_2_, ...), custom_call_target="tpu_custom_call" | custom-call | flops 1 | bytes 1 | tf_op jit(solution)/shard_map/pallas_call | solution.py:381
  582.7 7.4 collective-permute-done.19.refs_11_
  591.1 21.7 %shard_map.259 = (bf16[1024,512]{1,0:T(8,128)(2,1)S(1)}, bf16[1024,512]{1,0:T(8,128)(2,1)S(1)}, bf16[1024,512]{1,0:T(8,128)(2,1)S(1)}, f32[3,1,512]{2,1,0:T(1,128)S(1)}) custom-call(s32[13]{0:T(128)S(1)} %copy-done.69, bf16[1024,512]{1,0:T(8,128)(2,1)} %copy-done.13, bf16[1024,512]{1,0:T(8,128)(2,1)} %copy-done.15, bf16[1024,512]{1,0:T(8,128)(2,1)} %copy-done.29, ...), custom_call_target="tpu_custom_call" | custom-call | flops 1 | bytes 1 | tf_op jit(solution)/shard_map/pallas_call | solution.py:381
  613.9 9.1 %shard_map.260 = (bf16[1024,512]{1,0:T(8,128)(2,1)}, bf16[1024,512]{1,0:T(8,128)(2,1)S(1)}, bf16[1024,512]{1,0:T(8,128)(2,1)}, bf16[1024,1024]{1,0:T(8,128)(2,1)}) custom-call(s32[13]{0:T(128)S(1)} %copy-done.69, bf16[1024,2048]{1,0:T(8,128)(2,1)} %copy-done.2, bf16[1024,512]{1,0:T(8,128)(2,1)S(1)} %get-tuple-element.69.refs_1_.refs_0_, ...), custom_call_target="tpu_custom_call" | custom-call | flops 1 | bytes 1 | tf_op jit(solution)/shard_map/pallas_call | solution.py:381
  630.0 17.8 %collective-permute-done.24.refs_2_ = bf16[1024,512]{1,0:T(8,128)(2,1)} collective-permute-done((bf16[1024,512]{1,0:T(8,128)(2,1)}, bf16[1024,512]{1,0:T(8,128)(2,1)}, u32[]{:S(2)}, u32[]{:S(2)}) %collective-permute-start.24) | collective-permute-done | bytes 1048608 | tf_op jit(solution)/shard_map/ppermute | solution.py:24
  661.7 11.9 %shard_map.264 = (bf16[512,2048]{1,0:T(8,128)(2,1)S(1)}, bf16[512,2048]{1,0:T(8,128)(2,1)}) custom-call(s32[13]{0:T(128)S(1)} %copy-done.69, bf16[1024,512]{1,0:T(8,128)(2,1)S(1)} %copy-done.28, bf16[1024,512]{1,0:T(8,128)(2,1)S(1)} %copy-done.24, bf16[1024,512]{1,0:T(8,128)(2,1)S(1)} %copy-done.31, ...), custom_call_target="tpu_custom_call" | custom-call | flops 1 | bytes 1 | tf_op jit(solution)/shard_map/pallas_call | solution.py:381
  685.9 15.0 %collective-permute-done.41.refs_2_ = bf16[1024,512]{1,0:T(8,128)(2,1)} collective-permute-done((bf16[1024,512]{1,0:T(8,128)(2,1)}, bf16[1024,512]{1,0:T(8,128)(2,1)}, u32[]{:S(2)}, u32[]{:S(2)}) %collective-permute-start.41) | collective-permute-done | bytes 1048608 | tf_op jit(solution)/shard_map/ppermute | solution.py:24
  731.0 7.7 shard_map.269.refs_3_.refs_6_
  (394 shorter events, 281.3 us)
Async XLA Ops:
  19.8 81.3 %all-to-all-start = ((bf16[4,272,1536]{2,1,0:T(8,128)(2,1)}), bf16[4,272,1536]{2,1,0:T(8,128)(2,1)}, u32[]{:S(2)}, u32[]{:S(2)}) async-start(bf16[4,272,1536]{2,1,0:T(8,128)(2,1)} %broadcast_dynamic-update-slice_fusion), calls=%async_computation | async-start | bytes 6684672 | tf_op jit(solution)/shard_map/all_to_all | solution.py:1283
  26.2 328.1 %all-gather.5.cloned.1.call-start = ((), (), s32[]{:S(2)}) async-start(), calls=%async_computation.10 | async-start | bytes 12976128 | tf_op jit(solution)/shard_map/all_gather | solution.py:1374
  113.2 95.1 %collective-permute-start.3 = (bf16[4,272,1536]{2,1,0:T(8,128)(2,1)}, bf16[4,272,1536]{2,1,0:T(8,128)(2,1)}, u32[]{:S(2)}, u32[]{:S(2)}) collective-permute-start(bf16[4,272,1536]{2,1,0:T(8,128)(2,1)} %all-to-all-done.refs_1_.refs_2_.refs_3_), channel_id=1, source_target_pairs={{0,1},{1,0},{2,3},{3,2},{4,5},{5,4},{6,7},{7,6},{8,9},{9,8},{10,11... | collective-permute-start | bytes 10027016 | tf_op jit(solution)/shard_map/ppermute | solution.py:24
  144.4 49.7 %all-to-all-start.1 = ((bf16[4,64,2048]{2,1,0:T(8,128)(2,1)}), bf16[4,64,2048]{2,1,0:T(8,128)(2,1)}, u32[]{:S(2)}, u32[]{:S(2)}) async-start(bf16[4,64,2048]{2,1,0:T(8,128)(2,1)} %broadcast_in_dim.65), calls=%async_computation.1 | async-start | bytes 2097152 | tf_op jit(solution)/shard_map/all_to_all | solution.py:1283
  197.8 78.8 %all-to-all-start.2 = ((bf16[4,176,1024]{2,1,0:T(8,128)(2,1)}), bf16[4,176,1024]{2,1,0:T(8,128)(2,1)}, u32[]{:S(2)}, u32[]{:S(2)}) async-start(bf16[4,176,1024]{2,1,0:T(8,128)(2,1)} %broadcast_in_dim.66), calls=%async_computation.2 | async-start | bytes 2883584 | tf_op jit(solution)/shard_map/all_to_all | solution.py:1283
  202.6 58.2 %collective-permute-start.7 = (bf16[4,64,2048]{2,1,0:T(8,128)(2,1)}, bf16[4,64,2048]{2,1,0:T(8,128)(2,1)}, u32[]{:S(2)}, u32[]{:S(2)}) collective-permute-start(bf16[4,64,2048]{2,1,0:T(8,128)(2,1)} %all-to-all-done.1.refs_1_.refs_4_), channel_id=1, source_target_pairs={{0,1},{1,0},{2,3},{3,2},{4,5},{5,4},{6,7},{7,6},{8,9},{9,8},{10,11... | collective-permute-start | bytes 3145736 | tf_op jit(solution)/shard_map/ppermute | solution.py:24
  278.4 69.7 %all-to-all-start.3 = ((bf16[4,176,1024]{2,1,0:T(8,128)(2,1)}), bf16[4,176,1024]{2,1,0:T(8,128)(2,1)}, u32[]{:S(2)}, u32[]{:S(2)}) async-start(bf16[4,176,1024]{2,1,0:T(8,128)(2,1)} %copy-done.19), calls=%async_computation.3 | async-start | bytes 2883584 | tf_op jit(solution)/shard_map/all_to_all | solution.py:1283
  285.0 367.9 %reduce-scatter.2.cloned.1.call-start = ((), (), s32[]{:S(2)}) async-start(), calls=%async_computation.11 | async-start | bytes 12976128 | tf_op jit(solution)/shard_map/reduce_scatter | solution.py:1441
  314.8 33.3 %collective-permute-start.10 = (bf16[256,2048]{1,0:T(8,128)(2,1)}, bf16[256,2048]{1,0:T(8,128)(2,1)}, u32[]{:S(2)}, u32[]{:S(2)}) collective-permute-start(bf16[256,2048]{1,0:T(8,128)(2,1)} %get-tuple-element.51.refs_0_), channel_id=1, source_target_pairs={{0,4},{2,6},{4,0},{6,2},{1,5},{3,7},{5,1},{7,3},{8,12},{10,14},{12... | collective-permute-start | bytes 3145736 | tf_op jit(solution)/shard_map/ppermute | solution.py:24
  317.0 70.7 %collective-permute-start.13 = (bf16[4,176,1024]{2,1,0:T(8,128)(2,1)}, bf16[4,176,1024]{2,1,0:T(8,128)(2,1)}, u32[]{:S(2)}, u32[]{:S(2)}) collective-permute-start(bf16[4,176,1024]{2,1,0:T(8,128)(2,1)} %shard_map.244.refs_2_.refs_1_), channel_id=1, source_target_pairs={{0,1},{1,0},{2,3},{3,2},{4,5},{5,4},{6,7},{7,6},{8,9},{9,8},{10,11... | collective-permute-start | bytes 4325384 | tf_op jit(solution)/shard_map/ppermute | solution.py:24
  348.7 39.0 %collective-permute-start.14 = (bf16[4,176,1024]{2,1,0:T(8,128)(2,1)}, bf16[4,176,1024]{2,1,0:T(8,128)(2,1)}, u32[]{:S(2)}, u32[]{:S(2)}) collective-permute-start(bf16[4,176,1024]{2,1,0:T(8,128)(2,1)} %shard_map.246.refs_3_.refs_2_), channel_id=1, source_target_pairs={{0,1},{1,0},{2,3},{3,2},{4,5},{5,4},{6,7},{7,6},{8,9},{9,8},{10,11... | collective-permute-start | bytes 4325384 | tf_op jit(solution)/shard_map/ppermute | solution.py:24
  441.2 44.1 %collective-permute-start.18 = (bf16[4,176,1024]{2,1,0:T(8,128)(2,1)S(1)}, bf16[4,176,1024]{2,1,0:T(8,128)(2,1)S(1)}, u32[]{:S(2)}, u32[]{:S(2)}) collective-permute-start(bf16[4,176,1024]{2,1,0:T(8,128)(2,1)S(1)} %copy-done.79), channel_id=1, source_target_pairs={{0,1},{1,0},{2,3},{3,2},{4,5},{5,4},{6,7},{7,6},{8,9},{9,8},{10,11... | collective-permute-start | bytes 4325384 | tf_op jit(solution)/shard_map/ppermute | solution.py:24
  450.1 57.7 %collective-permute-start.17 = (bf16[256,2048]{1,0:T(8,128)(2,1)}, bf16[256,2048]{1,0:T(8,128)(2,1)}, u32[]{:S(2)}, u32[]{:S(2)}) collective-permute-start(bf16[256,2048]{1,0:T(8,128)(2,1)} %shard_map.252), channel_id=1, source_target_pairs={{0,4},{2,6},{4,0},{6,2},{1,5},{3,7},{5,1},{7,3},{8,12},{10,14},{12... | collective-permute-start | bytes 3145736 | tf_op jit(solution)/shard_map/ppermute | solution.py:24
  487.7 69.6 %all-to-all-start.4 = ((bf16[4,176,1024]{2,1,0:T(8,128)(2,1)}), bf16[4,176,1024]{2,1,0:T(8,128)(2,1)}, u32[]{:S(2)}, u32[]{:S(2)}) async-start(bf16[4,176,1024]{2,1,0:T(8,128)(2,1)} %add_convert_fusion.1.refs_7_), calls=%async_computation.4 | async-start | bytes 2883584 | tf_op jit(solution)/shard_map/all_to_all | solution.py:1283
  506.6 55.5 %collective-permute-start.16 = (bf16[512,2048]{1,0:T(8,128)(2,1)}, bf16[512,2048]{1,0:T(8,128)(2,1)}, u32[]{:S(2)}, u32[]{:S(2)}) collective-permute-start(bf16[512,2048]{1,0:T(8,128)(2,1)} %get-tuple-element.58), channel_id=1, source_target_pairs={{0,2},{2,0},{4,6},{6,4},{1,3},{3,1},{5,7},{7,5},{8,10},{10,8},{12,... | collective-permute-start | bytes 6291464 | tf_op jit(solution)/shard_map/ppermute | solution.py:24
  506.6 36.4 %collective-permute-start.23 = (bf16[4,176,1024]{2,1,0:T(8,128)(2,1)S(1)}, bf16[4,176,1024]{2,1,0:T(8,128)(2,1)S(1)}, u32[]{:S(2)}, u32[]{:S(2)}) collective-permute-start(bf16[4,176,1024]{2,1,0:T(8,128)(2,1)S(1)} %copy-done.65), channel_id=1, source_target_pairs={{0,1},{1,0},{2,3},{3,2},{4,5},{5,4},{6,7},{7,6},{8,9},{9,8},{10,11... | collective-permute-start | bytes 4325384 | tf_op jit(solution)/shard_map/ppermute | solution.py:24
  515.7 50.7 %collective-permute-start.21 = (bf16[256,2048]{1,0:T(8,128)(2,1)}, bf16[256,2048]{1,0:T(8,128)(2,1)}, u32[]{:S(2)}, u32[]{:S(2)}) collective-permute-start(bf16[256,2048]{1,0:T(8,128)(2,1)} %get-tuple-element.62.refs_2_.refs_0_), channel_id=1, source_target_pairs={{0,2},{2,0},{4,6},{6,4},{1,3},{3,1},{5,7},{7,5},{8,10},{10,8},{12,... | collective-permute-start | bytes 3145736 | tf_op jit(solution)/shard_map/ppermute | solution.py:24
  540.1 26.3 %collective-permute-start.22 = (bf16[256,2048]{1,0:T(8,128)(2,1)}, bf16[256,2048]{1,0:T(8,128)(2,1)}, u32[]{:S(2)}, u32[]{:S(2)}) collective-permute-start(bf16[256,2048]{1,0:T(8,128)(2,1)} %collective-permute-done.20.refs_1_), channel_id=1, source_target_pairs={{0,2},{2,0},{4,6},{6,4},{1,3},{3,1},{5,7},{7,5},{8,10},{10,8},{12,... | collective-permute-start | bytes 3145736 | tf_op jit(solution)/shard_map/ppermute | solution.py:24
  557.3 70.5 %all-to-all-start.5 = ((bf16[4,176,1024]{2,1,0:T(8,128)(2,1)}), bf16[4,176,1024]{2,1,0:T(8,128)(2,1)}, u32[]{:S(2)}, u32[]{:S(2)}) async-start(bf16[4,176,1024]{2,1,0:T(8,128)(2,1)} %add_convert_fusion.refs_6_), calls=%async_computation.5 | async-start | bytes 2883584 | tf_op jit(solution)/shard_map/all_to_all | solution.py:1283
  561.7 118.9 %all-gather.9.cloned.1.call-start = ((), (), s32[]{:S(2)}) async-start(), calls=%async_computation.13 | async-start | bytes 3604480 | tf_op jit(solution)/shard_map/all_gather | solution.py:1480
  581.3 45.3 %collective-permute-start.25 = (bf16[4,256,512]{2,1,0:T(8,128)(2,1)S(1)}, bf16[4,256,512]{2,1,0:T(8,128)(2,1)S(1)}, u32[]{:S(2)}, u32[]{:S(2)}) collective-permute-start(bf16[4,256,512]{2,1,0:T(8,128)(2,1)S(1)} %get-tuple-element.68.refs_10_), channel_id=1, source_target_pairs={{0,1},{1,0},{2,3},{3,2},{4,5},{5,4},{6,7},{7,6},{8,9},{9,8},{10,11... | collective-permute-start | bytes 3145736 | tf_op jit(solution)/shard_map/ppermute | solution.py:24
  652.9 75.5 %all-gather.7.cloned.1.call-start = ((), (), s32[]{:S(2)}) async-start(), calls=%async_computation.12 | async-start | bytes 7208960 | tf_op jit(solution)/shard_map/all_gather | solution.py:1480
  653.5 52.7 %all-to-all-start.6 = ((bf16[4,512,512]{2,1,0:T(8,128)(2,1)}), bf16[4,512,512]{2,1,0:T(8,128)(2,1)S(1)}, u32[]{:S(2)}, u32[]{:S(2)}) async-start(bf16[4,512,512]{2,1,0:T(8,128)(2,1)} %copy-done.5), calls=%async_computation.6 | async-start | bytes 4194304 | tf_op jit(solution)/shard_map/all_to_all | solution.py:1283
  675.0 37.8 %collective-permute-start.26 = (bf16[512,2048]{1,0:T(8,128)(2,1)}, bf16[512,2048]{1,0:T(8,128)(2,1)}, u32[]{:S(2)}, u32[]{:S(2)}) collective-permute-start(bf16[512,2048]{1,0:T(8,128)(2,1)} %get-tuple-element.77), channel_id=1, source_target_pairs={{0,2},{2,0},{4,6},{6,4},{1,3},{3,1},{5,7},{7,5},{8,10},{10,8},{12,... | collective-permute-start | bytes 6291464 | tf_op jit(solution)/shard_map/ppermute | solution.py:24
  706.2 36.6 %all-to-all-start.8 = ((bf16[4,256,512]{2,1,0:T(8,128)(2,1)}), bf16[4,256,512]{2,1,0:T(8,128)(2,1)}, u32[]{:S(2)}, u32[]{:S(2)}) async-start(bf16[4,256,512]{2,1,0:T(8,128)(2,1)} %bitcast.83), calls=%async_computation.9 | async-start | bytes 2097152 | tf_op jit(solution)/shard_map/all_to_all | solution.py:1283
  711.3 49.9 %all-gather.11.cloned.1.call-start = ((), (), s32[]{:S(2)}) async-start(), calls=%async_computation.14 | async-start | bytes 1310720 | tf_op jit(solution)/shard_map/all_gather | solution.py:1480
  711.3 27.4 %collective-permute-start.37 = (bf16[1024,512]{1,0:T(8,128)(2,1)}, bf16[1024,512]{1,0:T(8,128)(2,1)}, u32[]{:S(2)}, u32[]{:S(2)}) collective-permute-start(bf16[1024,512]{1,0:T(8,128)(2,1)} %copy-done.80), channel_id=1, source_target_pairs={{0,1},{1,0},{2,3},{3,2},{4,5},{5,4},{6,7},{7,6},{8,9},{9,8},{10,11... | collective-permute-start | bytes 3145736 | tf_op jit(solution)/shard_map/ppermute | solution.py:24
  718.7 34.0 %collective-permute-start.27 = (bf16[256,2048]{1,0:T(8,128)(2,1)}, bf16[256,2048]{1,0:T(8,128)(2,1)}, u32[]{:S(2)}, u32[]{:S(2)}) collective-permute-start(bf16[256,2048]{1,0:T(8,128)(2,1)} %shard_map.265), channel_id=1, source_target_pairs={{0,4},{2,6},{4,0},{6,2},{1,5},{3,7},{5,1},{7,3},{8,12},{10,14},{12... | collective-permute-start | bytes 3145736 | tf_op jit(solution)/shard_map/ppermute | solution.py:24
  742.8 30.9 %all-to-all-start.7 = ((bf16[4,256,512]{2,1,0:T(8,128)(2,1)}), bf16[4,256,512]{2,1,0:T(8,128)(2,1)}, u32[]{:S(2)}, u32[]{:S(2)}) async-start(bf16[4,256,512]{2,1,0:T(8,128)(2,1)} %bitcast.78), calls=%async_computation.8 | async-start | bytes 2097152 | tf_op jit(solution)/shard_map/all_to_all | solution.py:1283
  747.6 46.2 %collective-permute-start.34 = (bf16[256,512]{1,0:T(8,128)(2,1)S(1)}, bf16[256,512]{1,0:T(8,128)(2,1)S(1)}, u32[]{:S(2)}, u32[]{:S(2)}) collective-permute-start(bf16[256,512]{1,0:T(8,128)(2,1)S(1)} %get-tuple-element.103.refs_0_), channel_id=1, source_target_pairs={{0,4},{2,6},{4,0},{6,2},{1,5},{3,7},{5,1},{7,3},{8,12},{10,14},{12... | collective-permute-start | bytes 786440 | tf_op jit(solution)/shard_map/ppermute | solution.py:24
  747.7 47.9 %collective-permute-start.35 = (bf16[256,512]{1,0:T(8,128)(2,1)S(1)}, bf16[256,512]{1,0:T(8,128)(2,1)}, u32[]{:S(2)}, u32[]{:S(2)}) collective-permute-start(bf16[256,512]{1,0:T(8,128)(2,1)S(1)} %get-tuple-element.103.refs_0_), channel_id=1, source_target_pairs={{0,2},{2,0},{4,6},{6,4},{1,3},{3,1},{5,7},{7,5},{8,10},{10,8},{12,... | collective-permute-start | bytes 786440 | tf_op jit(solution)/shard_map/ppermute | solution.py:24
  767.0 28.2 %collective-permute-start.42 = (bf16[256,512]{1,0:T(8,128)(2,1)S(1)}, bf16[256,512]{1,0:T(8,128)(2,1)}, u32[]{:S(2)}, u32[]{:S(2)}) collective-permute-start(bf16[256,512]{1,0:T(8,128)(2,1)S(1)} %shard_map.274.refs_8_), channel_id=1, source_target_pairs={{0,4},{2,6},{4,0},{6,2},{1,5},{3,7},{5,1},{7,3},{8,12},{10,14},{12... | collective-permute-start | bytes 786440 | tf_op jit(solution)/shard_map/ppermute | solution.py:24
  (115 other events, 1496.9 us)
Sparse Core Ops, SparseCore 0:
  106.6 247.6 all-gather.4
  423.0 223.3 reduce-scatter.1
  653.0 27.5 all-gather.8
  682.0 46.3 all-gather.6
  730.4 23.0 all-gather.10

commit v5 on v4

--- a/solution.py
+++ b/solution.py
@@ -1441,7 +1441,7 @@
     gate_grad = lax.psum_scatter(gate_part, ("dp", "fsdp"), scatter_dimension=0, tiled=True)
     pieces = rows_scatter(places, *normed_grad(places, grad_both, gate_up, (gate_part,)))
     down_pieces = row_product(places, activ, down_parts, count, (pieces[1],))
-    left_total = both_sides(keep_left, hold(places, left_arrived, pieces[1]))
+    left_total = both_sides(keep_left, hold(places, left_arrived, down_pieces[0]))
     grad_hidden, grad_branch, sums_two = norm_back(
         places, hidden, pieces, gain_two, cotangent[0], 0, True, (down_pieces[0], left_total,)
     )

time: 820 us -> 819 us (level)
    ppermute x45, waiting for transfers between devices: 202 us -> 188 us  [swap(): return lax.ppermute(block, axis, [(i, i ^ bit) for i in range(count)])]
    all_to_all x9, waiting for transfers between devices: 139 us -> 152 us  [to_line(): return lax.all_to_all(blocks, 'dp', split_axis=0, concat_axis=0)]
    unnamed x191 -> x189, local copies, waits for them, and re-layouts: 52 us -> 53.6 us
where the time goes in v5:
time: 819 us; the launch traced here: 812 us
  waiting for transfers between devices  348 us (42%)
  Pallas kernels  281 us (34%)
  starting transfers between devices  75.6 us (9%)
  local copies, waits for them, and re-layouts  68 us (8%)
  other arithmetic  19.1 us (2%)
  between operations  15.1 us (2%)
    pallas_call x46, Pallas kernels, call(): return lambda *operands: run(*operands, *after)  281 us
    ppermute x45, waiting for transfers between devices, swap(): return lax.ppermute(block, axis, [(i, i ^ bit) for i in range(count)])  188 us
    all_to_all x9, waiting for transfers between devices, to_line(): return lax.all_to_all(blocks, 'dp', split_axis=0, concat_axis=0)  152 us
    unnamed x189, local copies, waits for them, and re-layouts  53.6 us
    all_to_all x9, starting transfers between devices, to_line(): return lax.all_to_all(blocks, 'dp', split_axis=0, concat_axis=0)  46.7 us
    ppermute x45, starting transfers between devices, swap(): return lax.ppermute(block, axis, [(i, i ^ bit) for i in range(count)])  28.3 us
  transfers between devices with their start and end apart: 59, of which 29 were waited for; matrix products, arithmetic and copies ran while one was open for 4% of the time, Pallas kernels for 28%

profile of v5, /device:TPU:0, one launch (start us, length us, event | category | flops | bytes accessed | tf_op | source)
XLA Modules:
  0.0 812.2 jit_solution(1084945251331509868)
XLA Ops:
  19.8 6.3 all-to-all-start
  27.7 23.3 %collective-permute-done = bf16[256,2048]{1,0:T(8,128)(2,1)S(1)} collective-permute-done((bf16[256,2048]{1,0:T(8,128)(2,1)}, bf16[256,2048]{1,0:T(8,128)(2,1)S(1)}, u32[]{:S(2)}, u32[]{:S(2)}) %collective-permute-start) | collective-permute-done | bytes 1048608 | tf_op jit(solution)/shard_map/ppermute | solution.py:24
  57.0 44.2 %all-to-all-done.refs_1_.refs_2_.refs_3_ = bf16[4,272,1536]{2,1,0:T(8,128)(2,1)} async-done(((bf16[4,272,1536]{2,1,0:T(8,128)(2,1)}), bf16[4,272,1536]{2,1,0:T(8,128)(2,1)}, u32[]{:S(2)}, u32[]{:S(2)}) %all-to-all-start) | async-done | bytes 3342368 | tf_op jit(solution)/shard_map/all_to_all | solution.py:1283
  114.7 21.2 %collective-permute-done.4 = bf16[256,2048]{1,0:T(8,128)(2,1)} collective-permute-done((bf16[256,2048]{1,0:T(8,128)(2,1)}, bf16[256,2048]{1,0:T(8,128)(2,1)}, u32[]{:S(2)}, u32[]{:S(2)}) %collective-permute-start.4) | collective-permute-done | bytes 1048608 | tf_op jit(solution)/shard_map/ppermute | solution.py:24
  155.6 38.4 %all-to-all-done.1.refs_1_.refs_4_ = bf16[4,64,2048]{2,1,0:T(8,128)(2,1)} async-done(((bf16[4,64,2048]{2,1,0:T(8,128)(2,1)}), bf16[4,64,2048]{2,1,0:T(8,128)(2,1)}, u32[]{:S(2)}, u32[]{:S(2)}) %all-to-all-start.1) | async-done | bytes 1048608 | tf_op jit(solution)/shard_map/all_to_all | solution.py:1283
  209.6 7.3 shard_map.231.refs_0_
  219.0 6.4 shard_map.232.refs_7_.refs_0_
  227.9 6.4 shard_map.233.refs_4_.refs_1_
  243.4 17.4 %shard_map.235 = (bf16[1024,512]{1,0:T(8,128)(2,1)S(1)}, f32[4,2,1024]{2,1,0:T(2,128)S(1)}) custom-call(s32[13]{0:T(128)S(1)} %compare_select_fusion.1.places_ref, bf16[1024,512]{1,0:T(8,128)(2,1)S(1)} %copy-done.17, bf16[1024,512]{1,0:T(8,128)(2,1)S(1)} %copy-done.19, bf16[1024,512]{1,0:T(8,128)(2,1)S(1)} %shard_map.234.refs_2_, s32[1024,1]{1,0:T(8,128)S(1)} %copy-done.50, ...), custom_call_target="tpu_custom_call" | custom-call | flops 1 | bytes 1 | tf_op jit(solution)/shard_map/pallas_call | solution.py:381
  268.1 8.4 %all-to-all-done.2.refs_0_.refs_1_ = bf16[4,176,1024]{2,1,0:T(8,128)(2,1)} async-done(((bf16[4,176,1024]{2,1,0:T(8,128)(2,1)}), bf16[4,176,1024]{2,1,0:T(8,128)(2,1)}, u32[]{:S(2)}, u32[]{:S(2)}) %all-to-all-start.2) | async-done | bytes 1441824 | tf_op jit(solution)/shard_map/all_to_all | solution.py:1283
  278.4 6.7 all-to-all-start.3
  288.1 21.9 %collective-permute-done.9.refs_3_ = bf16[256,2048]{1,0:T(8,128)(2,1)S(1)} collective-permute-done((bf16[256,2048]{1,0:T(8,128)(2,1)S(1)}, bf16[256,2048]{1,0:T(8,128)(2,1)S(1)}, u32[]{:S(2)}, u32[]{:S(2)}) %collective-permute-start.9) | collective-permute-done | bytes 1048608 | tf_op jit(solution)/shard_map/ppermute | solution.py:24
  317.6 30.5 %all-to-all-done.3.refs_0_ = bf16[4,176,1024]{2,1,0:T(8,128)(2,1)} async-done(((bf16[4,176,1024]{2,1,0:T(8,128)(2,1)}), bf16[4,176,1024]{2,1,0:T(8,128)(2,1)}, u32[]{:S(2)}, u32[]{:S(2)}) %all-to-all-start.3) | async-done | bytes 1441824 | tf_op jit(solution)/shard_map/all_to_all | solution.py:1283
  354.8 19.8 %shard_map.242 = (bf16[1024,2048]{1,0:T(8,128)(2,1)}, bf16[1024,2816]{1,0:T(8,128)(2,1)}, bf16[1024,1408]{1,0:T(8,128)(2,1)}) custom-call(s32[13]{0:T(128)} %copy-done.65, bf16[256,2048]{1,0:T(8,128)(2,1)} %get-tuple-element.51.refs_0_, bf16[256,2048]{1,0:T(8,128)(2,1)} %collective-permute-done.10.refs_1_, bf16[256,2048]{1,0:T(8,128)(2,1)} %copy-done.84, ...), custom_call_target="tpu_custom_call" | custom-call | flops 1 | bytes 1 | tf_op jit(solution)/shard_map/pallas_call | solution.py:381
  374.7 11.5 %shard_map.247 = (bf16[4,176,1024]{2,1,0:T(8,128)(2,1)S(1)}, bf16[4,176,1024]{2,1,0:T(8,128)(2,1)S(1)}, bf16[4,176,1024]{2,1,0:T(8,128)(2,1)S(1)}, bf16[4,176,1024]{2,1,0:T(8,128)(2,1)}) custom-call(s32[13]{0:T(128)S(1)} %copy-done.66, bf16[1024,1408]{1,0:T(8,128)(2,1)} %get-tuple-element.52.refs_0_, bf16[1024,2048]{1,0:T(8,128)(2,1)} %copy-done.3), custom_call_target="tpu_custom_call" | custom-call | flops 1 | bytes 1 | tf_op jit(solution)/shard_map/pallas_call | solution.py:381
  387.3 16.7 %shard_map.248.refs_1_.refs_0_ = bf16[1024,2816]{1,0:T(8,128)(2,1)} custom-call(s32[13]{0:T(128)} %copy-done.65, bf16[1024,2048]{1,0:T(8,128)(2,1)} %copy-done.3, bf16[1024,2816]{1,0:T(8,128)(2,1)} %get-tuple-element.53.refs_1_, bf16[4,176,1024]{2,1,0:T(8,128)(2,1)} %shard_map.244.refs_2_.refs_1_, bf16[4,176,1024]{2,1,0:T(8,128)(2,1)} %shard_map.246.refs_3_.refs_2_, ...), custom_call_target="tpu_custom_call" | custom-call | flops 1 | bytes 1 | tf_op jit(solution)/shard_map/pallas_call | solution.py:381
  404.1 18.4 %shard_map.249.refs_2_ = bf16[2048,2816]{1,0:T(8,128)(2,1)} custom-call(s32[13]{0:T(128)S(1)} %copy-done.67, bf16[1024,2048]{1,0:T(8,128)(2,1)S(1)} %copy-done.56, bf16[1024,2816]{1,0:T(8,128)(2,1)} %shard_map.248.refs_1_.refs_0_), custom_call_target="tpu_custom_call" | custom-call | flops 1 | bytes 1 | tf_op jit(solution)/shard_map/pallas_call | solution.py:381
  422.6 18.2 %shard_map.250 = (bf16[512,2048]{1,0:T(8,128)(2,1)}, bf16[512,2048]{1,0:T(8,128)(2,1)}) custom-call(s32[13]{0:T(128)} %copy-done.65, bf16[1024,2816]{1,0:T(8,128)(2,1)} %shard_map.248.refs_1_.refs_0_, bf16[2048,2816]{1,0:T(8,128)(2,1)} %all-gather.5.cloned.1.call-done.refs_4_.refs_1_, bf16[2048,2816]{1,0:T(8,128)(2,1)} %shard_map.249.refs_2_), custom_call_target="tpu_custom_call" | custom-call | flops 1 | bytes 1 | tf_op jit(solution)/shard_map/pallas_call | solution.py:381
  451.3 12.8 %shard_map.251 = (bf16[512,2048]{1,0:T(8,128)(2,1)}, bf16[512,2048]{1,0:T(8,128)(2,1)}) custom-call(s32[13]{0:T(128)S(1)} %copy-done.68, bf16[1024,1408]{1,0:T(8,128)(2,1)} %get-tuple-element.52.refs_0_, bf16[4,176,1024]{2,1,0:T(8,128)(2,1)} %shard_map.244.refs_2_.refs_1_, bf16[4,176,1024]{2,1,0:T(8,128)(2,1)} %shard_map.246.refs_3_.refs_2_, ...), custom_call_target="tpu_custom_call" | custom-call | flops 1 | bytes 1 | tf_op jit(solution)/shard_map/pallas_call | solution.py:381
  464.0 21.0 %collective-permute-done.18.refs_0_ = bf16[4,176,1024]{2,1,0:T(8,128)(2,1)S(1)} collective-permute-done((bf16[4,176,1024]{2,1,0:T(8,128)(2,1)S(1)}, bf16[4,176,1024]{2,1,0:T(8,128)(2,1)S(1)}, u32[]{:S(2)}, u32[]{:S(2)}) %collective-permute-start.18) | collective-permute-done | bytes 1441824 | tf_op jit(solution)/shard_map/ppermute | solution.py:24
  489.8 6.3 all-to-all-start.4
  497.1 6.8 shard_map.254
  505.0 24.5 %collective-permute-done.20.refs_1_ = bf16[256,2048]{1,0:T(8,128)(2,1)} collective-permute-done((bf16[256,2048]{1,0:T(8,128)(2,1)}, bf16[256,2048]{1,0:T(8,128)(2,1)}, u32[]{:S(2)}, u32[]{:S(2)}) %collective-permute-start.20) | collective-permute-done | bytes 1048608 | tf_op jit(solution)/shard_map/ppermute | solution.py:24
  532.5 24.5 %all-to-all-done.4.refs_0_.refs_1_.refs_2_.refs_3_ = bf16[4,176,1024]{2,1,0:T(8,128)(2,1)} async-done(((bf16[4,176,1024]{2,1,0:T(8,128)(2,1)}), bf16[4,176,1024]{2,1,0:T(8,128)(2,1)}, u32[]{:S(2)}, u32[]{:S(2)}) %all-to-all-start.4) | async-done | bytes 1441824 | tf_op jit(solution)/shard_map/all_to_all | solution.py:1283
  566.2 8.1 %shard_map.257 = (bf16[1024,512]{1,0:T(8,128)(2,1)S(1)}, bf16[1024,2048]{1,0:T(8,128)(2,1)}) custom-call(s32[13]{0:T(128)S(1)} %copy-done.68, bf16[256,2048]{1,0:T(8,128)(2,1)} %get-tuple-element.62.refs_2_.refs_0_, bf16[256,2048]{1,0:T(8,128)(2,1)} %collective-permute-done.20.refs_1_, bf16[256,2048]{1,0:T(8,128)(2,1)} %collective-permute-done.21.refs_2_, ...), custom_call_target="tpu_custom_call" | custom-call | flops 1 | bytes 1 | tf_op jit(solution)/shard_map/pallas_call | solution.py:381
  582.2 7.5 collective-permute-done.19.refs_11_
  590.7 22.0 %shard_map.259 = (bf16[1024,512]{1,0:T(8,128)(2,1)S(1)}, bf16[1024,512]{1,0:T(8,128)(2,1)S(1)}, bf16[1024,512]{1,0:T(8,128)(2,1)S(1)}, f32[3,1,512]{2,1,0:T(1,128)S(1)}) custom-call(s32[13]{0:T(128)S(1)} %copy-done.68, bf16[1024,512]{1,0:T(8,128)(2,1)} %copy-done.16, bf16[1024,512]{1,0:T(8,128)(2,1)} %copy-done.18, bf16[1024,512]{1,0:T(8,128)(2,1)} %copy-done.30, ...), custom_call_target="tpu_custom_call" | custom-call | flops 1 | bytes 1 | tf_op jit(solution)/shard_map/pallas_call | solution.py:381
  613.7 9.1 %shard_map.260 = (bf16[1024,512]{1,0:T(8,128)(2,1)}, bf16[1024,512]{1,0:T(8,128)(2,1)S(1)}, bf16[1024,512]{1,0:T(8,128)(2,1)}, bf16[1024,1024]{1,0:T(8,128)(2,1)}) custom-call(s32[13]{0:T(128)S(1)} %copy-done.68, bf16[1024,2048]{1,0:T(8,128)(2,1)} %copy-done.2, bf16[1024,512]{1,0:T(8,128)(2,1)S(1)} %get-tuple-element.69.refs_1_.refs_0_, ...), custom_call_target="tpu_custom_call" | custom-call | flops 1 | bytes 1 | tf_op jit(solution)/shard_map/pallas_call | solution.py:381
  629.3 17.8 %collective-permute-done.24.refs_2_ = bf16[1024,512]{1,0:T(8,128)(2,1)} collective-permute-done((bf16[1024,512]{1,0:T(8,128)(2,1)}, bf16[1024,512]{1,0:T(8,128)(2,1)}, u32[]{:S(2)}, u32[]{:S(2)}) %collective-permute-start.24) | collective-permute-done | bytes 1048608 | tf_op jit(solution)/shard_map/ppermute | solution.py:24
  661.3 11.9 %shard_map.264 = (bf16[512,2048]{1,0:T(8,128)(2,1)S(1)}, bf16[512,2048]{1,0:T(8,128)(2,1)}) custom-call(s32[13]{0:T(128)S(1)} %copy-done.68, bf16[1024,512]{1,0:T(8,128)(2,1)S(1)} %copy-done.29, bf16[1024,512]{1,0:T(8,128)(2,1)S(1)} %copy-done.25, bf16[1024,512]{1,0:T(8,128)(2,1)S(1)} %copy-done.32, ...), custom_call_target="tpu_custom_call" | custom-call | flops 1 | bytes 1 | tf_op jit(solution)/shard_map/pallas_call | solution.py:381
  684.7 15.7 %collective-permute-done.41.refs_2_ = bf16[1024,512]{1,0:T(8,128)(2,1)} collective-permute-done((bf16[1024,512]{1,0:T(8,128)(2,1)}, bf16[1024,512]{1,0:T(8,128)(2,1)}, u32[]{:S(2)}, u32[]{:S(2)}) %collective-permute-start.41) | collective-permute-done | bytes 1048608 | tf_op jit(solution)/shard_map/ppermute | solution.py:24
  730.0 7.7 shard_map.269.refs_3_.refs_6_
  (392 shorter events, 278.4 us)
Async XLA Ops:
  19.8 81.3 %all-to-all-start = ((bf16[4,272,1536]{2,1,0:T(8,128)(2,1)}), bf16[4,272,1536]{2,1,0:T(8,128)(2,1)}, u32[]{:S(2)}, u32[]{:S(2)}) async-start(bf16[4,272,1536]{2,1,0:T(8,128)(2,1)} %broadcast_dynamic-update-slice_fusion), calls=%async_computation | async-start | bytes 6684672 | tf_op jit(solution)/shard_map/all_to_all | solution.py:1283
  26.2 328.1 %all-gather.5.cloned.1.call-start = ((), (), s32[]{:S(2)}) async-start(), calls=%async_computation.10 | async-start | bytes 12976128 | tf_op jit(solution)/shard_map/all_gather | solution.py:1374
  113.2 95.0 %collective-permute-start.3 = (bf16[4,272,1536]{2,1,0:T(8,128)(2,1)}, bf16[4,272,1536]{2,1,0:T(8,128)(2,1)}, u32[]{:S(2)}, u32[]{:S(2)}) collective-permute-start(bf16[4,272,1536]{2,1,0:T(8,128)(2,1)} %all-to-all-done.refs_1_.refs_2_.refs_3_), channel_id=1, source_target_pairs={{0,1},{1,0},{2,3},{3,2},{4,5},{5,4},{6,7},{7,6},{8,9},{9,8},{10,11... | collective-permute-start | bytes 10027016 | tf_op jit(solution)/shard_map/ppermute | solution.py:24
  144.4 49.7 %all-to-all-start.1 = ((bf16[4,64,2048]{2,1,0:T(8,128)(2,1)}), bf16[4,64,2048]{2,1,0:T(8,128)(2,1)}, u32[]{:S(2)}, u32[]{:S(2)}) async-start(bf16[4,64,2048]{2,1,0:T(8,128)(2,1)} %broadcast_in_dim.65), calls=%async_computation.1 | async-start | bytes 2097152 | tf_op jit(solution)/shard_map/all_to_all | solution.py:1283
  197.8 78.7 %all-to-all-start.2 = ((bf16[4,176,1024]{2,1,0:T(8,128)(2,1)}), bf16[4,176,1024]{2,1,0:T(8,128)(2,1)}, u32[]{:S(2)}, u32[]{:S(2)}) async-start(bf16[4,176,1024]{2,1,0:T(8,128)(2,1)} %broadcast_in_dim.66), calls=%async_computation.2 | async-start | bytes 2883584 | tf_op jit(solution)/shard_map/all_to_all | solution.py:1283
  202.5 58.2 %collective-permute-start.7 = (bf16[4,64,2048]{2,1,0:T(8,128)(2,1)}, bf16[4,64,2048]{2,1,0:T(8,128)(2,1)}, u32[]{:S(2)}, u32[]{:S(2)}) collective-permute-start(bf16[4,64,2048]{2,1,0:T(8,128)(2,1)} %all-to-all-done.1.refs_1_.refs_4_), channel_id=1, source_target_pairs={{0,1},{1,0},{2,3},{3,2},{4,5},{5,4},{6,7},{7,6},{8,9},{9,8},{10,11... | collective-permute-start | bytes 3145736 | tf_op jit(solution)/shard_map/ppermute | solution.py:24
  278.4 69.7 %all-to-all-start.3 = ((bf16[4,176,1024]{2,1,0:T(8,128)(2,1)}), bf16[4,176,1024]{2,1,0:T(8,128)(2,1)}, u32[]{:S(2)}, u32[]{:S(2)}) async-start(bf16[4,176,1024]{2,1,0:T(8,128)(2,1)} %copy-done.20), calls=%async_computation.3 | async-start | bytes 2883584 | tf_op jit(solution)/shard_map/all_to_all | solution.py:1283
  285.0 367.2 %reduce-scatter.2.cloned.1.call-start = ((), (), s32[]{:S(2)}) async-start(), calls=%async_computation.11 | async-start | bytes 12976128 | tf_op jit(solution)/shard_map/reduce_scatter | solution.py:1441
  314.8 33.3 %collective-permute-start.10 = (bf16[256,2048]{1,0:T(8,128)(2,1)}, bf16[256,2048]{1,0:T(8,128)(2,1)}, u32[]{:S(2)}, u32[]{:S(2)}) collective-permute-start(bf16[256,2048]{1,0:T(8,128)(2,1)} %get-tuple-element.51.refs_0_), channel_id=1, source_target_pairs={{0,4},{2,6},{4,0},{6,2},{1,5},{3,7},{5,1},{7,3},{8,12},{10,14},{12... | collective-permute-start | bytes 3145736 | tf_op jit(solution)/shard_map/ppermute | solution.py:24
  316.9 70.4 %collective-permute-start.13 = (bf16[4,176,1024]{2,1,0:T(8,128)(2,1)}, bf16[4,176,1024]{2,1,0:T(8,128)(2,1)}, u32[]{:S(2)}, u32[]{:S(2)}) collective-permute-start(bf16[4,176,1024]{2,1,0:T(8,128)(2,1)} %shard_map.244.refs_2_.refs_1_), channel_id=1, source_target_pairs={{0,1},{1,0},{2,3},{3,2},{4,5},{5,4},{6,7},{7,6},{8,9},{9,8},{10,11... | collective-permute-start | bytes 4325384 | tf_op jit(solution)/shard_map/ppermute | solution.py:24
  348.6 38.7 %collective-permute-start.14 = (bf16[4,176,1024]{2,1,0:T(8,128)(2,1)}, bf16[4,176,1024]{2,1,0:T(8,128)(2,1)}, u32[]{:S(2)}, u32[]{:S(2)}) collective-permute-start(bf16[4,176,1024]{2,1,0:T(8,128)(2,1)} %shard_map.246.refs_3_.refs_2_), channel_id=1, source_target_pairs={{0,1},{1,0},{2,3},{3,2},{4,5},{5,4},{6,7},{7,6},{8,9},{9,8},{10,11... | collective-permute-start | bytes 4325384 | tf_op jit(solution)/shard_map/ppermute | solution.py:24
  440.9 44.1 %collective-permute-start.18 = (bf16[4,176,1024]{2,1,0:T(8,128)(2,1)S(1)}, bf16[4,176,1024]{2,1,0:T(8,128)(2,1)S(1)}, u32[]{:S(2)}, u32[]{:S(2)}) collective-permute-start(bf16[4,176,1024]{2,1,0:T(8,128)(2,1)S(1)} %copy-done.78), channel_id=1, source_target_pairs={{0,1},{1,0},{2,3},{3,2},{4,5},{5,4},{6,7},{7,6},{8,9},{9,8},{10,11... | collective-permute-start | bytes 4325384 | tf_op jit(solution)/shard_map/ppermute | solution.py:24
  449.7 47.3 %collective-permute-start.17 = (bf16[256,2048]{1,0:T(8,128)(2,1)}, bf16[256,2048]{1,0:T(8,128)(2,1)}, u32[]{:S(2)}, u32[]{:S(2)}) collective-permute-start(bf16[256,2048]{1,0:T(8,128)(2,1)} %shard_map.252), channel_id=1, source_target_pairs={{0,4},{2,6},{4,0},{6,2},{1,5},{3,7},{5,1},{7,3},{8,12},{10,14},{12... | collective-permute-start | bytes 3145736 | tf_op jit(solution)/shard_map/ppermute | solution.py:24
  489.8 67.3 %all-to-all-start.4 = ((bf16[4,176,1024]{2,1,0:T(8,128)(2,1)}), bf16[4,176,1024]{2,1,0:T(8,128)(2,1)}, u32[]{:S(2)}, u32[]{:S(2)}) async-start(bf16[4,176,1024]{2,1,0:T(8,128)(2,1)} %add_convert_fusion.1.refs_7_), calls=%async_computation.4 | async-start | bytes 2883584 | tf_op jit(solution)/shard_map/all_to_all | solution.py:1283
  496.1 65.8 %collective-permute-start.16 = (bf16[512,2048]{1,0:T(8,128)(2,1)}, bf16[512,2048]{1,0:T(8,128)(2,1)}, u32[]{:S(2)}, u32[]{:S(2)}) collective-permute-start(bf16[512,2048]{1,0:T(8,128)(2,1)} %get-tuple-element.58), channel_id=1, source_target_pairs={{0,2},{2,0},{4,6},{6,4},{1,3},{3,1},{5,7},{7,5},{8,10},{10,8},{12,... | collective-permute-start | bytes 6291464 | tf_op jit(solution)/shard_map/ppermute | solution.py:24
  496.1 34.2 %collective-permute-start.23 = (bf16[4,176,1024]{2,1,0:T(8,128)(2,1)}, bf16[4,176,1024]{2,1,0:T(8,128)(2,1)S(1)}, u32[]{:S(2)}, u32[]{:S(2)}) collective-permute-start(bf16[4,176,1024]{2,1,0:T(8,128)(2,1)} %get-tuple-element.54.refs_6_), channel_id=1, source_target_pairs={{0,1},{1,0},{2,3},{3,2},{4,5},{5,4},{6,7},{7,6},{8,9},{9,8},{10,11... | collective-permute-start | bytes 4325384 | tf_op jit(solution)/shard_map/ppermute | solution.py:24
  505.0 61.1 %collective-permute-start.21 = (bf16[256,2048]{1,0:T(8,128)(2,1)}, bf16[256,2048]{1,0:T(8,128)(2,1)}, u32[]{:S(2)}, u32[]{:S(2)}) collective-permute-start(bf16[256,2048]{1,0:T(8,128)(2,1)} %get-tuple-element.62.refs_2_.refs_0_), channel_id=1, source_target_pairs={{0,2},{2,0},{4,6},{6,4},{1,3},{3,1},{5,7},{7,5},{8,10},{10,8},{12,... | collective-permute-start | bytes 3145736 | tf_op jit(solution)/shard_map/ppermute | solution.py:24
  529.5 36.6 %collective-permute-start.22 = (bf16[256,2048]{1,0:T(8,128)(2,1)}, bf16[256,2048]{1,0:T(8,128)(2,1)}, u32[]{:S(2)}, u32[]{:S(2)}) collective-permute-start(bf16[256,2048]{1,0:T(8,128)(2,1)} %collective-permute-done.20.refs_1_), channel_id=1, source_target_pairs={{0,2},{2,0},{4,6},{6,4},{1,3},{3,1},{5,7},{7,5},{8,10},{10,8},{12,... | collective-permute-start | bytes 3145736 | tf_op jit(solution)/shard_map/ppermute | solution.py:24
  557.1 70.0 %all-to-all-start.5 = ((bf16[4,176,1024]{2,1,0:T(8,128)(2,1)}), bf16[4,176,1024]{2,1,0:T(8,128)(2,1)}, u32[]{:S(2)}, u32[]{:S(2)}) async-start(bf16[4,176,1024]{2,1,0:T(8,128)(2,1)} %add_convert_fusion.refs_6_), calls=%async_computation.5 | async-start | bytes 2883584 | tf_op jit(solution)/shard_map/all_to_all | solution.py:1283
  561.4 118.0 %all-gather.9.cloned.1.call-start = ((), (), s32[]{:S(2)}) async-start(), calls=%async_computation.13 | async-start | bytes 3604480 | tf_op jit(solution)/shard_map/all_gather | solution.py:1480
  580.9 44.9 %collective-permute-start.25 = (bf16[4,256,512]{2,1,0:T(8,128)(2,1)S(1)}, bf16[4,256,512]{2,1,0:T(8,128)(2,1)S(1)}, u32[]{:S(2)}, u32[]{:S(2)}) collective-permute-start(bf16[4,256,512]{2,1,0:T(8,128)(2,1)S(1)} %get-tuple-element.68.refs_10_), channel_id=1, source_target_pairs={{0,1},{1,0},{2,3},{3,2},{4,5},{5,4},{6,7},{7,6},{8,9},{9,8},{10,11... | collective-permute-start | bytes 3145736 | tf_op jit(solution)/shard_map/ppermute | solution.py:24
  652.2 75.2 %all-gather.7.cloned.1.call-start = ((), (), s32[]{:S(2)}) async-start(), calls=%async_computation.12 | async-start | bytes 7208960 | tf_op jit(solution)/shard_map/all_gather | solution.py:1480
  652.8 53.0 %all-to-all-start.6 = ((bf16[4,512,512]{2,1,0:T(8,128)(2,1)}), bf16[4,512,512]{2,1,0:T(8,128)(2,1)S(1)}, u32[]{:S(2)}, u32[]{:S(2)}) async-start(bf16[4,512,512]{2,1,0:T(8,128)(2,1)} %copy-done.5), calls=%async_computation.6 | async-start | bytes 4194304 | tf_op jit(solution)/shard_map/all_to_all | solution.py:1283
  674.5 37.0 %collective-permute-start.26 = (bf16[512,2048]{1,0:T(8,128)(2,1)}, bf16[512,2048]{1,0:T(8,128)(2,1)}, u32[]{:S(2)}, u32[]{:S(2)}) collective-permute-start(bf16[512,2048]{1,0:T(8,128)(2,1)} %get-tuple-element.77), channel_id=1, source_target_pairs={{0,2},{2,0},{4,6},{6,4},{1,3},{3,1},{5,7},{7,5},{8,10},{10,8},{12,... | collective-permute-start | bytes 6291464 | tf_op jit(solution)/shard_map/ppermute | solution.py:24
  705.8 36.0 %all-to-all-start.8 = ((bf16[4,256,512]{2,1,0:T(8,128)(2,1)}), bf16[4,256,512]{2,1,0:T(8,128)(2,1)}, u32[]{:S(2)}, u32[]{:S(2)}) async-start(bf16[4,256,512]{2,1,0:T(8,128)(2,1)} %bitcast.83), calls=%async_computation.9 | async-start | bytes 2097152 | tf_op jit(solution)/shard_map/all_to_all | solution.py:1283
  711.0 49.3 %all-gather.11.cloned.1.call-start = ((), (), s32[]{:S(2)}) async-start(), calls=%async_computation.14 | async-start | bytes 1310720 | tf_op jit(solution)/shard_map/all_gather | solution.py:1480
  711.0 26.7 %collective-permute-start.37 = (bf16[1024,512]{1,0:T(8,128)(2,1)}, bf16[1024,512]{1,0:T(8,128)(2,1)}, u32[]{:S(2)}, u32[]{:S(2)}) collective-permute-start(bf16[1024,512]{1,0:T(8,128)(2,1)} %copy-done.79), channel_id=1, source_target_pairs={{0,1},{1,0},{2,3},{3,2},{4,5},{5,4},{6,7},{7,6},{8,9},{9,8},{10,11... | collective-permute-start | bytes 3145736 | tf_op jit(solution)/shard_map/ppermute | solution.py:24
  717.5 34.0 %collective-permute-start.27 = (bf16[256,2048]{1,0:T(8,128)(2,1)}, bf16[256,2048]{1,0:T(8,128)(2,1)}, u32[]{:S(2)}, u32[]{:S(2)}) collective-permute-start(bf16[256,2048]{1,0:T(8,128)(2,1)} %shard_map.265), channel_id=1, source_target_pairs={{0,4},{2,6},{4,0},{6,2},{1,5},{3,7},{5,1},{7,3},{8,12},{10,14},{12... | collective-permute-start | bytes 3145736 | tf_op jit(solution)/shard_map/ppermute | solution.py:24
  741.8 30.9 %all-to-all-start.7 = ((bf16[4,256,512]{2,1,0:T(8,128)(2,1)}), bf16[4,256,512]{2,1,0:T(8,128)(2,1)}, u32[]{:S(2)}, u32[]{:S(2)}) async-start(bf16[4,256,512]{2,1,0:T(8,128)(2,1)} %bitcast.78), calls=%async_computation.8 | async-start | bytes 2097152 | tf_op jit(solution)/shard_map/all_to_all | solution.py:1283
  746.6 46.2 %collective-permute-start.34 = (bf16[256,512]{1,0:T(8,128)(2,1)S(1)}, bf16[256,512]{1,0:T(8,128)(2,1)S(1)}, u32[]{:S(2)}, u32[]{:S(2)}) collective-permute-start(bf16[256,512]{1,0:T(8,128)(2,1)S(1)} %get-tuple-element.103.refs_0_), channel_id=1, source_target_pairs={{0,4},{2,6},{4,0},{6,2},{1,5},{3,7},{5,1},{7,3},{8,12},{10,14},{12... | collective-permute-start | bytes 786440 | tf_op jit(solution)/shard_map/ppermute | solution.py:24
  746.7 47.9 %collective-permute-start.35 = (bf16[256,512]{1,0:T(8,128)(2,1)S(1)}, bf16[256,512]{1,0:T(8,128)(2,1)}, u32[]{:S(2)}, u32[]{:S(2)}) collective-permute-start(bf16[256,512]{1,0:T(8,128)(2,1)S(1)} %get-tuple-element.103.refs_0_), channel_id=1, source_target_pairs={{0,2},{2,0},{4,6},{6,4},{1,3},{3,1},{5,7},{7,5},{8,10},{10,8},{12,... | collective-permute-start | bytes 786440 | tf_op jit(solution)/shard_map/ppermute | solution.py:24
  766.1 28.0 %collective-permute-start.42 = (bf16[256,512]{1,0:T(8,128)(2,1)S(1)}, bf16[256,512]{1,0:T(8,128)(2,1)}, u32[]{:S(2)}, u32[]{:S(2)}) collective-permute-start(bf16[256,512]{1,0:T(8,128)(2,1)S(1)} %shard_map.274.refs_8_), channel_id=1, source_target_pairs={{0,4},{2,6},{4,0},{6,2},{1,5},{3,7},{5,1},{7,3},{8,12},{10,14},{12... | collective-permute-start | bytes 786440 | tf_op jit(solution)/shard_map/ppermute | solution.py:24
  (114 other events, 1418.7 us)
Sparse Core Ops, SparseCore 0:
  106.6 247.6 all-gather.4
  422.7 223.1 reduce-scatter.1
  652.3 27.0 all-gather.8
  680.8 46.4 all-gather.6
  729.3 22.1 all-gather.10
